TPU v7x, 32 devices: a whole 2x2x4 slice. The times are simulated.
32 devices in a mesh: dp: 4 (over y, x), seq: 8 (over z, core).
Axes of the slice: x: 2, y: 2, z: 4, core: 2. Of those that a mesh axis runs over, the one named last changes fastest.
Arguments:
- queries: bfloat16 [4, 2048, 1024], P('dp', 'seq'), may hold values from -7.5 to 7.5
- keys: bfloat16 [4, 2048, 1024], P('dp', 'seq'), may hold values from -7.5 to 7.5
- values: bfloat16 [4, 2048, 1024], P('dp', 'seq'), may hold values from -7.5 to 7.5
- grad_out: bfloat16 [4, 2048, 1024], P('dp', 'seq'), may hold values from -3 to 3
- w_out: bfloat16 [1024, 1024], replicated, may hold values from -0.1875 to 0.1875
Outputs:
- mixed: bfloat16 [4, 2048, 1024], P('dp', 'seq')
- grad_queries: bfloat16 [4, 2048, 1024], P('dp', 'seq')
- grad_keys: bfloat16 [4, 2048, 1024], P('dp', 'seq')
- grad_values: bfloat16 [4, 2048, 1024], P('dp', 'seq')
- grad_w_out: float32 [1024, 1024], P(('dp', 'seq'))
All inputs are finite; a program needn't handle non-finite values.
Results may differ from a plain program's by a relative error of at most 0.03.
Values may be sent and summed in bfloat16 or wider, within the bound.
No kernel may reach another device: no remote copies, remote signals or barrier semaphores. Data moves between devices by JAX's collectives and lax.ppermute only.
A program may use at most 128 MiB of HBM per device.

v0:
```python
import functools
import math

import jax
import jax.numpy as jnp
from jax import lax
from jax.experimental import pallas as pl
from jax.experimental.pallas import tpu as pltpu
from jax.sharding import PartitionSpec as P

HEADS = 8
HEAD_DIM = 128
BLOCK = 128
LANES = 128
SCALE = 1.0 / math.sqrt(HEAD_DIM)
SCALE2 = SCALE / math.log(2.0)
F32 = jnp.float32
BF16 = jnp.bfloat16
VMEM_LIMIT = 48 * 1024 * 1024


def dot(a, b, dims):
    return lax.dot_general(a, b, (dims, ((), ())), preferred_element_type=F32)


def nn(a, b):
    return dot(a, b, ((1,), (0,)))


def nt(a, b):
    return dot(a, b, ((1,), (1,)))


def tn(a, b):
    return dot(a, b, ((0,), (0,)))


def member(rows, cols, row_shift, col_shift, value):
    r = lax.broadcasted_iota(jnp.int32, (rows, cols), 0) >> row_shift
    c = lax.broadcasted_iota(jnp.int32, (rows, cols), 1) >> col_shift
    return jnp.where(r == c, value, 0.0).astype(BF16)


def call(kernel, outs, name, flops, *operands):
    moved = sum(x.size * x.dtype.itemsize for x in operands)
    moved += sum(math.prod(s) * jnp.dtype(t).itemsize for s, t in outs)
    return pl.pallas_call(
        kernel,
        name=name,
        out_shape=[jax.ShapeDtypeStruct(s, t) for s, t in outs],
        in_specs=[pl.BlockSpec(memory_space=pltpu.VMEM)] * len(operands),
        out_specs=[pl.BlockSpec(memory_space=pltpu.VMEM)] * len(outs),
        compiler_params=pltpu.CompilerParams(vmem_limit_bytes=VMEM_LIMIT),
        cost_estimate=pl.CostEstimate(flops=flops, bytes_accessed=moved, transcendentals=0),
    )(*operands)


def pool_kernel(levels, k_ref, v_ref, *outs):
    tokens, width = k_ref.shape
    pools = [member(tokens >> l, tokens, 0, l, 0.5**l) for l in range(1, levels)]
    for which, src in enumerate((k_ref, v_ref)):
        x = src[...]
        for pool, out in zip(pools, outs):
            out[which] = nn(pool, x).astype(BF16)


def early_kernel(levels, q_ref, g_ref, w_ref, qhat_ref, ga_ref, *qls):
    tokens, width = q_ref.shape
    q = q_ref[...]
    for l in range(1, levels):
        qhat_ref[l - 1] = nn(member(tokens, tokens, l, l, 0.5**l), q).astype(BF16)
        qls[l - 1][...] = nn(member(tokens >> l, tokens, 0, l, 0.5**l), q).astype(BF16)
    g = g_ref[...]
    for c in range(0, width, 256):
        ga_ref[:, c : c + 256] = nt(g, w_ref[c : c + 256, :]).astype(BF16)


def forward_kernel(levels, pieces, dp, q_ref, k_ref, v_ref, qhat_ref, ga_ref, *refs):
    tokens, width = q_ref.shape
    upper = levels - 1
    count = sum(pieces)
    qls, refs = refs[:upper], refs[upper:]
    kvs, refs = refs[:count], refs[count:]
    e_ref, gr_ref, dd_ref, att_ref = refs[:4]
    blocks, msgs = refs[4 : 4 + dp], refs[4 + dp :]
    lane = lax.broadcasted_iota(jnp.int32, (tokens, LANES), 1)
    ones = jnp.ones((tokens + upper * BLOCK, LANES), BF16)
    sums = [member(tokens >> l, tokens, 0, l, 1.0) for l in range(1, levels)]
    aux = [jnp.zeros((tokens, LANES), F32) for _ in range(upper)]
    dd = jnp.zeros((tokens, LANES), F32)
    for h in range(HEADS):
        hs = slice(h * HEAD_DIM, (h + 1) * HEAD_DIM)
        keys, vals, at = [], [v_ref[:, hs]], 0
        for l in range(1, levels):
            part = kvs[at : at + pieces[l - 1]]
            at += pieces[l - 1]
            keys.append(jnp.concatenate([p[0, :, hs] for p in part], axis=0))
            vals.extend(p[1, :, hs] for p in part)
        raw0 = nt(q_ref[:, hs], k_ref[:, hs])
        raws = [nt(qhat_ref[l - 1, :, hs], keys[l - 1]) for l in range(1, levels)]
        top = jnp.max(raw0, axis=1, keepdims=True) * SCALE2
        mus = []
        for l in range(1, levels):
            big = jnp.max(raws[l - 1], axis=1, keepdims=True)
            top = jnp.maximum(top, big * SCALE2 + float(l))
            mus.append(big.astype(BF16).astype(F32))
        es = [jnp.exp2(raw0 * SCALE2 - top).astype(BF16)]
        for l in range(1, levels):
            es.append(jnp.exp2(raws[l - 1] * SCALE2 + (float(l) - top)).astype(BF16))
        e = jnp.concatenate(es, axis=1)
        e_ref[h] = e
        v_all = jnp.concatenate([jnp.concatenate(vals, axis=0), ones], axis=1)
        both = nn(e, v_all)
        rden = 1.0 / both[:, HEAD_DIM:]
        att = (both[:, :HEAD_DIM] * rden).astype(BF16)
        att_ref[:, hs] = att
        ga = ga_ref[:, hs].astype(F32)
        gr = ga * rden
        gr_ref[:, hs] = gr.astype(BF16)
        delta = jnp.sum(gr * att.astype(F32), axis=1, keepdims=True)
        dd = jnp.where(lane == h, delta, dd)
        for l in range(1, levels):
            a = jnp.exp2(mus[l - 1] * SCALE2 + (float(l) - top))
            n = tokens >> l
            msgs[l - 1][:, hs] = nn(sums[l - 1], (gr * a).astype(BF16)).astype(BF16)
            mixed = jnp.where(lane == h, mus[l - 1] * 0.5**l, aux[l - 1])
            aux[l - 1] = jnp.where(lane == HEADS + h, delta * a, mixed)
    dd_ref[...] = dd
    for l in range(1, levels):
        msgs[l - 1][:, width : 2 * width] = qls[l - 1][...]
        msgs[l - 1][:, 2 * width :] = nn(sums[l - 1], aux[l - 1].astype(BF16)).astype(BF16)
    me = lax.axis_index("dp")
    span = width // dp
    for m in range(dp):
        at = pl.multiple_of((me ^ m) * span, span)
        blocks[m][...] = att_ref[:, pl.ds(at, span)]


def backward_kernel(levels, pieces, e_ref, gr_ref, dd_ref, ga_ref, q_ref, k_ref, v_ref, *refs):
    tokens, width = q_ref.shape
    count = sum(pieces)
    kvs = refs[:count]
    att_ref, w_ref, gq_ref, dk_ref, dv_ref, mixed_ref, y_ref = refs[count:]
    upper = levels - 1
    for h in range(HEADS):
        hs = slice(h * HEAD_DIM, (h + 1) * HEAD_DIM)
        keys, vals, at = [], [v_ref[:, hs]], 0
        for l in range(1, levels):
            part = kvs[at : at + pieces[l - 1]]
            at += pieces[l - 1]
            keys.append(jnp.concatenate([p[0, :, hs] for p in part], axis=0))
            vals.extend(p[1, :, hs] for p in part)
        e = e_ref[h]
        gr = gr_ref[:, hs]
        dp_all = nt(gr, jnp.concatenate(vals, axis=0))
        ds = (e.astype(F32) * (dp_all - dd_ref[:, h : h + 1])).astype(BF16)
        dv_ref[:, hs] = tn(e[:, :tokens], gr).astype(BF16)
        dk_ref[:, hs] = (tn(ds[:, :tokens], q_ref[:, hs]) * SCALE).astype(BF16)
        gq_ref[:, hs] = nn(ds[:, :tokens], k_ref[:, hs])
        for l in range(1, levels):
            at = tokens + (l - 1) * BLOCK
            y_ref[(l - 1) * tokens : l * tokens, hs] = nn(
                ds[:, at : at + BLOCK], keys[l - 1]
            ).astype(BF16)
    spread = jnp.concatenate(
        [member(tokens, tokens, l, l, 0.5**l) for l in range(1, levels)], axis=1
    )
    for c in range(0, width, 256):
        cs = slice(c, c + 256)
        gq_ref[:, cs] = (gq_ref[:, cs] + nn(spread, y_ref[:, cs])) * SCALE
        mixed_ref[:, cs] = nn(att_ref[...], w_ref[:, cs]).astype(BF16)


def weight_kernel(dp, nz, *refs):
    atts, refs = refs[:dp], refs[dp:]
    grads, refs = refs[: dp], refs[dp:]
    keep_ref, send_ref, total_ref = refs
    a = jnp.concatenate([x[...] for x in atts], axis=0)
    width = grads[0].shape[1]
    for c in range(0, width, 256):
        cs = slice(c, c + 256)
        g = jnp.concatenate([x[:, cs] for x in grads], axis=0)
        total_ref[:, cs] = tn(a, g)
    rows = total_ref.shape[0] // (2 * nz)
    seq = lax.axis_index("seq")
    core, z = seq & 1, seq >> 1
    for m in range(nz):
        base = (z ^ m) * 2 * rows
        mine = pl.multiple_of(base + core * rows, rows)
        other = pl.multiple_of(base + (1 - core) * rows, rows)
        keep_ref[m * rows : (m + 1) * rows, :] = total_ref[pl.ds(mine, rows), :]
        send_ref[m * rows : (m + 1) * rows, :] = total_ref[pl.ds(other, rows), :].astype(BF16)


def halves_kernel(keep_ref, got_ref, *outs):
    rows = outs[0].shape[0]
    total = keep_ref[...] + got_ref[...].astype(F32)
    for m, out in enumerate(outs):
        out[...] = total[m * rows : (m + 1) * rows].astype(out.dtype)


def final_kernel(factor, *refs):
    out = refs[-1]
    total = refs[0][...]
    for x in refs[1:-1]:
        total = total + x[...].astype(F32)
    out[...] = total * factor


def owner_kernel(levels, pieces, tokens, *refs):
    upper = levels - 1
    count = sum(pieces)
    kvs, refs = refs[:upper], refs[upper:]
    msgs, refs = refs[:count], refs[count:]
    dk0_ref, dv0_ref, gk_ref, gv_ref, dks_ref, dvs_ref = refs
    width = dk0_ref.shape[1]
    auxes, at = [], 0
    groups = []
    for l in range(1, levels):
        part = msgs[at : at + pieces[l - 1]]
        at += pieces[l - 1]
        groups.append(part)
        auxes.append(jnp.concatenate([p[:, 2 * width :] for p in part], axis=0))
    for h in range(HEADS):
        hs = slice(h * HEAD_DIM, (h + 1) * HEAD_DIM)
        qs = slice(width + h * HEAD_DIM, width + (h + 1) * HEAD_DIM)
        at = 0
        for l in range(1, levels):
            n = tokens >> l
            lane = lax.broadcasted_iota(jnp.int32, (n, LANES), 1)
            minus_mu = jnp.where(lane == h, -1.0, 0.0).astype(BF16)
            minus_d = jnp.where(lane == HEADS + h, -1.0, 0.0).astype(BF16)
            ga = jnp.concatenate([p[:, hs] for p in groups[l - 1]], axis=0)
            q = jnp.concatenate([p[:, qs] for p in groups[l - 1]], axis=0)
            aux = auxes[l - 1]
            k = jnp.concatenate([kvs[l - 1][0, :, hs], minus_mu], axis=1)
            v = jnp.concatenate([kvs[l - 1][1, :, hs], minus_d], axis=1)
            e = jnp.exp2(nt(k, jnp.concatenate([q, aux], axis=1)) * SCALE2)
            ds = e * nt(v, jnp.concatenate([ga, aux], axis=1))
            dvs_ref[at : at + n, hs] = nn(e.astype(BF16), ga).astype(BF16)
            dks_ref[at : at + n, hs] = (nn(ds.astype(BF16), q) * SCALE).astype(BF16)
            at += n
    total = dks_ref.shape[0]
    spread = jnp.concatenate(
        [member(tokens, tokens >> l, l, 0, 0.5**l) for l in range(1, levels)], axis=1
    )
    for c in range(0, width, 256):
        cs = slice(c, c + 256)
        gk_ref[:, cs] = (dk0_ref[:, cs].astype(F32) + nn(spread, dks_ref[:, cs])).astype(BF16)
        gv_ref[:, cs] = (dv0_ref[:, cs].astype(F32) + nn(spread, dvs_ref[:, cs])).astype(BF16)


def swap(x, axis, mask):
    count = lax.axis_size(axis)
    return lax.ppermute(x, axis, [(i, i ^ mask) for i in range(count)])


def body(queries, keys, values, grad_out, w_out):
    seq = lax.axis_size("seq")
    dp = lax.axis_size("dp")
    nz = seq // 2
    levels = seq.bit_length()
    upper = levels - 1
    q, k, v, g = queries[0], keys[0], values[0], grad_out[0]
    tokens, width = q.shape
    factor = 1.0 / math.sqrt(dp * seq * tokens)

    own = call(
        functools.partial(pool_kernel, levels),
        [((2, tokens >> l, width), BF16) for l in range(1, levels)],
        "pool",
        2 * 2 * tokens * tokens * width,
        k,
        v,
    )

    def exchange(per_level):
        first = swap(per_level[0], "seq", 1)
        across = []
        for m in range(1, nz):
            across.append((m.bit_length(), swap(per_level[m.bit_length()], "seq", 2 * m)))
        got = [[first]] + [[] for _ in range(upper - 1)]
        for at, x in across:
            got[at] += [x, swap(x, "seq", 1)]
        axis = per_level[0].ndim - 2
        return [x if x[0].shape[axis] >= 16 else [jnp.concatenate(x, axis=axis)] for x in got]

    pairs = exchange(own)
    pieces = [len(x) for x in pairs]
    flat = [x for part in pairs for x in part]

    grads = [g] + [swap(g, "dp", m) for m in range(1, min(dp, 3))]
    if dp == 4:
        half = tokens // 2
        grads.append(
            (swap(grads[1][:half], "dp", 2), swap(grads[2][half:], "dp", 1))
        )
    else:
        grads += [swap(g, "dp", m) for m in range(3, dp)]

    early = call(
        functools.partial(early_kernel, levels),
        [((upper, tokens, width), BF16), ((tokens, width), BF16)]
        + [((tokens >> l, width), BF16) for l in range(1, levels)],
        "early",
        2 * tokens * width * width + 2 * upper * tokens * tokens * width,
        q,
        g,
        w_out,
    )
    qhat, ga, qls = early[0], early[1], early[2:]

    total_keys = tokens + upper * BLOCK
    forward = call(
        functools.partial(forward_kernel, levels, pieces, dp),
        [
            ((HEADS, tokens, total_keys), BF16),
            ((tokens, width), BF16),
            ((tokens, LANES), F32),
            ((tokens, width), BF16),
        ]
        + [((tokens, width // dp), BF16)] * dp
        + [((tokens >> l, 2 * width + LANES), BF16) for l in range(1, levels)],
        "forward",
        6 * tokens * total_keys * width,
        q,
        k,
        v,
        qhat,
        ga,
        *qls,
        *flat,
    )
    e, gr, dd, att = forward[:4]
    blocks, outgoing = forward[4 : 4 + dp], forward[4 + dp :]

    atts = [blocks[0]] + [swap(blocks[m], "dp", m) for m in range(1, dp)]
    messages = exchange(outgoing)
    message_pieces = [len(x) for x in messages]

    if dp == 4:
        grads[3] = jnp.concatenate(grads[3], axis=0)
    rows = width // dp
    keep, send = pl.pallas_call(
        functools.partial(weight_kernel, dp, nz),
        name="weight",
        out_shape=[
            jax.ShapeDtypeStruct((rows // 2, width), F32),
            jax.ShapeDtypeStruct((rows // 2, width), BF16),
        ],
        in_specs=[pl.BlockSpec(memory_space=pltpu.VMEM)] * (2 * dp),
        out_specs=[pl.BlockSpec(memory_space=pltpu.VMEM)] * 2,
        scratch_shapes=[pltpu.VMEM((rows, width), F32)],
        compiler_params=pltpu.CompilerParams(vmem_limit_bytes=VMEM_LIMIT),
        cost_estimate=pl.CostEstimate(
            flops=2 * tokens * width * width, bytes_accessed=4 << 20, transcendentals=0
        ),
    )(*atts, *grads)
    got = swap(send, "seq", 1)
    own_rows = rows // (2 * nz)
    parts = call(
        halves_kernel,
        [((own_rows, width), F32)] + [((own_rows, width), BF16)] * (nz - 1),
        "halves",
        rows * width,
        keep,
        got,
    )
    parts = [parts[0]] + [swap(parts[m], "seq", 2 * m) for m in range(1, nz)]

    gq, dk0, dv0, mixed = pl.pallas_call(
        functools.partial(backward_kernel, levels, pieces),
        name="backward",
        out_shape=[
            jax.ShapeDtypeStruct((tokens, width), F32),
            jax.ShapeDtypeStruct((tokens, width), BF16),
            jax.ShapeDtypeStruct((tokens, width), BF16),
            jax.ShapeDtypeStruct((tokens, width), BF16),
        ],
        in_specs=[pl.BlockSpec(memory_space=pltpu.VMEM)] * (9 + len(flat)),
        out_specs=[pl.BlockSpec(memory_space=pltpu.VMEM)] * 4,
        scratch_shapes=[pltpu.VMEM((upper * tokens, width), BF16)],
        compiler_params=pltpu.CompilerParams(vmem_limit_bytes=VMEM_LIMIT),
        cost_estimate=pl.CostEstimate(
            flops=10 * tokens * total_keys * width, bytes_accessed=8 << 20, transcendentals=0
        ),
    )(e, gr, dd, ga, q, k, v, *flat, att, w_out)

    upper_rows = sum(tokens >> l for l in range(1, levels))
    flat_messages = [x for part in messages for x in part]
    gk, gv = pl.pallas_call(
        functools.partial(owner_kernel, levels, message_pieces, tokens),
        name="owner",
        out_shape=[jax.ShapeDtypeStruct((tokens, width), BF16)] * 2,
        in_specs=[pl.BlockSpec(memory_space=pltpu.VMEM)] * (upper + len(flat_messages) + 2),
        out_specs=[pl.BlockSpec(memory_space=pltpu.VMEM)] * 2,
        scratch_shapes=[pltpu.VMEM((upper_rows, width), BF16)] * 2,
        compiler_params=pltpu.CompilerParams(vmem_limit_bytes=VMEM_LIMIT),
        cost_estimate=pl.CostEstimate(
            flops=8 * BLOCK * upper_rows * width, bytes_accessed=5 << 20, transcendentals=0
        ),
    )(*own, *flat_messages, dk0, dv0)

    (gw,) = call(
        functools.partial(final_kernel, factor),
        [((own_rows, width), F32)],
        "total",
        rows * width,
        *parts,
    )
    return (mixed[None], gq.astype(BF16)[None], gk[None], gv[None], gw)


def solution(mesh):
    rows = P("dp", "seq", None)
    return jax.shard_map(
        body,
        mesh=mesh,
        in_specs=(rows, rows, rows, rows, P()),
        out_specs=(rows, rows, rows, rows, P(("dp", "seq"), None)),
        check_vma=False,
    )
```

profile of v0, /device:TPU:0, one launch (start us, length us, event | category | flops | bytes accessed | tf_op | source)
XLA Modules:
  0.0 82.0 jit_solution(6862993498085986271)
XLA Ops:
  0.6 3.0 %collective-permute-start.17 = (bf16[256,1024]{1,0:T(8,128)(2,1)}, bf16[256,1024]{1,0:T(8,128)(2,1)S(1)}, u32[]{:S(2)}, u32[]{:S(2)}) collective-permute-start(bf16[256,1024]{1,0:T(8,128)(2,1)} %bitcast.18), channel_id=1, source_target_pairs={{0,8},{8,0},{16,24},{24,16},{1,9},{9,1},{17,25},{25,17},{2,10},{10... | collective-permute-start | bytes 1572872 | tf_op jit(solution)/shard_map/ppermute | solution.py:255
  3.6 1.5 %collective-permute-start.18 = (bf16[256,1024]{1,0:T(8,128)(2,1)}, bf16[256,1024]{1,0:T(8,128)(2,1)S(1)}, u32[]{:S(2)}, u32[]{:S(2)}) collective-permute-start(bf16[256,1024]{1,0:T(8,128)(2,1)} %bitcast.19), channel_id=1, source_target_pairs={{0,16},{8,24},{16,0},{24,8},{1,17},{9,25},{17,1},{25,9},{2,18},{10... | collective-permute-start | bytes 1572872 | tf_op jit(solution)/shard_map/ppermute | solution.py:255
  5.2 1.0 %copy-done = bf16[1,256,1024]{2,1,0:T(8,128)(2,1)S(1)} copy-done((bf16[1,256,1024]{2,1,0:T(8,128)(2,1)S(1)}, bf16[1,256,1024]{2,1,0:T(8,128)(2,1)}, u32[]{:S(2)}) %copy-start) | copy-done | bytes 524312
  6.2 1.0 %copy-done.2 = bf16[1,256,1024]{2,1,0:T(8,128)(2,1)S(1)} copy-done((bf16[1,256,1024]{2,1,0:T(8,128)(2,1)S(1)}, bf16[1,256,1024]{2,1,0:T(8,128)(2,1)}, u32[]{:S(2)}) %copy-start.2) | copy-done | bytes 524312
  7.2 0.6 pool.1
  7.9 1.6 %collective-permute-start.1 = (bf16[2,64,1024]{2,1,0:T(8,128)(2,1)S(1)}, bf16[2,64,1024]{2,1,0:T(8,128)(2,1)S(1)}, u32[]{:S(2)}, u32[]{:S(2)}) collective-permute-start(bf16[2,64,1024]{2,1,0:T(8,128)(2,1)S(1)} %get-tuple-element.42.refs_1_), channel_id=1, source_target_pairs={{0,2},{1,3},{2,0},{3,1},{4,6},{5,7},{6,4},{7,5},{8,10},{9,11},{10,... | collective-permute-start | bytes 786440 | tf_op jit(solution)/shard_map/ppermute | solution.py:255
  9.5 0.0 collective-permute-start
  9.5 2.6 %collective-permute-start.3 = (bf16[2,32,1024]{2,1,0:T(8,128)(2,1)S(1)}, bf16[2,32,1024]{2,1,0:T(8,128)(2,1)S(1)}, u32[]{:S(2)}, u32[]{:S(2)}) collective-permute-start(bf16[2,32,1024]{2,1,0:T(8,128)(2,1)S(1)} %get-tuple-element.43.refs_2_), channel_id=1, source_target_pairs={{0,4},{1,5},{2,6},{3,7},{4,0},{5,1},{6,2},{7,3},{8,12},{9,13},{10,... | collective-permute-start | bytes 393224 | tf_op jit(solution)/shard_map/ppermute | solution.py:255
  12.1 5.2 %collective-permute-done.3.refs_6_.refs_3_ = bf16[2,32,1024]{2,1,0:T(8,128)(2,1)S(1)} collective-permute-done((bf16[2,32,1024]{2,1,0:T(8,128)(2,1)S(1)}, bf16[2,32,1024]{2,1,0:T(8,128)(2,1)S(1)}, u32[]{:S(2)}, u32[]{:S(2)}) %collective-permute-start.3) | collective-permute-done | bytes 131104 | tf_op jit(solution)/shard_map/ppermute | solution.py:255
  17.3 3.0 %collective-permute-start.5 = (bf16[2,32,1024]{2,1,0:T(8,128)(2,1)S(1)}, bf16[2,32,1024]{2,1,0:T(8,128)(2,1)S(1)}, u32[]{:S(2)}, u32[]{:S(2)}) collective-permute-start(bf16[2,32,1024]{2,1,0:T(8,128)(2,1)S(1)} %get-tuple-element.43.refs_2_), channel_id=1, source_target_pairs={{0,6},{1,7},{2,4},{3,5},{4,2},{5,3},{6,0},{7,1},{8,14},{9,15},{10,... | collective-permute-start | bytes 393224 | tf_op jit(solution)/shard_map/ppermute | solution.py:255
  20.3 0.0 collective-permute-done.1.refs_4_.refs_1_
  20.3 0.0 collective-permute-start.4
  20.3 0.0 collective-permute-done.17.refs_5_
  20.3 0.5 collective-permute-start.2
  20.8 0.0 copy-start.1
  20.8 0.0 copy-start.3
  20.8 0.0 collective-permute-done.18.refs_6_
  20.9 0.6 collective-permute-start.19
  21.4 2.7 %collective-permute-done.5.refs_8_.refs_5_ = bf16[2,32,1024]{2,1,0:T(8,128)(2,1)S(1)} collective-permute-done((bf16[2,32,1024]{2,1,0:T(8,128)(2,1)S(1)}, bf16[2,32,1024]{2,1,0:T(8,128)(2,1)S(1)}, u32[]{:S(2)}, u32[]{:S(2)}) %collective-permute-start.5) | collective-permute-done | bytes 131104 | tf_op jit(solution)/shard_map/ppermute | solution.py:255
  24.1 0.5 collective-permute-start.20
  24.7 0.0 collective-permute-done.4.refs_7_.refs_4_
  24.7 0.0 collective-permute-start.6
  24.7 0.0 copy-start.5
  24.7 1.0 %copy-done.5 = bf16[1,256,1024]{2,1,0:T(8,128)(2,1)S(1)} copy-done((bf16[1,256,1024]{2,1,0:T(8,128)(2,1)S(1)}, bf16[1,256,1024]{2,1,0:T(8,128)(2,1)}, u32[]{:S(2)}) %copy-start.5) | copy-done | bytes 524312
  25.7 1.0 %copy-done.10 = bf16[1,256,1024]{2,1,0:T(8,128)(2,1)S(1)} copy-done((bf16[1,256,1024]{2,1,0:T(8,128)(2,1)S(1)}, bf16[1,256,1024]{2,1,0:T(8,128)(2,1)}, u32[]{:S(2)}) %copy-start.10) | copy-done | bytes 524312
  26.8 1.4 %early.1 = (bf16[3,256,1024]{2,1,0:T(8,128)(2,1)S(1)}, bf16[256,1024]{1,0:T(8,128)(2,1)S(1)}, bf16[128,1024]{1,0:T(8,128)(2,1)S(1)}, bf16[64,1024]{1,0:T(8,128)(2,1)S(1)}, bf16[32,1024]{1,0:T(8,128)(2,1)S(1)}) custom-call(bf16[256,1024]{1,0:T(8,128)(2,1)S(1)} %bitcast.15, bf16[256,1024]{1,0:T(8,128)(2,1)S(1)} %bitcast.20, bf16[1024,1024]{1,0:T(8,128)(2,1)S(1)} %copy-done.4), custom_call_target="tpu_custom_call" | custom-call | flops 939524096 | bytes 5701632 | tf_op jit(solution)/shard_map/early/pallas_call | solution.py:47
  28.2 1.1 %copy-done.9 = bf16[3,256,1024]{2,1,0:T(8,128)(2,1)} copy-done((bf16[3,256,1024]{2,1,0:T(8,128)(2,1)}, bf16[3,256,1024]{2,1,0:T(8,128)(2,1)S(1)}, u32[]{:S(2)}) %copy-start.9) | copy-done | bytes 1572888
  29.4 0.0 collective-permute-done.6.refs_9_.refs_6_
  29.4 0.0 collective-permute-done.2.refs_5_.refs_2_
  29.4 0.0 collective-permute-done.refs_3_.refs_0_
  29.4 0.0 copy-start.7
  29.4 0.8 copy-done.7
  30.2 10.1 %forward.1 = (bf16[8,256,640]{2,1,0:T(8,128)(2,1)}, bf16[256,1024]{1,0:T(8,128)(2,1)S(1)}, f32[256,128]{1,0:T(8,128)S(1)}, bf16[256,1024]{1,0:T(8,128)(2,1)S(1)}...) custom-call(bf16[256,1024]{1,0:T(8,128)(2,1)S(1)} %bitcast.16, ...), custom_call_target="tpu_custom_call" | custom-call | flops 1006632960 | bytes 11001856 | tf_op jit(solution)/shard_map/forward/pallas_call | solution.py:47
  40.3 1.5 %collective-permute-start.14 = (bf16[256,256]{1,0:T(8,128)(2,1)S(1)}, bf16[256,256]{1,0:T(8,128)(2,1)S(1)}, u32[]{:S(2)}, u32[]{:S(2)}) collective-permute-start(bf16[256,256]{1,0:T(8,128)(2,1)S(1)} %get-tuple-element.58), channel_id=1, source_target_pairs={{0,8},{8,0},{16,24},{24,16},{1,9},{9,1},{17,25},{25,17},{2,10},{10... | collective-permute-start | bytes 393224 | tf_op jit(solution)/shard_map/ppermute | solution.py:255
  41.8 0.5 collective-permute-start.15
  42.3 1.5 %collective-permute-start.16 = (bf16[256,256]{1,0:T(8,128)(2,1)S(1)}, bf16[256,256]{1,0:T(8,128)(2,1)S(1)}, u32[]{:S(2)}, u32[]{:S(2)}) collective-permute-start(bf16[256,256]{1,0:T(8,128)(2,1)S(1)} %get-tuple-element.60), channel_id=1, source_target_pairs={{0,24},{8,16},{16,8},{24,0},{1,25},{9,17},{17,9},{25,1},{2,26},{10... | collective-permute-start | bytes 393224 | tf_op jit(solution)/shard_map/ppermute | solution.py:255
  43.8 0.0 collective-permute-done.19
  43.8 2.9 %collective-permute-start.8 = (bf16[64,2176]{1,0:T(8,128)(2,1)S(1)}, bf16[64,2176]{1,0:T(8,128)(2,1)S(1)}, u32[]{:S(2)}, u32[]{:S(2)}) collective-permute-start(bf16[64,2176]{1,0:T(8,128)(2,1)S(1)} %get-tuple-element.51), channel_id=1, source_target_pairs={{0,2},{1,3},{2,0},{3,1},{4,6},{5,7},{6,4},{7,5},{8,10},{9,11},{10,... | collective-permute-start | bytes 835592 | tf_op jit(solution)/shard_map/ppermute | solution.py:255
  46.7 0.0 collective-permute-done.20
  46.7 0.8 %collective-permute-start.10 = (bf16[32,2176]{1,0:T(8,128)(2,1)S(1)}, bf16[32,2176]{1,0:T(8,128)(2,1)S(1)}, u32[]{:S(2)}, u32[]{:S(2)}) collective-permute-start(bf16[32,2176]{1,0:T(8,128)(2,1)S(1)} %get-tuple-element.52), channel_id=1, source_target_pairs={{0,4},{1,5},{2,6},{3,7},{4,0},{5,1},{6,2},{7,3},{8,12},{9,13},{10,... | collective-permute-start | bytes 417800 | tf_op jit(solution)/shard_map/ppermute | solution.py:255
  47.6 0.0 collective-permute-done.14.refs_1_
  47.6 2.2 %collective-permute-start.12 = (bf16[32,2176]{1,0:T(8,128)(2,1)S(1)}, bf16[32,2176]{1,0:T(8,128)(2,1)S(1)}, u32[]{:S(2)}, u32[]{:S(2)}) collective-permute-start(bf16[32,2176]{1,0:T(8,128)(2,1)S(1)} %get-tuple-element.52), channel_id=1, source_target_pairs={{0,6},{1,7},{2,4},{3,5},{4,2},{5,3},{6,0},{7,1},{8,14},{9,15},{10,... | collective-permute-start | bytes 417800 | tf_op jit(solution)/shard_map/ppermute | solution.py:255
  49.8 0.5 collective-permute-done.15.refs_2_
  50.2 0.0 collective-permute-start.7
  50.3 0.0 collective-permute-done.16.refs_3_
  50.3 0.8 weight.1
  51.1 0.6 collective-permute-start.21
  51.6 5.2 %collective-permute-done.10.refs_6_ = bf16[32,2176]{1,0:T(8,128)(2,1)S(1)} collective-permute-done((bf16[32,2176]{1,0:T(8,128)(2,1)S(1)}, bf16[32,2176]{1,0:T(8,128)(2,1)S(1)}, u32[]{:S(2)}, u32[]{:S(2)}) %collective-permute-start.10) | collective-permute-done | bytes 139296 | tf_op jit(solution)/shard_map/ppermute | solution.py:255
  56.8 0.0 collective-permute-start.11
  56.8 4.3 %collective-permute-done.12.refs_8_ = bf16[32,2176]{1,0:T(8,128)(2,1)S(1)} collective-permute-done((bf16[32,2176]{1,0:T(8,128)(2,1)S(1)}, bf16[32,2176]{1,0:T(8,128)(2,1)S(1)}, u32[]{:S(2)}, u32[]{:S(2)}) %collective-permute-start.12) | collective-permute-done | bytes 139296 | tf_op jit(solution)/shard_map/ppermute | solution.py:255
  61.1 0.0 collective-permute-start.13
  61.1 0.0 collective-permute-done.8.refs_4_
  61.1 0.5 collective-permute-start.9
  61.6 7.6 %backward.1 = (f32[256,1024]{1,0:T(8,128)}, bf16[256,1024]{1,0:T(8,128)(2,1)S(1)}, bf16[256,1024]{1,0:T(8,128)(2,1)S(1)}, bf16[256,1024]{1,0:T(8,128)(2,1)}) custom-call(bf16[8,256,640]{2,1,0:T(8,128)(2,1)} %get-tuple-element.44.e_ref, bf16[256,1024]{1,0:T(8,128)(2,1)S(1)} %get-tuple-element.45.gr_ref, f32[256,128]{1,0:T(8,128)S(1)} %get-tuple-element.46.dd_ref, ...), custom_call_target="tpu_custom_call" | custom-call | flops 1677721600 | bytes 8388608 | tf_op jit(solution)/shard_map/backward/pallas_call | solution.py:371
  69.2 0.0 collective-permute-done.21.got_ref
  69.3 1.1 %collective-permute-start.22 = (bf16[32,1024]{1,0:T(8,128)(2,1)S(1)}, bf16[32,1024]{1,0:T(8,128)(2,1)S(1)}, u32[]{:S(2)}, u32[]{:S(2)}) collective-permute-start(bf16[32,1024]{1,0:T(8,128)(2,1)S(1)} %get-tuple-element.64), channel_id=1, source_target_pairs={{0,2},{1,3},{2,0},{3,1},{4,6},{5,7},{6,4},{7,5},{8,10},{9,11},{10,... | collective-permute-start | bytes 196616 | tf_op jit(solution)/shard_map/ppermute | solution.py:255
  70.4 0.0 collective-permute-done.11.refs_7_
  70.4 1.2 %collective-permute-start.23 = (bf16[32,1024]{1,0:T(8,128)(2,1)S(1)}, bf16[32,1024]{1,0:T(8,128)(2,1)S(1)}, u32[]{:S(2)}, u32[]{:S(2)}) collective-permute-start(bf16[32,1024]{1,0:T(8,128)(2,1)S(1)} %get-tuple-element.65), channel_id=1, source_target_pairs={{0,4},{1,5},{2,6},{3,7},{4,0},{5,1},{6,2},{7,3},{8,12},{9,13},{10,... | collective-permute-start | bytes 196616 | tf_op jit(solution)/shard_map/ppermute | solution.py:255
  71.6 0.0 collective-permute-done.13.refs_9_
  71.6 2.1 %collective-permute-start.24 = (bf16[32,1024]{1,0:T(8,128)(2,1)S(1)}, bf16[32,1024]{1,0:T(8,128)(2,1)S(1)}, u32[]{:S(2)}, u32[]{:S(2)}) collective-permute-start(bf16[32,1024]{1,0:T(8,128)(2,1)S(1)} %get-tuple-element.66), channel_id=1, source_target_pairs={{0,6},{1,7},{2,4},{3,5},{4,2},{5,3},{6,0},{7,1},{8,14},{9,15},{10,... | collective-permute-start | bytes 196616 | tf_op jit(solution)/shard_map/ppermute | solution.py:255
  73.7 2.1 %convert_bitcast_fusion = bf16[1,256,1024]{2,1,0:T(8,128)(2,1)} fusion(f32[256,1024]{1,0:T(8,128)} %get-tuple-element.49), kind=kLoop, calls=%fused_computation.1 | loop fusion | flops 262144 | bytes 1572864 | tf_op jit(solution)/shard_map/broadcast_in_dim | solution.py:411
  75.8 0.0 collective-permute-done.9.refs_5_
  75.8 5.4 %owner.1 = (bf16[256,1024]{1,0:T(8,128)(2,1)}, bf16[256,1024]{1,0:T(8,128)(2,1)}) custom-call(bf16[2,128,1024]{2,1,0:T(8,128)(2,1)S(1)} %get-tuple-element.41.refs_0_, bf16[2,64,1024]{2,1,0:T(8,128)(2,1)S(1)} %get-tuple-element.42.refs_1_, bf16[2,32,1024]{2,1,0:T(8,128)(2,1)S(1)} %get-tuple-element.43.refs_2_, ...), custom_call_target="tpu_custom_call" | custom-call | flops 234881024 | bytes 5242880 | tf_op jit(solution)/shard_map/owner/pallas_call | solution.py:391
  81.3 0.7 total.1
  (22 shorter events, 0.2 us)
Async XLA Ops:
  0.6 19.7 %collective-permute-start.17 = (bf16[256,1024]{1,0:T(8,128)(2,1)}, bf16[256,1024]{1,0:T(8,128)(2,1)S(1)}, u32[]{:S(2)}, u32[]{:S(2)}) collective-permute-start(bf16[256,1024]{1,0:T(8,128)(2,1)} %bitcast.18), channel_id=1, source_target_pairs={{0,8},{8,0},{16,24},{24,16},{1,9},{9,1},{17,25},{25,17},{2,10},{10... | collective-permute-start | bytes 1572872 | tf_op jit(solution)/shard_map/ppermute | solution.py:255
  3.6 17.2 %collective-permute-start.18 = (bf16[256,1024]{1,0:T(8,128)(2,1)}, bf16[256,1024]{1,0:T(8,128)(2,1)S(1)}, u32[]{:S(2)}, u32[]{:S(2)}) collective-permute-start(bf16[256,1024]{1,0:T(8,128)(2,1)} %bitcast.19), channel_id=1, source_target_pairs={{0,16},{8,24},{16,0},{24,8},{1,17},{9,25},{17,1},{25,9},{2,18},{10... | collective-permute-start | bytes 1572872 | tf_op jit(solution)/shard_map/ppermute | solution.py:255
  5.2 1.0 %copy-start = (bf16[1,256,1024]{2,1,0:T(8,128)(2,1)S(1)}, bf16[1,256,1024]{2,1,0:T(8,128)(2,1)}, u32[]{:S(2)}) copy-start(bf16[1,256,1024]{2,1,0:T(8,128)(2,1)} %param.6) | copy-start | bytes 1572868
  6.2 1.0 %copy-start.2 = (bf16[1,256,1024]{2,1,0:T(8,128)(2,1)S(1)}, bf16[1,256,1024]{2,1,0:T(8,128)(2,1)}, u32[]{:S(2)}) copy-start(bf16[1,256,1024]{2,1,0:T(8,128)(2,1)} %param.7) | copy-start | bytes 1572868
  7.2 17.4 %copy-start.4 = (bf16[1024,1024]{1,0:T(8,128)(2,1)S(1)}, bf16[1024,1024]{1,0:T(8,128)(2,1)}, u32[]{:S(2)}) copy-start(bf16[1024,1024]{1,0:T(8,128)(2,1)} %refs_8_.1) | copy-start | bytes 6291460
  7.9 12.4 %collective-permute-start.1 = (bf16[2,64,1024]{2,1,0:T(8,128)(2,1)S(1)}, bf16[2,64,1024]{2,1,0:T(8,128)(2,1)S(1)}, u32[]{:S(2)}, u32[]{:S(2)}) collective-permute-start(bf16[2,64,1024]{2,1,0:T(8,128)(2,1)S(1)} %get-tuple-element.42.refs_1_), channel_id=1, source_target_pairs={{0,2},{1,3},{2,0},{3,1},{4,6},{5,7},{6,4},{7,5},{8,10},{9,11},{10,... | collective-permute-start | bytes 786440 | tf_op jit(solution)/shard_map/ppermute | solution.py:255
  9.5 19.9 %collective-permute-start = (bf16[2,128,1024]{2,1,0:T(8,128)(2,1)S(1)}, bf16[2,128,1024]{2,1,0:T(8,128)(2,1)S(1)}, u32[]{:S(2)}, u32[]{:S(2)}) collective-permute-start(bf16[2,128,1024]{2,1,0:T(8,128)(2,1)S(1)} %get-tuple-element.41.refs_0_), channel_id=1, source_target_pairs={{0,1},{1,0},{2,3},{3,2},{4,5},{5,4},{6,7},{7,6},{8,9},{9,8},{10,11... | collective-permute-start | bytes 1572872 | tf_op jit(solution)/shard_map/ppermute | solution.py:255
  9.5 7.8 %collective-permute-start.3 = (bf16[2,32,1024]{2,1,0:T(8,128)(2,1)S(1)}, bf16[2,32,1024]{2,1,0:T(8,128)(2,1)S(1)}, u32[]{:S(2)}, u32[]{:S(2)}) collective-permute-start(bf16[2,32,1024]{2,1,0:T(8,128)(2,1)S(1)} %get-tuple-element.43.refs_2_), channel_id=1, source_target_pairs={{0,4},{1,5},{2,6},{3,7},{4,0},{5,1},{6,2},{7,3},{8,12},{9,13},{10,... | collective-permute-start | bytes 393224 | tf_op jit(solution)/shard_map/ppermute | solution.py:255
  17.3 6.8 %collective-permute-start.5 = (bf16[2,32,1024]{2,1,0:T(8,128)(2,1)S(1)}, bf16[2,32,1024]{2,1,0:T(8,128)(2,1)S(1)}, u32[]{:S(2)}, u32[]{:S(2)}) collective-permute-start(bf16[2,32,1024]{2,1,0:T(8,128)(2,1)S(1)} %get-tuple-element.43.refs_2_), channel_id=1, source_target_pairs={{0,6},{1,7},{2,4},{3,5},{4,2},{5,3},{6,0},{7,1},{8,14},{9,15},{10,... | collective-permute-start | bytes 393224 | tf_op jit(solution)/shard_map/ppermute | solution.py:255
  20.3 4.4 %collective-permute-start.4 = (bf16[2,32,1024]{2,1,0:T(8,128)(2,1)S(1)}, bf16[2,32,1024]{2,1,0:T(8,128)(2,1)S(1)}, u32[]{:S(2)}, u32[]{:S(2)}) collective-permute-start(bf16[2,32,1024]{2,1,0:T(8,128)(2,1)S(1)} %collective-permute-done.3.refs_6_.refs_3_), channel_id=1, source_target_pairs={{0,1},{1,0},{2,3},{3,2},{4,5},{5,4},{6,7},{7,6},{8,9},{9,8},{10,11... | collective-permute-start | bytes 393224 | tf_op jit(solution)/shard_map/ppermute | solution.py:255
  20.3 9.1 %collective-permute-start.2 = (bf16[2,64,1024]{2,1,0:T(8,128)(2,1)S(1)}, bf16[2,64,1024]{2,1,0:T(8,128)(2,1)S(1)}, u32[]{:S(2)}, u32[]{:S(2)}) collective-permute-start(bf16[2,64,1024]{2,1,0:T(8,128)(2,1)S(1)} %collective-permute-done.1.refs_4_.refs_1_), channel_id=1, source_target_pairs={{0,1},{1,0},{2,3},{3,2},{4,5},{5,4},{6,7},{7,6},{8,9},{9,8},{10,11... | collective-permute-start | bytes 786440 | tf_op jit(solution)/shard_map/ppermute | solution.py:255
  20.8 9.4 %copy-start.1 = (bf16[1,256,1024]{2,1,0:T(8,128)(2,1)S(1)}, bf16[1,256,1024]{2,1,0:T(8,128)(2,1)}, u32[]{:S(2)}) copy-start(bf16[1,256,1024]{2,1,0:T(8,128)(2,1)} %param.6) | copy-start | bytes 1572868
  20.8 9.3 %copy-start.3 = (bf16[1,256,1024]{2,1,0:T(8,128)(2,1)S(1)}, bf16[1,256,1024]{2,1,0:T(8,128)(2,1)}, u32[]{:S(2)}) copy-start(bf16[1,256,1024]{2,1,0:T(8,128)(2,1)} %param.7) | copy-start | bytes 1572868
  20.9 23.0 %collective-permute-start.19 = (bf16[128,1024]{1,0:T(8,128)(2,1)S(1)}, bf16[128,1024]{1,0:T(8,128)(2,1)S(1)}, u32[]{:S(2)}, u32[]{:S(2)}) collective-permute-start(bf16[128,1024]{1,0:T(8,128)(2,1)S(1)} %slice.8), channel_id=1, source_target_pairs={{0,16},{8,24},{16,0},{24,8},{1,17},{9,25},{17,1},{25,9},{2,18},{10... | collective-permute-start | bytes 786440 | tf_op jit(solution)/shard_map/ppermute | solution.py:255
  24.1 22.5 %collective-permute-start.20 = (bf16[128,1024]{1,0:T(8,128)(2,1)S(1)}, bf16[128,1024]{1,0:T(8,128)(2,1)S(1)}, u32[]{:S(2)}, u32[]{:S(2)}) collective-permute-start(bf16[128,1024]{1,0:T(8,128)(2,1)S(1)} %slice.9), channel_id=1, source_target_pairs={{0,8},{8,0},{16,24},{24,16},{1,9},{9,1},{17,25},{25,17},{2,10},{10... | collective-permute-start | bytes 786440 | tf_op jit(solution)/shard_map/ppermute | solution.py:255
  24.7 4.7 %collective-permute-start.6 = (bf16[2,32,1024]{2,1,0:T(8,128)(2,1)S(1)}, bf16[2,32,1024]{2,1,0:T(8,128)(2,1)S(1)}, u32[]{:S(2)}, u32[]{:S(2)}) collective-permute-start(bf16[2,32,1024]{2,1,0:T(8,128)(2,1)S(1)} %collective-permute-done.5.refs_8_.refs_5_), channel_id=1, source_target_pairs={{0,1},{1,0},{2,3},{3,2},{4,5},{5,4},{6,7},{7,6},{8,9},{9,8},{10,11... | collective-permute-start | bytes 393224 | tf_op jit(solution)/shard_map/ppermute | solution.py:255
  24.7 1.0 %copy-start.5 = (bf16[1,256,1024]{2,1,0:T(8,128)(2,1)S(1)}, bf16[1,256,1024]{2,1,0:T(8,128)(2,1)}, u32[]{:S(2)}) copy-start(bf16[1,256,1024]{2,1,0:T(8,128)(2,1)} %param.5) | copy-start | bytes 1572868
  25.7 1.0 %copy-start.10 = (bf16[1,256,1024]{2,1,0:T(8,128)(2,1)S(1)}, bf16[1,256,1024]{2,1,0:T(8,128)(2,1)}, u32[]{:S(2)}) copy-start(bf16[1,256,1024]{2,1,0:T(8,128)(2,1)} %param.8) | copy-start | bytes 1572868
  28.2 1.1 %copy-start.9 = (bf16[3,256,1024]{2,1,0:T(8,128)(2,1)}, bf16[3,256,1024]{2,1,0:T(8,128)(2,1)S(1)}, u32[]{:S(2)}) copy-start(bf16[3,256,1024]{2,1,0:T(8,128)(2,1)S(1)} %get-tuple-element.36.qhat_ref) | copy-start | bytes 4718596
  29.4 0.8 copy-start.7
  30.2 20.1 %copy-start.11 = (bf16[1,256,1024]{2,1,0:T(8,128)(2,1)S(1)}, bf16[1,256,1024]{2,1,0:T(8,128)(2,1)}, u32[]{:S(2)}) copy-start(bf16[1,256,1024]{2,1,0:T(8,128)(2,1)} %param.8) | copy-start | bytes 1572868
  40.3 21.3 %copy-start.6 = (bf16[1,256,1024]{2,1,0:T(8,128)(2,1)S(1)}, bf16[1,256,1024]{2,1,0:T(8,128)(2,1)}, u32[]{:S(2)}) copy-start(bf16[1,256,1024]{2,1,0:T(8,128)(2,1)} %param.5) | copy-start | bytes 1572868
  40.3 21.3 %copy-start.8 = (bf16[2,128,1024]{2,1,0:T(8,128)(2,1)S(1)}, bf16[2,128,1024]{2,1,0:T(8,128)(2,1)}, u32[]{:S(2)}) copy-start(bf16[2,128,1024]{2,1,0:T(8,128)(2,1)} %copy-done.7) | copy-start | bytes 1572868
  40.3 7.2 %collective-permute-start.14 = (bf16[256,256]{1,0:T(8,128)(2,1)S(1)}, bf16[256,256]{1,0:T(8,128)(2,1)S(1)}, u32[]{:S(2)}, u32[]{:S(2)}) collective-permute-start(bf16[256,256]{1,0:T(8,128)(2,1)S(1)} %get-tuple-element.58), channel_id=1, source_target_pairs={{0,8},{8,0},{16,24},{24,16},{1,9},{9,1},{17,25},{25,17},{2,10},{10... | collective-permute-start | bytes 393224 | tf_op jit(solution)/shard_map/ppermute | solution.py:255
  41.8 8.4 %collective-permute-start.15 = (bf16[256,256]{1,0:T(8,128)(2,1)S(1)}, bf16[256,256]{1,0:T(8,128)(2,1)S(1)}, u32[]{:S(2)}, u32[]{:S(2)}) collective-permute-start(bf16[256,256]{1,0:T(8,128)(2,1)S(1)} %get-tuple-element.59), channel_id=1, source_target_pairs={{0,16},{8,24},{16,0},{24,8},{1,17},{9,25},{17,1},{25,9},{2,18},{10... | collective-permute-start | bytes 393224 | tf_op jit(solution)/shard_map/ppermute | solution.py:255
  42.3 7.9 %collective-permute-start.16 = (bf16[256,256]{1,0:T(8,128)(2,1)S(1)}, bf16[256,256]{1,0:T(8,128)(2,1)S(1)}, u32[]{:S(2)}, u32[]{:S(2)}) collective-permute-start(bf16[256,256]{1,0:T(8,128)(2,1)S(1)} %get-tuple-element.60), channel_id=1, source_target_pairs={{0,24},{8,16},{16,8},{24,0},{1,25},{9,17},{17,9},{25,1},{2,26},{10... | collective-permute-start | bytes 393224 | tf_op jit(solution)/shard_map/ppermute | solution.py:255
  43.8 17.3 %collective-permute-start.8 = (bf16[64,2176]{1,0:T(8,128)(2,1)S(1)}, bf16[64,2176]{1,0:T(8,128)(2,1)S(1)}, u32[]{:S(2)}, u32[]{:S(2)}) collective-permute-start(bf16[64,2176]{1,0:T(8,128)(2,1)S(1)} %get-tuple-element.51), channel_id=1, source_target_pairs={{0,2},{1,3},{2,0},{3,1},{4,6},{5,7},{6,4},{7,5},{8,10},{9,11},{10,... | collective-permute-start | bytes 835592 | tf_op jit(solution)/shard_map/ppermute | solution.py:255
  46.7 10.1 %collective-permute-start.10 = (bf16[32,2176]{1,0:T(8,128)(2,1)S(1)}, bf16[32,2176]{1,0:T(8,128)(2,1)S(1)}, u32[]{:S(2)}, u32[]{:S(2)}) collective-permute-start(bf16[32,2176]{1,0:T(8,128)(2,1)S(1)} %get-tuple-element.52), channel_id=1, source_target_pairs={{0,4},{1,5},{2,6},{3,7},{4,0},{5,1},{6,2},{7,3},{8,12},{9,13},{10,... | collective-permute-start | bytes 417800 | tf_op jit(solution)/shard_map/ppermute | solution.py:255
  47.6 13.5 %collective-permute-start.12 = (bf16[32,2176]{1,0:T(8,128)(2,1)S(1)}, bf16[32,2176]{1,0:T(8,128)(2,1)S(1)}, u32[]{:S(2)}, u32[]{:S(2)}) collective-permute-start(bf16[32,2176]{1,0:T(8,128)(2,1)S(1)} %get-tuple-element.52), channel_id=1, source_target_pairs={{0,6},{1,7},{2,4},{3,5},{4,2},{5,3},{6,0},{7,1},{8,14},{9,15},{10,... | collective-permute-start | bytes 417800 | tf_op jit(solution)/shard_map/ppermute | solution.py:255
  50.2 25.6 %collective-permute-start.7 = (bf16[128,2176]{1,0:T(8,128)(2,1)}, bf16[128,2176]{1,0:T(8,128)(2,1)S(1)}, u32[]{:S(2)}, u32[]{:S(2)}) collective-permute-start(bf16[128,2176]{1,0:T(8,128)(2,1)} %get-tuple-element.50), channel_id=1, source_target_pairs={{0,1},{1,0},{2,3},{3,2},{4,5},{5,4},{6,7},{7,6},{8,9},{9,8},{10,11... | collective-permute-start | bytes 1671176 | tf_op jit(solution)/shard_map/ppermute | solution.py:255
  51.1 18.2 %collective-permute-start.21 = (bf16[128,1024]{1,0:T(8,128)(2,1)S(1)}, bf16[128,1024]{1,0:T(8,128)(2,1)S(1)}, u32[]{:S(2)}, u32[]{:S(2)}) collective-permute-start(bf16[128,1024]{1,0:T(8,128)(2,1)S(1)} %get-tuple-element.62), channel_id=1, source_target_pairs={{0,1},{1,0},{2,3},{3,2},{4,5},{5,4},{6,7},{7,6},{8,9},{9,8},{10,11... | collective-permute-start | bytes 786440 | tf_op jit(solution)/shard_map/ppermute | solution.py:255
  56.8 13.6 %collective-permute-start.11 = (bf16[32,2176]{1,0:T(8,128)(2,1)S(1)}, bf16[32,2176]{1,0:T(8,128)(2,1)S(1)}, u32[]{:S(2)}, u32[]{:S(2)}) collective-permute-start(bf16[32,2176]{1,0:T(8,128)(2,1)S(1)} %collective-permute-done.10.refs_6_), channel_id=1, source_target_pairs={{0,1},{1,0},{2,3},{3,2},{4,5},{5,4},{6,7},{7,6},{8,9},{9,8},{10,11... | collective-permute-start | bytes 417800 | tf_op jit(solution)/shard_map/ppermute | solution.py:255
  61.1 10.5 %collective-permute-start.13 = (bf16[32,2176]{1,0:T(8,128)(2,1)S(1)}, bf16[32,2176]{1,0:T(8,128)(2,1)S(1)}, u32[]{:S(2)}, u32[]{:S(2)}) collective-permute-start(bf16[32,2176]{1,0:T(8,128)(2,1)S(1)} %collective-permute-done.12.refs_8_), channel_id=1, source_target_pairs={{0,1},{1,0},{2,3},{3,2},{4,5},{5,4},{6,7},{7,6},{8,9},{9,8},{10,11... | collective-permute-start | bytes 417800 | tf_op jit(solution)/shard_map/ppermute | solution.py:255
  61.1 14.7 %collective-permute-start.9 = (bf16[64,2176]{1,0:T(8,128)(2,1)S(1)}, bf16[64,2176]{1,0:T(8,128)(2,1)S(1)}, u32[]{:S(2)}, u32[]{:S(2)}) collective-permute-start(bf16[64,2176]{1,0:T(8,128)(2,1)S(1)} %collective-permute-done.8.refs_4_), channel_id=1, source_target_pairs={{0,1},{1,0},{2,3},{3,2},{4,5},{5,4},{6,7},{7,6},{8,9},{9,8},{10,11... | collective-permute-start | bytes 835592 | tf_op jit(solution)/shard_map/ppermute | solution.py:255
  69.3 12.0 %collective-permute-start.22 = (bf16[32,1024]{1,0:T(8,128)(2,1)S(1)}, bf16[32,1024]{1,0:T(8,128)(2,1)S(1)}, u32[]{:S(2)}, u32[]{:S(2)}) collective-permute-start(bf16[32,1024]{1,0:T(8,128)(2,1)S(1)} %get-tuple-element.64), channel_id=1, source_target_pairs={{0,2},{1,3},{2,0},{3,1},{4,6},{5,7},{6,4},{7,5},{8,10},{9,11},{10,... | collective-permute-start | bytes 196616 | tf_op jit(solution)/shard_map/ppermute | solution.py:255
  70.4 10.9 %collective-permute-start.23 = (bf16[32,1024]{1,0:T(8,128)(2,1)S(1)}, bf16[32,1024]{1,0:T(8,128)(2,1)S(1)}, u32[]{:S(2)}, u32[]{:S(2)}) collective-permute-start(bf16[32,1024]{1,0:T(8,128)(2,1)S(1)} %get-tuple-element.65), channel_id=1, source_target_pairs={{0,4},{1,5},{2,6},{3,7},{4,0},{5,1},{6,2},{7,3},{8,12},{9,13},{10,... | collective-permute-start | bytes 196616 | tf_op jit(solution)/shard_map/ppermute | solution.py:255
  71.6 9.7 %collective-permute-start.24 = (bf16[32,1024]{1,0:T(8,128)(2,1)S(1)}, bf16[32,1024]{1,0:T(8,128)(2,1)S(1)}, u32[]{:S(2)}, u32[]{:S(2)}) collective-permute-start(bf16[32,1024]{1,0:T(8,128)(2,1)S(1)} %get-tuple-element.66), channel_id=1, source_target_pairs={{0,6},{1,7},{2,4},{3,5},{4,2},{5,3},{6,0},{7,1},{8,14},{9,15},{10,... | collective-permute-start | bytes 196616 | tf_op jit(solution)/shard_map/ppermute | solution.py:255
where the time goes:
time: 82.4 us; the launch traced here: 82 us
  starting transfers between devices  28.2 us (34%)
  Pallas kernels  26.8 us (33%)
  waiting for transfers between devices  17.9 us (22%)
  local copies, waits for them, and re-layouts  6.15 us (7%)
  other arithmetic  2.13 us (3%)
    ppermute x25, starting transfers between devices, swap(): return lax.ppermute(x, axis, [(i, i ^ mask) for i in range(count)])  28.2 us
    ppermute x25, waiting for transfers between devices, swap(): return lax.ppermute(x, axis, [(i, i ^ mask) for i in range(count)])  17.9 us
    pallas_call x5, Pallas kernels, call(): pl.pallas_call(kernel, name=name, out_shape=[jax.ShapeDtypeStruct(s, t) f...  13 us
    pallas_call x1, Pallas kernels, body(): pl.pallas_call(functools.partial(backward_kernel, levels, pieces), name='...  7.62 us
    unnamed x24, local copies, waits for them, and re-layouts  6.12 us
    pallas_call x1, Pallas kernels, body(): pl.pallas_call(functools.partial(owner_kernel, levels, message_pieces, to...  5.45 us
    broadcast_in_dim x1, other arithmetic, body(): return (mixed[None], gq.astype(BF16)[None], gk[None], gv[None], gw)  2.09 us
  transfers between devices with their start and end apart: 25, of which 5 were waited for; matrix products, arithmetic and copies ran while one was open for 3% of the time, Pallas kernels for 32%

commit v1 on v0

v1 whole, which is shorter than its diff:
```python
import functools
import math

import jax
import jax.numpy as jnp
from jax import lax
from jax.experimental import pallas as pl
from jax.experimental.pallas import tpu as pltpu
from jax.sharding import PartitionSpec as P

HEADS = 8
HEAD_DIM = 128
BLOCK = 128
LANES = 128
SCALE = 1.0 / math.sqrt(HEAD_DIM)
SCALE2 = SCALE / math.log(2.0)
F32 = jnp.float32
BF16 = jnp.bfloat16
COST = 5_000_000_000
VMEM_LIMIT = 24 * 1024 * 1024


def dot(a, b, dims):
    return lax.dot_general(a, b, (dims, ((), ())), preferred_element_type=F32)


def nn(a, b):
    return dot(a, b, ((1,), (0,)))


def nt(a, b):
    return dot(a, b, ((1,), (1,)))


def tn(a, b):
    return dot(a, b, ((0,), (0,)))


def member(rows, cols, row_shift, col_shift, value):
    r = lax.broadcasted_iota(jnp.int32, (rows, cols), 0) >> row_shift
    c = lax.broadcasted_iota(jnp.int32, (rows, cols), 1) >> col_shift
    return jnp.where(r == c, value, 0.0).astype(BF16)


def call(kernel, outs, name, cost, *operands, scratch=(), space=pltpu.VMEM):
    return pl.pallas_call(
        kernel,
        name=name,
        out_shape=[jax.ShapeDtypeStruct(s, t) for s, t in outs],
        in_specs=[pl.BlockSpec(memory_space=space)] * len(operands),
        out_specs=[pl.BlockSpec(memory_space=pltpu.VMEM)] * len(outs),
        scratch_shapes=list(scratch),
        compiler_params=pltpu.CompilerParams(vmem_limit_bytes=VMEM_LIMIT),
        cost_estimate=pl.CostEstimate(flops=cost, bytes_accessed=1, transcendentals=0),
    )(*operands)


def pool_kernel(levels, k_ref, v_ref, *refs):
    outs, (held, sems) = refs[:-2], refs[-2:]
    tokens, width = k_ref.shape
    copies = [
        pltpu.make_async_copy(src, held.at[i], sems.at[i]) for i, src in enumerate((k_ref, v_ref))
    ]
    for copy in copies:
        copy.start()
    pools = [member(tokens >> l, tokens, 0, l, 0.5**l) for l in range(1, levels)]
    for i, copy in enumerate(copies):
        copy.wait()
        for pool, out in zip(pools, outs):
            out[i] = nn(pool, held[i]).astype(BF16)


def early_kernel(levels, q_ref, g_ref, w_ref, qhat_ref, gat_ref, *qls):
    tokens, width = q_ref.shape
    q = q_ref[...]
    for l in range(1, levels):
        qhat_ref[l - 1] = nn(member(tokens, tokens, l, l, 0.5**l), q).astype(BF16)
        qls[l - 1][...] = nn(member(tokens >> l, tokens, 0, l, 0.5**l), q).astype(BF16)
    g = g_ref[...]
    for c in range(0, width, 256):
        gat_ref[c : c + 256, :] = nt(w_ref[c : c + 256, :], g).astype(BF16)


def gathered(levels, pieces, kvs, which, hs):
    out, at = [], 0
    for l in range(1, levels):
        part = kvs[at : at + pieces[l - 1]]
        at += pieces[l - 1]
        out.append(jnp.concatenate([p[which, :, hs] for p in part], axis=0))
    return out


def forward_kernel(levels, pieces, dp, q_ref, k_ref, v_ref, qhat_ref, gat_ref, *refs):
    tokens, width = q_ref.shape
    upper = levels - 1
    count = sum(pieces)
    qls, refs = refs[:upper], refs[upper:]
    kvs, refs = refs[:count], refs[count:]
    e_ref, grt_ref, dd_ref, att_ref = refs[:4]
    blocks, msgs, aux_ref = refs[4 : 4 + dp], refs[4 + dp : -1], refs[-1]
    ones = jnp.ones((16, tokens + upper * BLOCK), BF16)
    sums = [member(tokens >> l, tokens, 0, l, 1.0) for l in range(1, levels)]
    aux_ref[...] = jnp.zeros_like(aux_ref)

    def scores(h):
        hs = slice(h * HEAD_DIM, (h + 1) * HEAD_DIM)
        keys = gathered(levels, pieces, kvs, 0, hs)
        return [nt(k_ref[:, hs], q_ref[:, hs])] + [
            nt(keys[l - 1], qhat_ref[l - 1, :, hs]) for l in range(1, levels)
        ]

    def attend(h, raws):
        hs = slice(h * HEAD_DIM, (h + 1) * HEAD_DIM)
        tops = [jnp.max(raw, axis=0, keepdims=True) for raw in raws]
        top = tops[0] * SCALE2
        for l in range(1, levels):
            top = jnp.maximum(top, tops[l] * SCALE2 + float(l))
        at, es = 0, []
        for l, raw in enumerate(raws):
            es.append(jnp.exp2(raw * SCALE2 + (float(l) - top)).astype(BF16))
            e_ref[h, at : at + raw.shape[0], :] = es[-1]
            at += raw.shape[0]
        vals = jnp.concatenate([v_ref[:, hs]] + gathered(levels, pieces, kvs, 1, hs), axis=0)
        lhs = jnp.concatenate([vals.T, ones], axis=0)
        return top, tops, nn(lhs, jnp.concatenate(es, axis=0))

    def finish(h, top, tops, both):
        hs = slice(h * HEAD_DIM, (h + 1) * HEAD_DIM)
        rden = 1.0 / both[HEAD_DIM : HEAD_DIM + 1]
        att = (both[:HEAD_DIM] * rden).astype(BF16)
        att_ref[hs, :] = att
        grt = gat_ref[hs, :].astype(F32) * rden
        grt_ref[hs, :] = grt.astype(BF16)
        delta = jnp.sum(grt * att.astype(F32), axis=0, keepdims=True)
        dd_ref[h : h + 1, :] = delta
        for l in range(1, levels):
            mu = tops[l].astype(BF16).astype(F32)
            a = jnp.exp2(mu * SCALE2 + (float(l) - top))
            msgs[l - 1][:, hs] = nt(sums[l - 1], (grt * a).astype(BF16)).astype(BF16)
            aux_ref[l - 1, h : h + 1, :] = mu * 0.5**l
            aux_ref[l - 1, HEADS + h : HEADS + h + 1, :] = delta * a

    ahead, behind = scores(0), None
    for h in range(HEADS):
        raws = ahead
        if h + 1 < HEADS:
            ahead = scores(h + 1)
        state = attend(h, raws)
        if behind is not None:
            finish(h - 1, *behind)
        behind = state
    finish(HEADS - 1, *behind)
    me = lax.axis_index("dp")
    span = width // dp
    for m in range(dp):
        at = pl.multiple_of((me ^ m) * span, span)
        blocks[m][...] = att_ref[pl.ds(at, span), :]
    for l in range(1, levels):
        msgs[l - 1][:, width : 2 * width] = qls[l - 1][...]
        msgs[l - 1][:, 2 * width :] = nt(sums[l - 1], aux_ref[l - 1].astype(BF16)).astype(BF16)


def backward_kernel(levels, pieces, e_ref, grt_ref, dd_ref, q_ref, k_ref, v_ref, *refs):
    tokens, width = q_ref.shape
    count = sum(pieces)
    kvs = refs[:count]
    gq_ref, dk_ref, dv_ref, y_ref = refs[count:]
    starts = [0] + [tokens + l * BLOCK for l in range(levels)]

    def probs(h):
        hs = slice(h * HEAD_DIM, (h + 1) * HEAD_DIM)
        vals = jnp.concatenate([v_ref[:, hs]] + gathered(levels, pieces, kvs, 1, hs), axis=0)
        return nn(vals, grt_ref[hs, :])

    def rest(h, dpt):
        hs = slice(h * HEAD_DIM, (h + 1) * HEAD_DIM)
        e = e_ref[h]
        ds = (e.astype(F32) * (dpt - dd_ref[h : h + 1, :])).astype(BF16)
        keys = [k_ref[:, hs]] + gathered(levels, pieces, kvs, 0, hs)
        for l in range(levels):
            part = ds[starts[l] : starts[l + 1]]
            y_ref[hs, l * tokens : (l + 1) * tokens] = tn(keys[l], part).astype(BF16)
        dv_ref[:, hs] = nt(e[:tokens], grt_ref[hs, :]).astype(BF16)
        dk_ref[:, hs] = (nn(ds[:tokens], q_ref[:, hs]) * SCALE).astype(BF16)

    ahead = probs(0)
    for h in range(HEADS):
        dpt = ahead
        if h + 1 < HEADS:
            ahead = probs(h + 1)
        rest(h, dpt)
    spread = jnp.concatenate(
        [member(tokens, tokens, l, l, 0.5**l) for l in range(levels)], axis=1
    )
    for c in range(0, width, 256):
        cs = slice(c, c + 256)
        gq_ref[:, cs] = (nt(spread, y_ref[cs, :]) * SCALE).astype(BF16)


def weight_kernel(dp, nz, *refs):
    atts, refs = refs[:dp], refs[dp:]
    grads, (keep_ref, even_ref, odd_ref, total_ref) = refs[:-4], refs[-4:]
    a = jnp.concatenate([x[...] for x in atts], axis=1)
    width = grads[0].shape[1]
    for c in range(0, width, 256):
        cs = slice(c, c + 256)
        g = jnp.concatenate([x[:, cs] for x in grads], axis=0)
        total_ref[:, cs] = nn(a, g)
    rows = total_ref.shape[0] // (2 * nz)
    seq = lax.axis_index("seq")
    core, z = seq & 1, seq >> 1
    for m in range(nz):
        base = (z ^ m) * 2 * rows
        mine = pl.multiple_of(base + core * rows, rows)
        other = pl.multiple_of(base + (1 - core) * rows, rows)
        keep_ref[m] = total_ref[pl.ds(mine, rows), :]
        send_ref = odd_ref if m % 2 else even_ref
        send_ref[m // 2] = total_ref[pl.ds(other, rows), :].astype(BF16)


def halve_kernel(offset, count, keep_ref, *refs):
    got, relay, (next_ref, send_ref) = refs[:count], refs[count:-2], refs[-2:]
    width = keep_ref.shape[2]

    def total(i):
        if offset is None:
            came = got[i % 2][i // 2]
        else:
            came = got[0][:, offset + i * width : offset + (i + 1) * width]
        return keep_ref[i] + came.astype(F32)

    for i in range(next_ref.shape[0]):
        next_ref[i] = total(2 * i)
        out = total(2 * i + 1).astype(BF16)
        if relay:
            at = relay[0].shape[1] + i * width
            send_ref[:, at : at + width] = out
        else:
            send_ref[i] = out
    if relay:
        send_ref[:, : relay[0].shape[1]] = relay[0][...]


def mixed_kernel(att_ref, w_ref, out_ref):
    att = att_ref[...].T
    for c in range(0, w_ref.shape[1], 256):
        out_ref[:, c : c + 256] = nn(att, w_ref[:, c : c + 256]).astype(BF16)


def final_kernel(factor, keep_ref, got_ref, out_ref):
    out_ref[...] = (keep_ref[0] + got_ref[0].astype(F32)) * factor


def owner_kernel(levels, pieces, tokens, *refs):
    upper = levels - 1
    count = sum(pieces)
    kvs, refs = refs[:upper], refs[upper:]
    msgs, refs = refs[:count], refs[count:]
    dk0_ref, dv0_ref, gk_ref, gv_ref, dks_ref, dvs_ref = refs
    width = dk0_ref.shape[1]
    auxes, at = [], 0
    groups = []
    for l in range(1, levels):
        part = msgs[at : at + pieces[l - 1]]
        at += pieces[l - 1]
        groups.append(part)
        auxes.append(jnp.concatenate([p[:, 2 * width : 2 * width + LANES] for p in part], axis=0))
    lane = lax.broadcasted_iota(jnp.int32, (tokens >> 1, LANES), 1)

    def products(h):
        hs = slice(h * HEAD_DIM, (h + 1) * HEAD_DIM)
        qs = slice(width + h * HEAD_DIM, width + (h + 1) * HEAD_DIM)
        minus_mu = jnp.where(lane == h, -1.0, 0.0).astype(BF16)
        minus_d = jnp.where(lane == HEADS + h, -1.0, 0.0).astype(BF16)
        out = []
        for l in range(1, levels):
            n = tokens >> l
            ga = jnp.concatenate([p[:, hs] for p in groups[l - 1]], axis=0)
            q = jnp.concatenate([p[:, qs] for p in groups[l - 1]], axis=0)
            aux = auxes[l - 1]
            k = jnp.concatenate([kvs[l - 1][0, :, hs], minus_mu[:n]], axis=1)
            v = jnp.concatenate([kvs[l - 1][1, :, hs], minus_d[:n]], axis=1)
            raw = nt(k, jnp.concatenate([q, aux], axis=1))
            out.append((ga, q, raw, nt(v, jnp.concatenate([ga, aux], axis=1))))
        return out

    def gradients(h, parts):
        hs = slice(h * HEAD_DIM, (h + 1) * HEAD_DIM)
        at = 0
        for ga, q, raw, dp_raw in parts:
            n = raw.shape[0]
            e = jnp.exp2(raw * SCALE2)
            ds = (e * dp_raw).astype(BF16)
            dvs_ref[at : at + n, hs] = nn(e.astype(BF16), ga).astype(BF16)
            dks_ref[at : at + n, hs] = (nn(ds, q) * SCALE).astype(BF16)
            at += n

    ahead = products(0)
    for h in range(HEADS):
        parts = ahead
        if h + 1 < HEADS:
            ahead = products(h + 1)
        gradients(h, parts)
    total = dks_ref.shape[0]
    spread = jnp.concatenate(
        [member(tokens, tokens >> l, l, 0, 0.5**l) for l in range(1, levels)], axis=1
    )
    for c in range(0, width, 256):
        cs = slice(c, c + 256)
        gk_ref[:, cs] = (dk0_ref[:, cs].astype(F32) + nn(spread, dks_ref[:, cs])).astype(BF16)
        gv_ref[:, cs] = (dv0_ref[:, cs].astype(F32) + nn(spread, dvs_ref[:, cs])).astype(BF16)


def after(x, *others):
    return lax.optimization_barrier((x, *others))[0]


def swap(x, axis, mask):
    count = lax.axis_size(axis)
    return lax.ppermute(x, axis, [(i, i ^ mask) for i in range(count)])


def body(queries, keys, values, grad_out, w_out):
    seq = lax.axis_size("seq")
    dp = lax.axis_size("dp")
    nz = seq // 2
    levels = seq.bit_length()
    upper = levels - 1
    q, k, v, g = queries[0], keys[0], values[0], grad_out[0]
    tokens, width = q.shape
    factor = 1.0 / math.sqrt(dp * seq * tokens)

    own = call(
        functools.partial(pool_kernel, levels),
        [((2, tokens >> l, width), BF16) for l in range(1, levels)],
        "pool",
        1,
        k,
        v,
        scratch=[pltpu.VMEM((2, tokens, width), BF16), pltpu.SemaphoreType.DMA((2,))],
        space=pltpu.HBM,
    )

    def across(per_level):
        return [
            (m.bit_length(), swap(per_level[m.bit_length()], "seq", 2 * m)) for m in range(1, nz)
        ]

    def joined(first, received, *wait):
        got = [[swap(first, "seq", 1)]] + [[] for _ in range(upper - 1)]
        for at, x in received:
            x = after(x, *wait)
            got[at] += [x, swap(x, "seq", 1)]
        axis = first.ndim - 2
        return [x if x[0].shape[axis] >= 16 else [jnp.concatenate(x, axis=axis)] for x in got]

    received = across(own)

    early = call(
        functools.partial(early_kernel, levels),
        [((upper, tokens, width), BF16), ((width, tokens), BF16)]
        + [((tokens >> l, width), BF16) for l in range(1, levels)],
        "early",
        1,
        after(q, own[0]),
        g,
        w_out,
    )
    qhat, gat, qls = early[0], early[1], early[2:]

    g_late = g
    grads = [g] + [swap(g_late, "dp", m) for m in range(1, min(dp, 3))]
    if dp == 4:
        half = tokens // 2
        grads += [swap(grads[1][:half], "dp", 2), swap(grads[2][half:], "dp", 1)]
    else:
        grads += [swap(g_late, "dp", m) for m in range(3, dp)]

    arrived = [x for _, x in received]
    pairs = joined(after(own[0], *arrived, gat), received, *arrived, gat)
    pieces = [len(x) for x in pairs]
    flat = [x for part in pairs for x in part]

    total_keys = tokens + upper * BLOCK
    outs = [
        ((HEADS, total_keys, tokens), BF16),
        ((width, tokens), BF16),
        ((HEADS, tokens), F32),
        ((width, tokens), BF16),
    ]
    outs += [((width // dp, tokens), BF16)] * dp
    outs += [((tokens >> l, 2 * width + LANES), BF16) for l in range(1, levels)]
    forward = call(
        functools.partial(forward_kernel, levels, pieces, dp),
        outs,
        "forward",
        1,
        q,
        k,
        v,
        qhat,
        gat,
        *qls,
        *flat,
        scratch=[pltpu.VMEM((upper, LANES, tokens), F32)],
    )
    e, grt, dd, att = forward[:4]
    blocks, outgoing = forward[4 : 4 + dp], forward[4 + dp :]

    atts = [blocks[0]] + [swap(blocks[m], "dp", m) for m in range(1, dp)]
    outgoing = list(lax.optimization_barrier((*outgoing, *grads[3:]))[:upper])
    relayed = nz == 4
    if relayed:
        far = swap(outgoing[2], "seq", 4)
        near = swap(outgoing[1], "seq", 2)
    else:
        received = across(outgoing)

    rows = width // dp
    own_rows = rows // (2 * nz)
    keep, even, odd = call(
        functools.partial(weight_kernel, dp, nz),
        [((nz, own_rows, width), F32)] + [((nz // 2, own_rows, width), BF16)] * 2,
        "weight",
        COST,
        *atts,
        *grads,
        scratch=[pltpu.VMEM((rows, width), F32)],
    )

    def halve(keep, got, offset=None, relay=()):
        n = keep.shape[0] // 2
        sent = (n, own_rows, width)
        if relay:
            sent = (own_rows, relay[0].shape[1] + n * width)
        outs = [((n, own_rows, width), F32), (sent, BF16)]
        kernel = functools.partial(halve_kernel, offset, len(got))
        return call(kernel, outs, "halve", 1, keep, *got, *relay)

    got = [swap(even, "seq", 1), swap(odd, "seq", 1)]
    if relayed:
        keep, send = halve(keep, got, None, (far,))
        both = swap(send, "seq", 2)
        grt = after(grt, keep, near)
    else:
        keep, send = halve(keep, got)
        grt = after(grt, keep)

    gq, dk0, dv0 = call(
        functools.partial(backward_kernel, levels, pieces),
        [((tokens, width), BF16)] * 3,
        "backward",
        COST,
        e,
        grt,
        dd,
        q,
        k,
        v,
        *flat,
        scratch=[pltpu.VMEM((width, levels * tokens), BF16)],
    )

    keep = after(keep, dk0)
    if relayed:
        keep, send = halve(keep, [both], far.shape[1])
        step = 4
        first = swap(after(outgoing[0], got[0]), "seq", 1)
        near, far, both = (after(x, dk0, send) for x in (near, far, both))
        messages = [
            [first],
            [near, swap(near, "seq", 1)],
            [far, swap(far, "seq", 1), both, swap(both, "seq", 1)],
        ]
    else:
        step = 2
        while keep.shape[0] > 1:
            got = swap(send, "seq", step)
            keep, send = halve(keep, [got[0::2], got[1::2]])
            step *= 2
        messages = joined(after(outgoing[0], dk0, send), received, dk0, send)
    message_pieces = [len(x) for x in messages]
    flat_messages = [x for part in messages for x in part]

    (mixed,) = call(
        mixed_kernel, [((tokens, width), BF16)], "mixed", 1, after(att, send), w_out
    )
    upper_rows = sum(tokens >> l for l in range(1, levels))
    gk, gv = call(
        functools.partial(owner_kernel, levels, message_pieces, tokens),
        [((tokens, width), BF16)] * 2,
        "owner",
        1,
        *own,
        *flat_messages,
        dk0,
        dv0,
        scratch=[pltpu.VMEM((upper_rows, width), BF16)] * 2,
    )

    (gw,) = call(
        functools.partial(final_kernel, factor),
        [((own_rows, width), F32)],
        "total",
        1,
        after(keep, gk),
        swap(send, "seq", step),
    )
    return (mixed[None], gq[None], gk[None], gv[None], gw)


def solution(mesh):
    rows = P("dp", "seq", None)
    return jax.shard_map(
        body,
        mesh=mesh,
        in_specs=(rows, rows, rows, rows, P()),
        out_specs=(rows, rows, rows, rows, P(("dp", "seq"), None)),
        check_vma=False,
    )
```

time: 82.4 us -> 58.4 us (0.71)
  Pallas kernels: 26.8 us -> 14.9 us
  waiting for transfers between devices: 17.9 us -> 11 us
  starting transfers between devices: 28.2 us -> 25.6 us
  other arithmetic: 2.13 us -> 0 us
    pallas_call x3 -> x0, Pallas kernels: 13.9 us -> none  [the longest x1 7.62 us: body(): pl.pallas_call(functools.partial(backward_kernel, levels, pieces), name='...]
    ppermute x25 -> x24, waiting for transfers between devices: 17.9 us -> 11 us  [swap(): return lax.ppermute(x, axis, [(i, i ^ mask) for i in range(count)])]
    ppermute x25 -> x24, starting transfers between devices: 28.2 us -> 25.6 us  [swap(): return lax.ppermute(x, axis, [(i, i ^ mask) for i in range(count)])]
    broadcast_in_dim x1 -> x0, other arithmetic: 2.09 us -> none  [body(): return (mixed[None], gq.astype(BF16)[None], gk[None], gv[None], gw)]
    pallas_call x5 -> x10, Pallas kernels: 13 us -> 14.9 us  [call(): pl.pallas_call(kernel, name=name, out_shape=[jax.ShapeDtypeStruct(s, t) f...]
    unnamed x24 -> x20, local copies, waits for them, and re-layouts: 6.12 us -> 5.77 us
  transfers between devices with their start and end apart: 25 -> 24, of which waited for: 5 -> 8; matrix products, arithmetic and copies ran while one was open for 3% -> 0% of each run, Pallas kernels for 32% -> 23%
where the time goes in v1:
time: 58.4 us; the launch traced here: 58.1 us
  starting transfers between devices  25.6 us (44%)
  Pallas kernels  14.9 us (26%)
  waiting for transfers between devices  11 us (19%)
  local copies, waits for them, and re-layouts  5.81 us (10%)
  between operations  0.8 us (1%)
    ppermute x24, starting transfers between devices, swap(): return lax.ppermute(x, axis, [(i, i ^ mask) for i in range(count)])  25.6 us
    pallas_call x10, Pallas kernels, call(): pl.pallas_call(kernel, name=name, out_shape=[jax.ShapeDtypeStruct(s, t) f...  14.9 us
    ppermute x24, waiting for transfers between devices, swap(): return lax.ppermute(x, axis, [(i, i ^ mask) for i in range(count)])  11 us
    unnamed x20, local copies, waits for them, and re-layouts  5.77 us
  transfers between devices with their start and end apart: 24, of which 8 were waited for; matrix products, arithmetic and copies ran while one was open for 0% of the time, Pallas kernels for 23%

profile of v1, /device:TPU:0, one launch (start us, length us, event | category | flops | bytes accessed | tf_op | source)
XLA Modules:
  0.0 58.1 jit_solution(9040339380026718944)
XLA Ops:
  0.6 0.0 copy-start.2
  0.6 1.0 %copy-done.2 = bf16[1,256,1024]{2,1,0:T(8,128)(2,1)S(1)} copy-done((bf16[1,256,1024]{2,1,0:T(8,128)(2,1)S(1)}, bf16[1,256,1024]{2,1,0:T(8,128)(2,1)}, u32[]{:S(2)}) %copy-start.2) | copy-done | bytes 524312
  1.7 1.0 %copy-done.4 = bf16[1,256,1024]{2,1,0:T(8,128)(2,1)S(1)} copy-done((bf16[1,256,1024]{2,1,0:T(8,128)(2,1)S(1)}, bf16[1,256,1024]{2,1,0:T(8,128)(2,1)}, u32[]{:S(2)}) %copy-start.4) | copy-done | bytes 524312
  2.7 0.9 %pool.1 = (bf16[2,128,1024]{2,1,0:T(8,128)(2,1)S(1)}, bf16[2,64,1024]{2,1,0:T(8,128)(2,1)S(1)}, bf16[2,32,1024]{2,1,0:T(8,128)(2,1)S(1)}) custom-call(bf16[256,1024]{1,0:T(8,128)(2,1)S(1)} %bitcast.8, bf16[256,1024]{1,0:T(8,128)(2,1)S(1)} %bitcast.11), custom_call_target="tpu_custom_call" | custom-call | flops 1 | bytes 1 | tf_op jit(solution)/shard_map/pool/pallas_call | solution.py:46
  3.6 3.1 %collective-permute-start = (bf16[2,64,1024]{2,1,0:T(8,128)(2,1)S(1)}, bf16[2,64,1024]{2,1,0:T(8,128)(2,1)S(1)}, u32[]{:S(2)}, u32[]{:S(2)}) collective-permute-start(bf16[2,64,1024]{2,1,0:T(8,128)(2,1)S(1)} %get-tuple-element.59.refs_1_), channel_id=1, source_target_pairs={{0,2},{1,3},{2,0},{3,1},{4,6},{5,7},{6,4},{7,5},{8,10},{9,11},{10,... | collective-permute-start | bytes 786440 | tf_op jit(solution)/shard_map/ppermute | solution.py:320
  6.7 1.5 %collective-permute-start.10 = (bf16[256,1024]{1,0:T(8,128)(2,1)}, bf16[256,1024]{1,0:T(8,128)(2,1)S(1)}, u32[]{:S(2)}, u32[]{:S(2)}) collective-permute-start(bf16[256,1024]{1,0:T(8,128)(2,1)} %bitcast.17), channel_id=1, source_target_pairs={{0,8},{8,0},{16,24},{24,16},{1,9},{9,1},{17,25},{25,17},{2,10},{10... | collective-permute-start | bytes 1572872 | tf_op jit(solution)/shard_map/ppermute | solution.py:320
  8.2 2.6 %collective-permute-start.1 = (bf16[2,32,1024]{2,1,0:T(8,128)(2,1)S(1)}, bf16[2,32,1024]{2,1,0:T(8,128)(2,1)S(1)}, u32[]{:S(2)}, u32[]{:S(2)}) collective-permute-start(bf16[2,32,1024]{2,1,0:T(8,128)(2,1)S(1)} %get-tuple-element.60.refs_2_), channel_id=1, source_target_pairs={{0,4},{1,5},{2,6},{3,7},{4,0},{5,1},{6,2},{7,3},{8,12},{9,13},{10,... | collective-permute-start | bytes 393224 | tf_op jit(solution)/shard_map/ppermute | solution.py:320
  10.8 0.2 collective-permute-start.2
  11.0 1.5 %collective-permute-start.11 = (bf16[256,1024]{1,0:T(8,128)(2,1)}, bf16[256,1024]{1,0:T(8,128)(2,1)S(1)}, u32[]{:S(2)}, u32[]{:S(2)}) collective-permute-start(bf16[256,1024]{1,0:T(8,128)(2,1)} %bitcast.18), channel_id=1, source_target_pairs={{0,16},{8,24},{16,0},{24,8},{1,17},{9,25},{17,1},{25,9},{2,18},{10... | collective-permute-start | bytes 1572872 | tf_op jit(solution)/shard_map/ppermute | solution.py:320
  12.5 1.6 %copy-done = bf16[1024,1024]{1,0:T(8,128)(2,1)S(1)} copy-done((bf16[1024,1024]{1,0:T(8,128)(2,1)S(1)}, bf16[1024,1024]{1,0:T(8,128)(2,1)}, u32[]{:S(2)}) %copy-start) | copy-done | bytes 2097176
  14.1 1.0 %copy-done.6 = bf16[1,256,1024]{2,1,0:T(8,128)(2,1)S(1)} copy-done((bf16[1,256,1024]{2,1,0:T(8,128)(2,1)S(1)}, bf16[1,256,1024]{2,1,0:T(8,128)(2,1)}, u32[]{:S(2)}) %copy-start.6) | copy-done | bytes 524312
  15.1 1.0 %copy-done.8 = bf16[1,256,1024]{2,1,0:T(8,128)(2,1)S(1)} copy-done((bf16[1,256,1024]{2,1,0:T(8,128)(2,1)S(1)}, bf16[1,256,1024]{2,1,0:T(8,128)(2,1)}, u32[]{:S(2)}) %copy-start.8) | copy-done | bytes 524312
  16.2 1.4 %early.1 = (bf16[3,256,1024]{2,1,0:T(8,128)(2,1)S(1)}, bf16[1024,256]{1,0:T(8,128)(2,1)S(1)}, bf16[128,1024]{1,0:T(8,128)(2,1)S(1)}, bf16[64,1024]{1,0:T(8,128)(2,1)S(1)}, bf16[32,1024]{1,0:T(8,128)(2,1)S(1)}) custom-call(bf16[256,1024]{1,0:T(8,128)(2,1)S(1)} %bitcast.14, bf16[256,1024]{1,0:T(8,128)(2,1)S(1)} %bitcast.19, bf16[1024,1024]{1,0:T(8,128)(2,1)S(1)} %copy-done), custom_call_target="tpu_custom_call" | custom-call | flops 1 | bytes 1 | tf_op jit(solution)/shard_map/early/pallas_call | solution.py:46
  17.6 0.0 collective-permute-done.1.refs_6_.refs_3_
  17.6 3.3 %collective-permute-done.2.refs_8_.refs_5_ = bf16[2,32,1024]{2,1,0:T(8,128)(2,1)S(1)} collective-permute-done((bf16[2,32,1024]{2,1,0:T(8,128)(2,1)S(1)}, bf16[2,32,1024]{2,1,0:T(8,128)(2,1)S(1)}, u32[]{:S(2)}, u32[]{:S(2)}) %collective-permute-start.2) | collective-permute-done | bytes 131104 | tf_op jit(solution)/shard_map/ppermute | solution.py:320
  20.9 0.0 collective-permute-done.refs_4_.refs_1_
  20.9 0.0 collective-permute-start.3
  20.9 0.5 collective-permute-start.6
  21.4 0.0 collective-permute-start.4
  21.4 0.0 collective-permute-done.10.refs_5_
  21.4 0.5 collective-permute-start.5
  22.0 1.8 %collective-permute-done.11.refs_6_ = bf16[256,1024]{1,0:T(8,128)(2,1)S(1)} collective-permute-done((bf16[256,1024]{1,0:T(8,128)(2,1)}, bf16[256,1024]{1,0:T(8,128)(2,1)S(1)}, u32[]{:S(2)}, u32[]{:S(2)}) %collective-permute-start.11) | collective-permute-done | bytes 524320 | tf_op jit(solution)/shard_map/ppermute | solution.py:320
  23.8 1.5 %collective-permute-start.12 = (bf16[128,1024]{1,0:T(8,128)(2,1)S(1)}, bf16[128,1024]{1,0:T(8,128)(2,1)S(1)}, u32[]{:S(2)}, u32[]{:S(2)}) collective-permute-start(bf16[128,1024]{1,0:T(8,128)(2,1)S(1)} %slice.8), channel_id=1, source_target_pairs={{0,16},{8,24},{16,0},{24,8},{1,17},{9,25},{17,1},{25,9},{2,18},{10... | collective-permute-start | bytes 786440 | tf_op jit(solution)/shard_map/ppermute | solution.py:320
  25.4 0.0 collective-permute-done.6.refs_9_.refs_6_
  25.4 0.6 %collective-permute-start.13 = (bf16[128,1024]{1,0:T(8,128)(2,1)S(1)}, bf16[128,1024]{1,0:T(8,128)(2,1)S(1)}, u32[]{:S(2)}, u32[]{:S(2)}) collective-permute-start(bf16[128,1024]{1,0:T(8,128)(2,1)S(1)} %slice.9), channel_id=1, source_target_pairs={{0,8},{8,0},{16,24},{24,16},{1,9},{9,1},{17,25},{25,17},{2,10},{10... | collective-permute-start | bytes 786440 | tf_op jit(solution)/shard_map/ppermute | solution.py:320
  26.0 0.0 collective-permute-done.5.refs_7_.refs_4_
  26.0 0.0 collective-permute-done.4.refs_5_.refs_2_
  26.0 0.0 collective-permute-done.3.refs_3_.refs_0_
  26.0 0.0 copy-start.9
  26.0 3.1 %forward.1 = (bf16[8,640,256]{2,1,0:T(8,128)(2,1)S(1)}, bf16[1024,256]{1,0:T(8,128)(2,1)S(1)}, f32[8,256]{1,0:T(8,128)S(1)}, bf16[1024,256]{1,0:T(8,128)(2,1)S(1...) custom-call(bf16[256,1024]{1,0:T(8,128)(2,1)S(1)} %bitcast.15, ...), custom_call_target="tpu_custom_call" | custom-call | flops 1 | bytes 1 | tf_op jit(solution)/shard_map/forward/pallas_call | solution.py:46
  29.1 1.6 %collective-permute-start.7 = (bf16[256,256]{1,0:T(8,128)(2,1)S(1)}, bf16[256,256]{1,0:T(8,128)(2,1)S(1)}, u32[]{:S(2)}, u32[]{:S(2)}) collective-permute-start(bf16[256,256]{1,0:T(8,128)(2,1)S(1)} %get-tuple-element.67), channel_id=1, source_target_pairs={{0,8},{8,0},{16,24},{24,16},{1,9},{9,1},{17,25},{25,17},{2,10},{10... | collective-permute-start | bytes 393224 | tf_op jit(solution)/shard_map/ppermute | solution.py:320
  30.7 0.5 collective-permute-start.8
  31.2 1.5 %collective-permute-start.9 = (bf16[256,256]{1,0:T(8,128)(2,1)S(1)}, bf16[256,256]{1,0:T(8,128)(2,1)S(1)}, u32[]{:S(2)}, u32[]{:S(2)}) collective-permute-start(bf16[256,256]{1,0:T(8,128)(2,1)S(1)} %get-tuple-element.69), channel_id=1, source_target_pairs={{0,24},{8,16},{16,8},{24,0},{1,25},{9,17},{17,9},{25,1},{2,26},{10... | collective-permute-start | bytes 393224 | tf_op jit(solution)/shard_map/ppermute | solution.py:320
  32.7 0.0 collective-permute-done.12.refs_7_
  32.7 0.5 collective-permute-done.13.refs_8_
  33.2 3.1 %collective-permute-start.16 = (bf16[32,2176]{1,0:T(8,128)(2,1)S(1)}, bf16[32,2176]{1,0:T(8,128)(2,1)S(1)}, u32[]{:S(2)}, u32[]{:S(2)}) collective-permute-start(bf16[32,2176]{1,0:T(8,128)(2,1)S(1)} %get-tuple-element.76), channel_id=1, source_target_pairs={{0,4},{1,5},{2,6},{3,7},{4,0},{5,1},{6,2},{7,3},{8,12},{9,13},{10,... | collective-permute-start | bytes 417800 | tf_op jit(solution)/shard_map/ppermute | solution.py:320
  36.3 2.4 %collective-permute-start.17 = (bf16[64,2176]{1,0:T(8,128)(2,1)S(1)}, bf16[64,2176]{1,0:T(8,128)(2,1)S(1)}, u32[]{:S(2)}, u32[]{:S(2)}) collective-permute-start(bf16[64,2176]{1,0:T(8,128)(2,1)S(1)} %get-tuple-element.80), channel_id=1, source_target_pairs={{0,2},{1,3},{2,0},{3,1},{4,6},{5,7},{6,4},{7,5},{8,10},{9,11},{10,... | collective-permute-start | bytes 835592 | tf_op jit(solution)/shard_map/ppermute | solution.py:320
  38.7 0.0 collective-permute-done.7.refs_1_
  38.7 0.0 collective-permute-done.8.refs_2_
  38.7 0.0 collective-permute-done.9.refs_3_
  38.7 0.0 copy-start.7
  38.7 0.8 %weight.1 = (f32[4,32,1024]{2,1,0:T(8,128)S(1)}, bf16[2,32,1024]{2,1,0:T(8,128)(2,1)S(1)}, bf16[2,32,1024]{2,1,0:T(8,128)(2,1)S(1)}) custom-call(bf16[256,256]{1,0:T(8,128)(2,1)S(1)} %get-tuple-element.66.refs_0_, bf16[256,256]{1,0:T(8,128)(2,1)S(1)} %collective-permute-done.7.refs_1_, bf16[256,256]{1,0:T(8,128)(2,1)S(1)} %collective-permute-done.8.refs_2_, ...), custom_call_target="tpu_custom_call" | custom-call | flops 5000000000 | bytes 1 | tf_op jit(solution)/shard_map/weight/pallas_call | solution.py:46
  39.5 0.1 collective-permute-start.14
  39.6 0.5 collective-permute-start.15
  40.1 0.8 %collective-permute-done.14.refs_0_ = bf16[2,32,1024]{2,1,0:T(8,128)(2,1)S(1)} collective-permute-done((bf16[2,32,1024]{2,1,0:T(8,128)(2,1)S(1)}, bf16[2,32,1024]{2,1,0:T(8,128)(2,1)S(1)}, u32[]{:S(2)}, u32[]{:S(2)}) %collective-permute-start.14) | collective-permute-done | bytes 131104 | tf_op jit(solution)/shard_map/ppermute | solution.py:320
  40.9 0.2 collective-permute-done.15.refs_1_
  41.1 0.1 halve.2
  41.2 1.1 %collective-permute-start.18 = (bf16[32,4224]{1,0:T(8,128)(2,1)S(1)}, bf16[32,4224]{1,0:T(8,128)(2,1)S(1)}, u32[]{:S(2)}, u32[]{:S(2)}) collective-permute-start(bf16[32,4224]{1,0:T(8,128)(2,1)S(1)} %get-tuple-element.85), channel_id=1, source_target_pairs={{0,2},{1,3},{2,0},{3,1},{4,6},{5,7},{6,4},{7,5},{8,10},{9,11},{10,... | collective-permute-start | bytes 811016 | tf_op jit(solution)/shard_map/ppermute | solution.py:320
  42.3 0.0 collective-permute-start.19
  42.4 0.9 %collective-permute-done.17.refs_4_ = bf16[64,2176]{1,0:T(8,128)(2,1)S(1)} collective-permute-done((bf16[64,2176]{1,0:T(8,128)(2,1)S(1)}, bf16[64,2176]{1,0:T(8,128)(2,1)S(1)}, u32[]{:S(2)}, u32[]{:S(2)}) %collective-permute-start.17) | collective-permute-done | bytes 278560 | tf_op jit(solution)/shard_map/ppermute | solution.py:320
  43.2 3.4 %backward.1 = (bf16[256,1024]{1,0:T(8,128)(2,1)}, bf16[256,1024]{1,0:T(8,128)(2,1)S(1)}, bf16[256,1024]{1,0:T(8,128)(2,1)S(1)}) custom-call(bf16[8,640,256]{2,1,0:T(8,128)(2,1)S(1)} %get-tuple-element.78.e_ref, bf16[1024,256]{1,0:T(8,128)(2,1)S(1)} %get-tuple-element.81.grt_ref, f32[8,256]{1,0:T(8,128)S(1)} %get-tuple-element.82.dd_ref, ...), custom_call_target="tpu_custom_call" | custom-call | flops 5000000000 | bytes 1 | tf_op jit(solution)/shard_map/backward/pallas_call | solution.py:46
  46.6 3.3 %collective-permute-done.18.refs_0_.refs_8_ = bf16[32,4224]{1,0:T(8,128)(2,1)S(1)} collective-permute-done((bf16[32,4224]{1,0:T(8,128)(2,1)S(1)}, bf16[32,4224]{1,0:T(8,128)(2,1)S(1)}, u32[]{:S(2)}, u32[]{:S(2)}) %collective-permute-start.18) | collective-permute-done | bytes 270368 | tf_op jit(solution)/shard_map/ppermute | solution.py:320
  50.0 0.1 collective-permute-start.20
  50.1 0.5 collective-permute-start.22
  50.6 0.1 collective-permute-start.21
  50.6 2.1 %collective-permute-start.23 = (bf16[1,32,1024]{2,1,0:T(8,128)(2,1)S(1)}, bf16[1,32,1024]{2,1,0:T(8,128)(2,1)S(1)}, u32[]{:S(2)}, u32[]{:S(2)}) collective-permute-start(bf16[1,32,1024]{2,1,0:T(8,128)(2,1)S(1)} %get-tuple-element.86), channel_id=1, source_target_pairs={{0,4},{1,5},{2,6},{3,7},{4,0},{5,1},{6,2},{7,3},{8,12},{9,13},{10,... | collective-permute-start | bytes 196616 | tf_op jit(solution)/shard_map/ppermute | solution.py:320
  52.7 1.5 %mixed.1 = bf16[256,1024]{1,0:T(8,128)(2,1)} custom-call(bf16[1024,256]{1,0:T(8,128)(2,1)S(1)} %get-tuple-element.87.att_ref, bf16[1024,1024]{1,0:T(8,128)(2,1)S(1)} %copy-done.1), custom_call_target="tpu_custom_call" | custom-call | flops 1 | bytes 1 | tf_op jit(solution)/shard_map/mixed/pallas_call | solution.py:46
  54.3 0.0 collective-permute-done.21.refs_7_
  54.3 0.0 collective-permute-done.22.refs_9_
  54.3 0.0 collective-permute-done.20.refs_5_
  54.3 0.0 collective-permute-done.19.refs_3_
  54.3 3.0 %owner.1 = (bf16[256,1024]{1,0:T(8,128)(2,1)}, bf16[256,1024]{1,0:T(8,128)(2,1)}) custom-call(bf16[2,128,1024]{2,1,0:T(8,128)(2,1)S(1)} %get-tuple-element.61.refs_0_, bf16[2,64,1024]{2,1,0:T(8,128)(2,1)S(1)} %get-tuple-element.59.refs_1_, bf16[2,32,1024]{2,1,0:T(8,128)(2,1)S(1)} %get-tuple-element.60.refs_2_, ...), custom_call_target="tpu_custom_call" | custom-call | flops 1 | bytes 1 | tf_op jit(solution)/shard_map/owner/pallas_call | solution.py:46
  57.3 0.1 collective-permute-done.23.got_ref
  57.4 0.7 %total.1 = f32[32,1024]{1,0:T(8,128)} custom-call(f32[1,32,1024]{2,1,0:T(8,128)S(1)} %get-tuple-element.98.keep_ref, bf16[1,32,1024]{2,1,0:T(8,128)(2,1)S(1)} %collective-permute-done.23.got_ref), custom_call_target="tpu_custom_call" | custom-call | flops 1 | bytes 1 | tf_op jit(solution)/shard_map/total/pallas_call | solution.py:46
  (16 shorter events, 0.1 us)
Async XLA Ops:
  0.6 1.0 %copy-start.2 = (bf16[1,256,1024]{2,1,0:T(8,128)(2,1)S(1)}, bf16[1,256,1024]{2,1,0:T(8,128)(2,1)}, u32[]{:S(2)}) copy-start(bf16[1,256,1024]{2,1,0:T(8,128)(2,1)} %param.6) | copy-start | bytes 1572868
  1.7 1.0 %copy-start.4 = (bf16[1,256,1024]{2,1,0:T(8,128)(2,1)S(1)}, bf16[1,256,1024]{2,1,0:T(8,128)(2,1)}, u32[]{:S(2)}) copy-start(bf16[1,256,1024]{2,1,0:T(8,128)(2,1)} %param.7) | copy-start | bytes 1572868
  3.6 17.3 %collective-permute-start = (bf16[2,64,1024]{2,1,0:T(8,128)(2,1)S(1)}, bf16[2,64,1024]{2,1,0:T(8,128)(2,1)S(1)}, u32[]{:S(2)}, u32[]{:S(2)}) collective-permute-start(bf16[2,64,1024]{2,1,0:T(8,128)(2,1)S(1)} %get-tuple-element.59.refs_1_), channel_id=1, source_target_pairs={{0,2},{1,3},{2,0},{3,1},{4,6},{5,7},{6,4},{7,5},{8,10},{9,11},{10,... | collective-permute-start | bytes 786440 | tf_op jit(solution)/shard_map/ppermute | solution.py:320
  6.7 14.7 %collective-permute-start.10 = (bf16[256,1024]{1,0:T(8,128)(2,1)}, bf16[256,1024]{1,0:T(8,128)(2,1)S(1)}, u32[]{:S(2)}, u32[]{:S(2)}) collective-permute-start(bf16[256,1024]{1,0:T(8,128)(2,1)} %bitcast.17), channel_id=1, source_target_pairs={{0,8},{8,0},{16,24},{24,16},{1,9},{9,1},{17,25},{25,17},{2,10},{10... | collective-permute-start | bytes 1572872 | tf_op jit(solution)/shard_map/ppermute | solution.py:320
  8.2 9.5 %collective-permute-start.1 = (bf16[2,32,1024]{2,1,0:T(8,128)(2,1)S(1)}, bf16[2,32,1024]{2,1,0:T(8,128)(2,1)S(1)}, u32[]{:S(2)}, u32[]{:S(2)}) collective-permute-start(bf16[2,32,1024]{2,1,0:T(8,128)(2,1)S(1)} %get-tuple-element.60.refs_2_), channel_id=1, source_target_pairs={{0,4},{1,5},{2,6},{3,7},{4,0},{5,1},{6,2},{7,3},{8,12},{9,13},{10,... | collective-permute-start | bytes 393224 | tf_op jit(solution)/shard_map/ppermute | solution.py:320
  10.8 10.1 %collective-permute-start.2 = (bf16[2,32,1024]{2,1,0:T(8,128)(2,1)S(1)}, bf16[2,32,1024]{2,1,0:T(8,128)(2,1)S(1)}, u32[]{:S(2)}, u32[]{:S(2)}) collective-permute-start(bf16[2,32,1024]{2,1,0:T(8,128)(2,1)S(1)} %get-tuple-element.60.refs_2_), channel_id=1, source_target_pairs={{0,6},{1,7},{2,4},{3,5},{4,2},{5,3},{6,0},{7,1},{8,14},{9,15},{10,... | collective-permute-start | bytes 393224 | tf_op jit(solution)/shard_map/ppermute | solution.py:320
  11.0 12.8 %collective-permute-start.11 = (bf16[256,1024]{1,0:T(8,128)(2,1)}, bf16[256,1024]{1,0:T(8,128)(2,1)S(1)}, u32[]{:S(2)}, u32[]{:S(2)}) collective-permute-start(bf16[256,1024]{1,0:T(8,128)(2,1)} %bitcast.18), channel_id=1, source_target_pairs={{0,16},{8,24},{16,0},{24,8},{1,17},{9,25},{17,1},{25,9},{2,18},{10... | collective-permute-start | bytes 1572872 | tf_op jit(solution)/shard_map/ppermute | solution.py:320
  12.5 1.6 %copy-start = (bf16[1024,1024]{1,0:T(8,128)(2,1)S(1)}, bf16[1024,1024]{1,0:T(8,128)(2,1)}, u32[]{:S(2)}) copy-start(bf16[1024,1024]{1,0:T(8,128)(2,1)} %w_ref.3) | copy-start | bytes 6291460
  14.1 1.0 %copy-start.6 = (bf16[1,256,1024]{2,1,0:T(8,128)(2,1)S(1)}, bf16[1,256,1024]{2,1,0:T(8,128)(2,1)}, u32[]{:S(2)}) copy-start(bf16[1,256,1024]{2,1,0:T(8,128)(2,1)} %param.5) | copy-start | bytes 1572868
  15.1 1.0 %copy-start.8 = (bf16[1,256,1024]{2,1,0:T(8,128)(2,1)S(1)}, bf16[1,256,1024]{2,1,0:T(8,128)(2,1)}, u32[]{:S(2)}) copy-start(bf16[1,256,1024]{2,1,0:T(8,128)(2,1)} %param.8) | copy-start | bytes 1572868
  16.2 9.8 %copy-start.3 = (bf16[1,256,1024]{2,1,0:T(8,128)(2,1)S(1)}, bf16[1,256,1024]{2,1,0:T(8,128)(2,1)}, u32[]{:S(2)}) copy-start(bf16[1,256,1024]{2,1,0:T(8,128)(2,1)} %param.6) | copy-start | bytes 1572868
  16.2 9.8 %copy-start.5 = (bf16[1,256,1024]{2,1,0:T(8,128)(2,1)S(1)}, bf16[1,256,1024]{2,1,0:T(8,128)(2,1)}, u32[]{:S(2)}) copy-start(bf16[1,256,1024]{2,1,0:T(8,128)(2,1)} %param.7) | copy-start | bytes 1572868
  20.9 5.1 %collective-permute-start.3 = (bf16[2,128,1024]{2,1,0:T(8,128)(2,1)S(1)}, bf16[2,128,1024]{2,1,0:T(8,128)(2,1)S(1)}, u32[]{:S(2)}, u32[]{:S(2)}) collective-permute-start(bf16[2,128,1024]{2,1,0:T(8,128)(2,1)S(1)} %get-tuple-element.61.refs_0_), channel_id=1, source_target_pairs={{0,1},{1,0},{2,3},{3,2},{4,5},{5,4},{6,7},{7,6},{8,9},{9,8},{10,11... | collective-permute-start | bytes 1572872 | tf_op jit(solution)/shard_map/ppermute | solution.py:320
  20.9 4.4 %collective-permute-start.6 = (bf16[2,32,1024]{2,1,0:T(8,128)(2,1)S(1)}, bf16[2,32,1024]{2,1,0:T(8,128)(2,1)S(1)}, u32[]{:S(2)}, u32[]{:S(2)}) collective-permute-start(bf16[2,32,1024]{2,1,0:T(8,128)(2,1)S(1)} %collective-permute-done.2.refs_8_.refs_5_), channel_id=1, source_target_pairs={{0,1},{1,0},{2,3},{3,2},{4,5},{5,4},{6,7},{7,6},{8,9},{9,8},{10,11... | collective-permute-start | bytes 393224 | tf_op jit(solution)/shard_map/ppermute | solution.py:320
  21.4 4.5 %collective-permute-start.4 = (bf16[2,64,1024]{2,1,0:T(8,128)(2,1)S(1)}, bf16[2,64,1024]{2,1,0:T(8,128)(2,1)S(1)}, u32[]{:S(2)}, u32[]{:S(2)}) collective-permute-start(bf16[2,64,1024]{2,1,0:T(8,128)(2,1)S(1)} %collective-permute-done.refs_4_.refs_1_), channel_id=1, source_target_pairs={{0,1},{1,0},{2,3},{3,2},{4,5},{5,4},{6,7},{7,6},{8,9},{9,8},{10,11... | collective-permute-start | bytes 786440 | tf_op jit(solution)/shard_map/ppermute | solution.py:320
  21.4 4.5 %collective-permute-start.5 = (bf16[2,32,1024]{2,1,0:T(8,128)(2,1)S(1)}, bf16[2,32,1024]{2,1,0:T(8,128)(2,1)S(1)}, u32[]{:S(2)}, u32[]{:S(2)}) collective-permute-start(bf16[2,32,1024]{2,1,0:T(8,128)(2,1)S(1)} %collective-permute-done.1.refs_6_.refs_3_), channel_id=1, source_target_pairs={{0,1},{1,0},{2,3},{3,2},{4,5},{5,4},{6,7},{7,6},{8,9},{9,8},{10,11... | collective-permute-start | bytes 393224 | tf_op jit(solution)/shard_map/ppermute | solution.py:320
  23.8 8.8 %collective-permute-start.12 = (bf16[128,1024]{1,0:T(8,128)(2,1)S(1)}, bf16[128,1024]{1,0:T(8,128)(2,1)S(1)}, u32[]{:S(2)}, u32[]{:S(2)}) collective-permute-start(bf16[128,1024]{1,0:T(8,128)(2,1)S(1)} %slice.8), channel_id=1, source_target_pairs={{0,16},{8,24},{16,0},{24,8},{1,17},{9,25},{17,1},{25,9},{2,18},{10... | collective-permute-start | bytes 786440 | tf_op jit(solution)/shard_map/ppermute | solution.py:320
  25.4 7.8 %collective-permute-start.13 = (bf16[128,1024]{1,0:T(8,128)(2,1)S(1)}, bf16[128,1024]{1,0:T(8,128)(2,1)S(1)}, u32[]{:S(2)}, u32[]{:S(2)}) collective-permute-start(bf16[128,1024]{1,0:T(8,128)(2,1)S(1)} %slice.9), channel_id=1, source_target_pairs={{0,8},{8,0},{16,24},{24,16},{1,9},{9,1},{17,25},{25,17},{2,10},{10... | collective-permute-start | bytes 786440 | tf_op jit(solution)/shard_map/ppermute | solution.py:320
  26.0 12.7 %copy-start.9 = (bf16[1,256,1024]{2,1,0:T(8,128)(2,1)S(1)}, bf16[1,256,1024]{2,1,0:T(8,128)(2,1)}, u32[]{:S(2)}) copy-start(bf16[1,256,1024]{2,1,0:T(8,128)(2,1)} %param.8) | copy-start | bytes 1572868
  29.1 9.6 %collective-permute-start.7 = (bf16[256,256]{1,0:T(8,128)(2,1)S(1)}, bf16[256,256]{1,0:T(8,128)(2,1)S(1)}, u32[]{:S(2)}, u32[]{:S(2)}) collective-permute-start(bf16[256,256]{1,0:T(8,128)(2,1)S(1)} %get-tuple-element.67), channel_id=1, source_target_pairs={{0,8},{8,0},{16,24},{24,16},{1,9},{9,1},{17,25},{25,17},{2,10},{10... | collective-permute-start | bytes 393224 | tf_op jit(solution)/shard_map/ppermute | solution.py:320
  30.7 8.1 %collective-permute-start.8 = (bf16[256,256]{1,0:T(8,128)(2,1)S(1)}, bf16[256,256]{1,0:T(8,128)(2,1)S(1)}, u32[]{:S(2)}, u32[]{:S(2)}) collective-permute-start(bf16[256,256]{1,0:T(8,128)(2,1)S(1)} %get-tuple-element.68), channel_id=1, source_target_pairs={{0,16},{8,24},{16,0},{24,8},{1,17},{9,25},{17,1},{25,9},{2,18},{10... | collective-permute-start | bytes 393224 | tf_op jit(solution)/shard_map/ppermute | solution.py:320
  31.2 7.6 %collective-permute-start.9 = (bf16[256,256]{1,0:T(8,128)(2,1)S(1)}, bf16[256,256]{1,0:T(8,128)(2,1)S(1)}, u32[]{:S(2)}, u32[]{:S(2)}) collective-permute-start(bf16[256,256]{1,0:T(8,128)(2,1)S(1)} %get-tuple-element.69), channel_id=1, source_target_pairs={{0,24},{8,16},{16,8},{24,0},{1,25},{9,17},{17,9},{25,1},{2,26},{10... | collective-permute-start | bytes 393224 | tf_op jit(solution)/shard_map/ppermute | solution.py:320
  33.2 6.9 %collective-permute-start.16 = (bf16[32,2176]{1,0:T(8,128)(2,1)S(1)}, bf16[32,2176]{1,0:T(8,128)(2,1)S(1)}, u32[]{:S(2)}, u32[]{:S(2)}) collective-permute-start(bf16[32,2176]{1,0:T(8,128)(2,1)S(1)} %get-tuple-element.76), channel_id=1, source_target_pairs={{0,4},{1,5},{2,6},{3,7},{4,0},{5,1},{6,2},{7,3},{8,12},{9,13},{10,... | collective-permute-start | bytes 417800 | tf_op jit(solution)/shard_map/ppermute | solution.py:320
  36.3 6.9 %collective-permute-start.17 = (bf16[64,2176]{1,0:T(8,128)(2,1)S(1)}, bf16[64,2176]{1,0:T(8,128)(2,1)S(1)}, u32[]{:S(2)}, u32[]{:S(2)}) collective-permute-start(bf16[64,2176]{1,0:T(8,128)(2,1)S(1)} %get-tuple-element.80), channel_id=1, source_target_pairs={{0,2},{1,3},{2,0},{3,1},{4,6},{5,7},{6,4},{7,5},{8,10},{9,11},{10,... | collective-permute-start | bytes 835592 | tf_op jit(solution)/shard_map/ppermute | solution.py:320
  38.7 4.5 %copy-start.7 = (bf16[1,256,1024]{2,1,0:T(8,128)(2,1)S(1)}, bf16[1,256,1024]{2,1,0:T(8,128)(2,1)}, u32[]{:S(2)}) copy-start(bf16[1,256,1024]{2,1,0:T(8,128)(2,1)} %param.5) | copy-start | bytes 1572868
  39.5 1.4 %collective-permute-start.14 = (bf16[2,32,1024]{2,1,0:T(8,128)(2,1)S(1)}, bf16[2,32,1024]{2,1,0:T(8,128)(2,1)S(1)}, u32[]{:S(2)}, u32[]{:S(2)}) collective-permute-start(bf16[2,32,1024]{2,1,0:T(8,128)(2,1)S(1)} %get-tuple-element.71), channel_id=1, source_target_pairs={{0,1},{1,0},{2,3},{3,2},{4,5},{5,4},{6,7},{7,6},{8,9},{9,8},{10,11... | collective-permute-start | bytes 393224 | tf_op jit(solution)/shard_map/ppermute | solution.py:320
  39.6 1.5 %collective-permute-start.15 = (bf16[2,32,1024]{2,1,0:T(8,128)(2,1)S(1)}, bf16[2,32,1024]{2,1,0:T(8,128)(2,1)S(1)}, u32[]{:S(2)}, u32[]{:S(2)}) collective-permute-start(bf16[2,32,1024]{2,1,0:T(8,128)(2,1)S(1)} %get-tuple-element.72), channel_id=1, source_target_pairs={{0,1},{1,0},{2,3},{3,2},{4,5},{5,4},{6,7},{7,6},{8,9},{9,8},{10,11... | collective-permute-start | bytes 393224 | tf_op jit(solution)/shard_map/ppermute | solution.py:320
  41.2 8.8 %collective-permute-start.18 = (bf16[32,4224]{1,0:T(8,128)(2,1)S(1)}, bf16[32,4224]{1,0:T(8,128)(2,1)S(1)}, u32[]{:S(2)}, u32[]{:S(2)}) collective-permute-start(bf16[32,4224]{1,0:T(8,128)(2,1)S(1)} %get-tuple-element.85), channel_id=1, source_target_pairs={{0,2},{1,3},{2,0},{3,1},{4,6},{5,7},{6,4},{7,5},{8,10},{9,11},{10,... | collective-permute-start | bytes 811016 | tf_op jit(solution)/shard_map/ppermute | solution.py:320
  42.3 12.0 %collective-permute-start.19 = (bf16[128,2176]{1,0:T(8,128)(2,1)S(1)}, bf16[128,2176]{1,0:T(8,128)(2,1)S(1)}, u32[]{:S(2)}, u32[]{:S(2)}) collective-permute-start(bf16[128,2176]{1,0:T(8,128)(2,1)S(1)} %get-tuple-element.90), channel_id=1, source_target_pairs={{0,1},{1,0},{2,3},{3,2},{4,5},{5,4},{6,7},{7,6},{8,9},{9,8},{10,11... | collective-permute-start | bytes 1671176 | tf_op jit(solution)/shard_map/ppermute | solution.py:320
  43.2 9.5 %copy-start.1 = (bf16[1024,1024]{1,0:T(8,128)(2,1)S(1)}, bf16[1024,1024]{1,0:T(8,128)(2,1)}, u32[]{:S(2)}) copy-start(bf16[1024,1024]{1,0:T(8,128)(2,1)} %w_ref.3) | copy-start | bytes 6291460
  50.0 4.3 %collective-permute-start.20 = (bf16[64,2176]{1,0:T(8,128)(2,1)S(1)}, bf16[64,2176]{1,0:T(8,128)(2,1)S(1)}, u32[]{:S(2)}, u32[]{:S(2)}) collective-permute-start(bf16[64,2176]{1,0:T(8,128)(2,1)S(1)} %collective-permute-done.17.refs_4_), channel_id=1, source_target_pairs={{0,1},{1,0},{2,3},{3,2},{4,5},{5,4},{6,7},{7,6},{8,9},{9,8},{10,11... | collective-permute-start | bytes 835592 | tf_op jit(solution)/shard_map/ppermute | solution.py:320
  50.1 4.2 %collective-permute-start.22 = (bf16[32,4224]{1,0:T(8,128)(2,1)S(1)}, bf16[32,4224]{1,0:T(8,128)(2,1)S(1)}, u32[]{:S(2)}, u32[]{:S(2)}) collective-permute-start(bf16[32,4224]{1,0:T(8,128)(2,1)S(1)} %collective-permute-done.18.refs_0_.refs_8_), channel_id=1, source_target_pairs={{0,1},{1,0},{2,3},{3,2},{4,5},{5,4},{6,7},{7,6},{8,9},{9,8},{10,11... | collective-permute-start | bytes 811016 | tf_op jit(solution)/shard_map/ppermute | solution.py:320
  50.6 3.7 %collective-permute-start.21 = (bf16[32,2176]{1,0:T(8,128)(2,1)S(1)}, bf16[32,2176]{1,0:T(8,128)(2,1)S(1)}, u32[]{:S(2)}, u32[]{:S(2)}) collective-permute-start(bf16[32,2176]{1,0:T(8,128)(2,1)S(1)} %collective-permute-done.16.refs_2_.refs_6_), channel_id=1, source_target_pairs={{0,1},{1,0},{2,3},{3,2},{4,5},{5,4},{6,7},{7,6},{8,9},{9,8},{10,11... | collective-permute-start | bytes 417800 | tf_op jit(solution)/shard_map/ppermute | solution.py:320
  50.6 6.7 %collective-permute-start.23 = (bf16[1,32,1024]{2,1,0:T(8,128)(2,1)S(1)}, bf16[1,32,1024]{2,1,0:T(8,128)(2,1)S(1)}, u32[]{:S(2)}, u32[]{:S(2)}) collective-permute-start(bf16[1,32,1024]{2,1,0:T(8,128)(2,1)S(1)} %get-tuple-element.86), channel_id=1, source_target_pairs={{0,4},{1,5},{2,6},{3,7},{4,0},{5,1},{6,2},{7,3},{8,12},{9,13},{10,... | collective-permute-start | bytes 196616 | tf_op jit(solution)/shard_map/ppermute | solution.py:320

commit v2 on v1

v2 whole, which is shorter than its diff:
```python
import functools
import math

import jax
import jax.numpy as jnp
from jax import lax
from jax.experimental import pallas as pl
from jax.experimental.pallas import tpu as pltpu
from jax.sharding import PartitionSpec as P

HEADS = 8
HEAD_DIM = 128
BLOCK = 128
LANES = 128
SCALE = 1.0 / math.sqrt(HEAD_DIM)
SCALE2 = SCALE / math.log(2.0)
F32 = jnp.float32
BF16 = jnp.bfloat16
COST = 5_000_000_000
VMEM_LIMIT = 24 * 1024 * 1024


def dot(a, b, dims):
    return lax.dot_general(a, b, (dims, ((), ())), preferred_element_type=F32)


def nn(a, b):
    return dot(a, b, ((1,), (0,)))


def nt(a, b):
    return dot(a, b, ((1,), (1,)))


def tn(a, b):
    return dot(a, b, ((0,), (0,)))


def member(rows, cols, row_shift, col_shift, value):
    r = lax.broadcasted_iota(jnp.int32, (rows, cols), 0) >> row_shift
    c = lax.broadcasted_iota(jnp.int32, (rows, cols), 1) >> col_shift
    return jnp.where(r == c, value, 0.0).astype(BF16)


def call(kernel, outs, name, cost, *operands, scratch=(), space=pltpu.VMEM):
    return pl.pallas_call(
        kernel,
        name=name,
        out_shape=[jax.ShapeDtypeStruct(s, t) for s, t in outs],
        in_specs=[pl.BlockSpec(memory_space=space)] * len(operands),
        out_specs=[pl.BlockSpec(memory_space=pltpu.VMEM)] * len(outs),
        scratch_shapes=list(scratch),
        compiler_params=pltpu.CompilerParams(vmem_limit_bytes=VMEM_LIMIT),
        cost_estimate=pl.CostEstimate(flops=cost, bytes_accessed=1, transcendentals=0),
    )(*operands)


def pool_kernel(levels, k_ref, v_ref, *refs):
    outs, (held, sems) = refs[:-2], refs[-2:]
    tokens, width = k_ref.shape
    copies = [
        pltpu.make_async_copy(src, held.at[i], sems.at[i]) for i, src in enumerate((k_ref, v_ref))
    ]
    for copy in copies:
        copy.start()
    pools = [member(tokens >> l, tokens, 0, l, 0.5**l) for l in range(1, levels)]
    for i, copy in enumerate(copies):
        copy.wait()
        for pool, out in zip(pools, outs):
            out[i] = nn(pool, held[i]).astype(BF16)


def early_kernel(levels, q_ref, k_ref, v_ref, g_ref, w_ref, *refs):
    qhat_ref, gat_ref, e_ref, o_ref, stat_ref = refs[:5]
    qls = refs[5:]
    tokens, width = q_ref.shape
    q = q_ref[...]
    for l in range(1, levels):
        qhat_ref[l - 1] = nn(member(tokens, tokens, l, l, 0.5**l), q).astype(BF16)
        qls[l - 1][...] = nn(member(tokens >> l, tokens, 0, l, 0.5**l), q).astype(BF16)
    ones = jnp.ones((16, tokens), BF16)

    def attend(h, raw):
        hs = slice(h * HEAD_DIM, (h + 1) * HEAD_DIM)
        top = jnp.max(raw, axis=0, keepdims=True) * SCALE2
        e = jnp.exp2(raw * SCALE2 - top).astype(BF16)
        e_ref[h] = e
        both = nn(jnp.concatenate([v_ref[:, hs].T, ones], axis=0), e)
        o_ref[hs, :] = both[:HEAD_DIM]
        stat_ref[h : h + 1, :] = top
        stat_ref[HEADS + h : HEADS + h + 1, :] = both[HEAD_DIM : HEAD_DIM + 1]

    def scores(h):
        hs = slice(h * HEAD_DIM, (h + 1) * HEAD_DIM)
        return nt(k_ref[:, hs], q_ref[:, hs])

    g = g_ref[...]
    ahead = scores(0)
    for h in range(HEADS):
        raw = ahead
        if h + 1 < HEADS:
            ahead = scores(h + 1)
        if h % 2 == 0:
            rows = slice(h * HEAD_DIM, (h + 2) * HEAD_DIM)
            gat_ref[rows, :] = nt(w_ref[rows, :], g).astype(BF16)
        attend(h, raw)


def gathered(levels, pieces, kvs, which, hs):
    out, at = [], 0
    for l in range(1, levels):
        part = kvs[at : at + pieces[l - 1]]
        at += pieces[l - 1]
        out.append(jnp.concatenate([p[which, :, hs] for p in part], axis=0))
    return out


def forward_kernel(levels, pieces, dp, qhat_ref, gat_ref, o_ref, stat_ref, *refs):
    width, tokens = gat_ref.shape
    upper = levels - 1
    count = sum(pieces)
    qls, refs = refs[:upper], refs[upper:]
    kvs, refs = refs[:count], refs[count:]
    e_ref, grt_ref, grt0_ref, dd_ref, att_ref = refs[:5]
    blocks, msgs, aux_ref = refs[5 : 5 + dp], refs[5 + dp : -1], refs[-1]
    ones = jnp.ones((16, upper * BLOCK), BF16)
    sums = [member(tokens >> l, tokens, 0, l, 1.0) for l in range(1, levels)]
    aux_ref[...] = jnp.zeros_like(aux_ref)

    def scores(h):
        hs = slice(h * HEAD_DIM, (h + 1) * HEAD_DIM)
        keys = gathered(levels, pieces, kvs, 0, hs)
        return [nt(keys[l - 1], qhat_ref[l - 1, :, hs]) for l in range(1, levels)]

    def attend(h, raws):
        hs = slice(h * HEAD_DIM, (h + 1) * HEAD_DIM)
        tops = [jnp.max(raw, axis=0, keepdims=True) for raw in raws]
        top = stat_ref[h : h + 1, :]
        for l in range(1, levels):
            top = jnp.maximum(top, tops[l - 1] * SCALE2 + float(l))
        es = []
        for l, raw in enumerate(raws, 1):
            es.append(jnp.exp2(raw * SCALE2 + (float(l) - top)).astype(BF16))
            e_ref[h, (l - 1) * BLOCK : l * BLOCK, :] = es[-1]
        vals = jnp.concatenate(gathered(levels, pieces, kvs, 1, hs), axis=0)
        lhs = jnp.concatenate([vals.T, ones], axis=0)
        return top, tops, nn(lhs, jnp.concatenate(es, axis=0))

    def finish(h, top, tops, both):
        hs = slice(h * HEAD_DIM, (h + 1) * HEAD_DIM)
        a0 = jnp.exp2(stat_ref[h : h + 1, :] - top)
        den0 = stat_ref[HEADS + h : HEADS + h + 1, :]
        rden = 1.0 / (both[HEAD_DIM : HEAD_DIM + 1] + den0 * a0)
        att = ((both[:HEAD_DIM] + o_ref[hs, :] * a0) * rden).astype(BF16)
        att_ref[hs, :] = att
        grt = gat_ref[hs, :].astype(F32) * rden
        grt_ref[hs, :] = grt.astype(BF16)
        grt0_ref[hs, :] = (grt * a0).astype(BF16)
        delta = jnp.sum(grt * att.astype(F32), axis=0, keepdims=True)
        dd_ref[h : h + 1, :] = delta
        dd_ref[HEADS + h : HEADS + h + 1, :] = delta * a0
        for l in range(1, levels):
            mu = tops[l - 1].astype(BF16).astype(F32)
            a = jnp.exp2(mu * SCALE2 + (float(l) - top))
            msgs[l - 1][:, hs] = nt(sums[l - 1], (grt * a).astype(BF16)).astype(BF16)
            aux_ref[l - 1, h : h + 1, :] = mu * 0.5**l
            aux_ref[l - 1, HEADS + h : HEADS + h + 1, :] = delta * a

    ahead, behind = scores(0), None
    for h in range(HEADS):
        raws = ahead
        if h + 1 < HEADS:
            ahead = scores(h + 1)
        state = attend(h, raws)
        if behind is not None:
            finish(h - 1, *behind)
        behind = state
    finish(HEADS - 1, *behind)
    me, core = lax.axis_index("dp"), lax.axis_index("seq") & 1
    span = width // dp
    for role in range(dp):
        at = pl.multiple_of((me ^ role_mask(role, core, dp)) * span, span)
        blocks[role][...] = att_ref[pl.ds(at, span), :]
    for l in range(1, levels):
        msgs[l - 1][:, width : 2 * width] = qls[l - 1][...]
        msgs[l - 1][:, 2 * width :] = nt(sums[l - 1], aux_ref[l - 1].astype(BF16)).astype(BF16)


def backward_kernel(levels, pieces, e0_ref, e_ref, grt0_ref, grt_ref, dd_ref, *refs):
    q_ref, k_ref, v_ref = refs[:3]
    tokens, width = q_ref.shape
    kvs, (gq_ref, dk_ref, dv_ref, y_ref) = refs[3:-4], refs[-4:]

    def probs(h):
        hs = slice(h * HEAD_DIM, (h + 1) * HEAD_DIM)
        vals = jnp.concatenate(gathered(levels, pieces, kvs, 1, hs), axis=0)
        return nn(v_ref[:, hs], grt0_ref[hs, :]), nn(vals, grt_ref[hs, :])

    def rest(h, dpt0, dpt):
        hs = slice(h * HEAD_DIM, (h + 1) * HEAD_DIM)
        e0 = e0_ref[h]
        ds0 = (e0.astype(F32) * (dpt0 - dd_ref[HEADS + h : HEADS + h + 1, :])).astype(BF16)
        ds = (e_ref[h].astype(F32) * (dpt - dd_ref[h : h + 1, :])).astype(BF16)
        keys = gathered(levels, pieces, kvs, 0, hs)
        y_ref[hs, :tokens] = tn(k_ref[:, hs], ds0).astype(BF16)
        for l in range(1, levels):
            part = ds[(l - 1) * BLOCK : l * BLOCK]
            y_ref[hs, l * tokens : (l + 1) * tokens] = tn(keys[l - 1], part).astype(BF16)
        dv_ref[:, hs] = nt(e0, grt0_ref[hs, :]).astype(BF16)
        dk_ref[:, hs] = (nn(ds0, q_ref[:, hs]) * SCALE).astype(BF16)

    ahead = probs(0)
    for h in range(HEADS):
        now = ahead
        if h + 1 < HEADS:
            ahead = probs(h + 1)
        rest(h, *now)
    spread = jnp.concatenate(
        [member(tokens, tokens, l, l, 0.5**l) for l in range(levels)], axis=1
    )
    for c in range(0, width, 256):
        cs = slice(c, c + 256)
        gq_ref[:, cs] = (nt(spread, y_ref[cs, :]) * SCALE).astype(BF16)


def weight_kernel(dp, nz, *refs):
    atts, refs = refs[:dp], refs[dp:]
    grads, (keep_ref, even_ref, odd_ref, total_ref) = refs[:-4], refs[-4:]
    a = jnp.concatenate([x[...] for x in atts], axis=1)
    width = grads[0].shape[1]
    for c in range(0, width, 256):
        cs = slice(c, c + 256)
        g = jnp.concatenate([x[:, cs] for x in grads], axis=0)
        total_ref[:, cs] = nn(a, g)
    rows = total_ref.shape[0] // (2 * nz)
    seq = lax.axis_index("seq")
    core, z = seq & 1, seq >> 1
    for m in range(nz):
        base = (z ^ m) * 2 * rows
        mine = pl.multiple_of(base + core * rows, rows)
        other = pl.multiple_of(base + (1 - core) * rows, rows)
        keep_ref[m] = total_ref[pl.ds(mine, rows), :]
        send_ref = odd_ref if m % 2 else even_ref
        send_ref[m // 2] = total_ref[pl.ds(other, rows), :].astype(BF16)


def halve_kernel(count, keep_ref, *refs):
    got, (next_ref, send_ref) = refs[:count], refs[count:]

    def total(i):
        return keep_ref[i] + got[i % count][i // count].astype(F32)

    for i in range(next_ref.shape[0]):
        next_ref[i] = total(2 * i)
        send_ref[i] = total(2 * i + 1).astype(BF16)


def mixed_kernel(att_ref, w_ref, out_ref):
    att = att_ref[...].T
    for c in range(0, w_ref.shape[1], 256):
        out_ref[:, c : c + 256] = nn(att, w_ref[:, c : c + 256]).astype(BF16)


def final_kernel(factor, keep_ref, got_ref, out_ref):
    out_ref[...] = (keep_ref[0] + got_ref[0].astype(F32)) * factor


def owner_kernel(chosen, pieces, tokens, *refs):
    kvs, refs = refs[: len(chosen)], refs[len(chosen) :]
    msgs, refs = refs[: sum(pieces)], refs[sum(pieces) :]
    dk0_ref, dv0_ref, gk_ref, gv_ref, dks_ref, dvs_ref = refs
    width = dk0_ref.shape[1]
    auxes, at = [], 0
    groups = []
    for count in pieces:
        part = msgs[at : at + count]
        at += count
        groups.append(part)
        auxes.append(
            jnp.concatenate([p[:, 2 * width : 2 * width + LANES] for p in part], axis=0)
        )
    lane = lax.broadcasted_iota(jnp.int32, (tokens >> 1, LANES), 1)

    def products(h):
        hs = slice(h * HEAD_DIM, (h + 1) * HEAD_DIM)
        qs = slice(width + h * HEAD_DIM, width + (h + 1) * HEAD_DIM)
        minus_mu = jnp.where(lane == h, -1.0, 0.0).astype(BF16)
        minus_d = jnp.where(lane == HEADS + h, -1.0, 0.0).astype(BF16)
        out = []
        for group, aux, kv, l in zip(groups, auxes, kvs, chosen):
            n = tokens >> l
            ga = jnp.concatenate([p[:, hs] for p in group], axis=0)
            q = jnp.concatenate([p[:, qs] for p in group], axis=0)
            k = jnp.concatenate([kv[0, :, hs], minus_mu[:n]], axis=1)
            v = jnp.concatenate([kv[1, :, hs], minus_d[:n]], axis=1)
            raw = nt(k, jnp.concatenate([q, aux], axis=1))
            out.append((ga, q, raw, nt(v, jnp.concatenate([ga, aux], axis=1))))
        return out

    def gradients(h, parts):
        hs = slice(h * HEAD_DIM, (h + 1) * HEAD_DIM)
        at = 0
        for ga, q, raw, dp_raw in parts:
            n = raw.shape[0]
            e = jnp.exp2(raw * SCALE2)
            ds = (e * dp_raw).astype(BF16)
            dvs_ref[at : at + n, hs] = nn(e.astype(BF16), ga).astype(BF16)
            dks_ref[at : at + n, hs] = (nn(ds, q) * SCALE).astype(BF16)
            at += n

    depth = 2 if len(chosen) > 1 else HEADS
    ahead = [products(h) for h in range(depth)]
    for h in range(HEADS):
        parts = ahead.pop(0)
        if h + depth < HEADS:
            ahead.append(products(h + depth))
        gradients(h, parts)
    spread = jnp.concatenate([member(tokens, tokens >> l, l, 0, 0.5**l) for l in chosen], axis=1)
    for c in range(0, width, 256):
        cs = slice(c, c + 256)
        gk = dk0_ref[:, cs].astype(F32) + nn(spread, dks_ref[:, cs])
        gv = dv0_ref[:, cs].astype(F32) + nn(spread, dvs_ref[:, cs])
        gk_ref[:, cs] = gk.astype(gk_ref.dtype)
        gv_ref[:, cs] = gv.astype(gv_ref.dtype)


def after(x, *others):
    return lax.optimization_barrier((x, *others))[0]


def role_mask(role, core, dp):
    if dp != 4 or role % 3 == 0:
        return role
    return role + core if role == 1 else role - core


def exchange_role(x, role):
    dp, seq = lax.axis_size("dp"), lax.axis_size("seq")
    pairs = []
    for i in range(dp):
        for j in range(seq):
            pairs.append((i * seq + j, (i ^ role_mask(role, j & 1, dp)) * seq + j))
    return lax.ppermute(x, ("dp", "seq"), pairs)


def swap(x, axis, mask):
    count = lax.axis_size(axis)
    return lax.ppermute(x, axis, [(i, i ^ mask) for i in range(count)])


def body(queries, keys, values, grad_out, w_out):
    seq = lax.axis_size("seq")
    dp = lax.axis_size("dp")
    nz = seq // 2
    levels = seq.bit_length()
    upper = levels - 1
    q, k, v, g = queries[0], keys[0], values[0], grad_out[0]
    tokens, width = q.shape
    factor = 1.0 / math.sqrt(dp * seq * tokens)

    own = call(
        functools.partial(pool_kernel, levels),
        [((2, tokens >> l, width), BF16) for l in range(1, levels)],
        "pool",
        1,
        k,
        v,
        scratch=[pltpu.VMEM((2, tokens, width), BF16), pltpu.SemaphoreType.DMA((2,))],
        space=pltpu.HBM,
    )

    def across(per_level):
        return [
            (m.bit_length(), swap(per_level[m.bit_length()], "seq", 2 * m)) for m in range(1, nz)
        ]

    def joined(first, received, *wait):
        got = [[swap(first, "seq", 1)]] + [[] for _ in range(upper - 1)]
        for at, x in received:
            x = after(x, *wait)
            got[at] += [x, swap(x, "seq", 1)]
        axis = first.ndim - 2
        return [x if x[0].shape[axis] >= 16 else [jnp.concatenate(x, axis=axis)] for x in got]

    received = across(own)

    early = call(
        functools.partial(early_kernel, levels),
        [
            ((upper, tokens, width), BF16),
            ((width, tokens), BF16),
            ((HEADS, tokens, tokens), BF16),
            ((width, tokens), F32),
            ((2 * HEADS, tokens), F32),
        ]
        + [((tokens >> l, width), BF16) for l in range(1, levels)],
        "early",
        1,
        after(q, own[0]),
        k,
        v,
        g,
        w_out,
    )
    qhat, gat, e0, o0, stats = early[:5]
    qls = early[5:]

    g_late = after(g, own[0])
    grads = [g] + [exchange_role(g_late, r) for r in range(1, min(dp, 3))]
    if dp == 4:
        grads.append(exchange_role(grads[1], 2))
    else:
        grads += [exchange_role(g_late, r) for r in range(3, dp)]

    stats = after(stats, *grads[1:3])
    arrived = [x for _, x in received]
    arrived += [gat]
    pairs = joined(after(own[0], *arrived), received, *arrived)
    pieces = [len(x) for x in pairs]
    flat = [x for part in pairs for x in part]

    outs = [
        ((HEADS, upper * BLOCK, tokens), BF16),
        ((width, tokens), BF16),
        ((width, tokens), BF16),
        ((2 * HEADS, tokens), F32),
        ((width, tokens), BF16),
    ]
    outs += [((width // dp, tokens), BF16)] * dp
    outs += [((tokens >> l, 2 * width + LANES), BF16) for l in range(1, levels)]
    forward = call(
        functools.partial(forward_kernel, levels, pieces, dp),
        outs,
        "forward",
        1,
        qhat,
        gat,
        o0,
        stats,
        *qls,
        *flat,
        scratch=[pltpu.VMEM((upper, LANES, tokens), F32)],
    )
    e, grt, grt0, dd, att = forward[:5]
    blocks, outgoing = forward[5 : 5 + dp], forward[5 + dp :]

    atts = [blocks[0]] + [exchange_role(blocks[r], r) for r in range(1, dp)]
    relayed = nz == 4
    if relayed:
        far = swap(after(outgoing[2], *grads[3:4]), "seq", 4)
        near = swap(after(outgoing[1], *grads[3:]), "seq", 2)
    else:
        received = across(outgoing)

    rows = width // dp
    own_rows = rows // (2 * nz)
    keep, even, odd = call(
        functools.partial(weight_kernel, dp, nz),
        [((nz, own_rows, width), F32)] + [((nz // 2, own_rows, width), BF16)] * 2,
        "weight",
        COST,
        *atts,
        *grads,
        scratch=[pltpu.VMEM((rows, width), F32)],
    )

    def halve(keep, *got):
        n = keep.shape[0] // 2
        outs = [((n, own_rows, width), F32), ((n, own_rows, width), BF16)]
        return call(functools.partial(halve_kernel, len(got)), outs, "halve", 1, keep, *got)

    keep, send = halve(keep, swap(even, "seq", 1), swap(odd, "seq", 1))
    came = swap(send, "seq", 2)
    if relayed:
        relay = swap(after(far, keep, near), "seq", 2)
        near = after(near, keep)
    grt = after(grt, keep)

    gq, dk0, dv0 = call(
        functools.partial(backward_kernel, levels, pieces),
        [((tokens, width), BF16)] * 3,
        "backward",
        COST,
        e0,
        e,
        grt0,
        grt,
        dd,
        q,
        k,
        v,
        *flat,
        scratch=[pltpu.VMEM((width, levels * tokens), BF16)],
    )

    def owned(chosen, messages, dk, dv, dtype):
        flat = [x for part in messages for x in part]
        rows = sum(tokens >> l for l in chosen)
        return call(
            functools.partial(owner_kernel, chosen, [len(x) for x in messages], tokens),
            [((tokens, width), dtype)] * 2,
            "owner",
            1,
            *[own[l - 1] for l in chosen],
            *flat,
            dk,
            dv,
            scratch=[pltpu.VMEM((rows, width), BF16)] * 2,
        )

    last = levels - 1
    some = list(range(1, last))
    step = 2
    first = after(outgoing[0], keep)
    keep = after(keep, dk0)
    while keep.shape[0] > 1:
        keep, send = halve(keep, came)
        step *= 2
        came = swap(send, "seq", step)
    if relayed:
        messages = [[swap(first, "seq", 1)], [near, swap(near, "seq", 1)]]
        far, relay = after(far, send), after(relay, send)
        messages.append([far, swap(far, "seq", 1), relay, swap(relay, "seq", 1)])
    else:
        messages = joined(first, received, dk0, send)
    gk, gv = owned(some, messages[:-1], after(dk0, send), dv0, F32)
    mixed = call(mixed_kernel, [((tokens, width), BF16)], "mixed", 1, after(att, gk), w_out)[0]
    gk, gv = owned([last], messages[-1:], gk, gv, BF16)

    (gw,) = call(
        functools.partial(final_kernel, factor),
        [((own_rows, width), F32)],
        "total",
        1,
        after(keep, gk),
        came,
    )
    return (mixed[None], gq[None], gk[None], gv[None], gw)


def solution(mesh):
    rows = P("dp", "seq", None)
    return jax.shard_map(
        body,
        mesh=mesh,
        in_specs=(rows, rows, rows, rows, P()),
        out_specs=(rows, rows, rows, rows, P(("dp", "seq"), None)),
        check_vma=False,
    )
```

time: 58.4 us -> 56.4 us (0.966)
  starting transfers between devices: 25.6 us -> 22.7 us
  local copies, waits for them, and re-layouts: 5.81 us -> 7.85 us
  waiting for transfers between devices: 11 us -> 9.02 us
  Pallas kernels: 14.9 us -> 15.6 us
    ppermute x24 -> x18, starting transfers between devices: 25.6 us -> 14 us  [swap(): return lax.ppermute(x, axis, [(i, i ^ mask) for i in range(count)])]
    ppermute x0 -> x6, starting transfers between devices: none -> 8.65 us  [exchange_role(): return lax.ppermute(x, ('dp', 'seq'), pairs)]
    ppermute x24 -> x18, waiting for transfers between devices: 11 us -> 6.41 us  [swap(): return lax.ppermute(x, axis, [(i, i ^ mask) for i in range(count)])]
    ppermute x0 -> x6, waiting for transfers between devices: none -> 2.61 us  [exchange_role(): return lax.ppermute(x, ('dp', 'seq'), pairs)]
    unnamed x20 -> x24, local copies, waits for them, and re-layouts: 5.77 us -> 7.85 us
    pallas_call x10 -> x11, Pallas kernels: 14.9 us -> 15.6 us  [call(): pl.pallas_call(kernel, name=name, out_shape=[jax.ShapeDtypeStruct(s, t) f...]
  transfers between devices with their start and end apart: 24 -> 24, of which waited for: 8 -> 10; matrix products, arithmetic and copies ran while one was open for 0% -> 0% of each run, Pallas kernels for 23% -> 25%
where the time goes in v2:
time: 56.4 us; the launch traced here: 56 us
  starting transfers between devices  22.7 us (40%)
  Pallas kernels  15.6 us (28%)
  waiting for transfers between devices  9.02 us (16%)
  local copies, waits for them, and re-layouts  7.85 us (14%)
  between operations  0.76 us (1%)
    pallas_call x11, Pallas kernels, call(): pl.pallas_call(kernel, name=name, out_shape=[jax.ShapeDtypeStruct(s, t) f...  15.6 us
    ppermute x18, starting transfers between devices, swap(): return lax.ppermute(x, axis, [(i, i ^ mask) for i in range(count)])  14 us
    ppermute x6, starting transfers between devices, exchange_role(): return lax.ppermute(x, ('dp', 'seq'), pairs)  8.65 us
    unnamed x24, local copies, waits for them, and re-layouts  7.85 us
    ppermute x18, waiting for transfers between devices, swap(): return lax.ppermute(x, axis, [(i, i ^ mask) for i in range(count)])  6.41 us
    ppermute x6, waiting for transfers between devices, exchange_role(): return lax.ppermute(x, ('dp', 'seq'), pairs)  2.61 us
  transfers between devices with their start and end apart: 24, of which 10 were waited for; matrix products, arithmetic and copies ran while one was open for 0% of the time, Pallas kernels for 25%

profile of v2, /device:TPU:0, one launch (start us, length us, event | category | flops | bytes accessed | tf_op | source)
XLA Modules:
  0.0 56.0 jit_solution(17787132566579422943)
XLA Ops:
  0.6 0.0 copy-start.2
  0.6 1.0 %copy-done.2 = bf16[1,256,1024]{2,1,0:T(8,128)(2,1)S(1)} copy-done((bf16[1,256,1024]{2,1,0:T(8,128)(2,1)S(1)}, bf16[1,256,1024]{2,1,0:T(8,128)(2,1)}, u32[]{:S(2)}) %copy-start.2) | copy-done | bytes 524312
  1.7 1.0 %copy-done.5 = bf16[1,256,1024]{2,1,0:T(8,128)(2,1)S(1)} copy-done((bf16[1,256,1024]{2,1,0:T(8,128)(2,1)S(1)}, bf16[1,256,1024]{2,1,0:T(8,128)(2,1)}, u32[]{:S(2)}) %copy-start.5) | copy-done | bytes 524312
  2.7 0.9 %pool.1 = (bf16[2,128,1024]{2,1,0:T(8,128)(2,1)S(1)}, bf16[2,64,1024]{2,1,0:T(8,128)(2,1)S(1)}, bf16[2,32,1024]{2,1,0:T(8,128)(2,1)S(1)}) custom-call(bf16[256,1024]{1,0:T(8,128)(2,1)S(1)} %bitcast.8, bf16[256,1024]{1,0:T(8,128)(2,1)S(1)} %bitcast.11), custom_call_target="tpu_custom_call" | custom-call | flops 1 | bytes 1 | tf_op jit(solution)/shard_map/pool/pallas_call | solution.py:46
  3.6 3.0 %collective-permute-start = (bf16[256,1024]{1,0:T(8,128)(2,1)}, bf16[256,1024]{1,0:T(8,128)(2,1)S(1)}, u32[]{:S(2)}, u32[]{:S(2)}) collective-permute-start(bf16[256,1024]{1,0:T(8,128)(2,1)} %bitcast.14), channel_id=1, source_target_pairs={{0,8},{1,17},{2,10},{3,19},{4,12},{5,21},{6,14},{7,23},{8,0},{9,25... | collective-permute-start | bytes 1572872 | tf_op jit(solution)/shard_map/ppermute | solution.py:343
  6.6 1.6 %collective-permute-start.2 = (bf16[2,64,1024]{2,1,0:T(8,128)(2,1)S(1)}, bf16[2,64,1024]{2,1,0:T(8,128)(2,1)S(1)}, u32[]{:S(2)}, u32[]{:S(2)}) collective-permute-start(bf16[2,64,1024]{2,1,0:T(8,128)(2,1)S(1)} %get-tuple-element.72.refs_1_), channel_id=1, source_target_pairs={{0,2},{1,3},{2,0},{3,1},{4,6},{5,7},{6,4},{7,5},{8,10},{9,11},{10,... | collective-permute-start | bytes 786440 | tf_op jit(solution)/shard_map/ppermute | solution.py:348
  8.2 2.6 %collective-permute-start.3 = (bf16[2,32,1024]{2,1,0:T(8,128)(2,1)S(1)}, bf16[2,32,1024]{2,1,0:T(8,128)(2,1)S(1)}, u32[]{:S(2)}, u32[]{:S(2)}) collective-permute-start(bf16[2,32,1024]{2,1,0:T(8,128)(2,1)S(1)} %get-tuple-element.73.refs_0_), channel_id=1, source_target_pairs={{0,4},{1,5},{2,6},{3,7},{4,0},{5,1},{6,2},{7,3},{8,12},{9,13},{10,... | collective-permute-start | bytes 393224 | tf_op jit(solution)/shard_map/ppermute | solution.py:348
  10.8 0.2 collective-permute-start.4
  11.0 1.5 %collective-permute-start.1 = (bf16[256,1024]{1,0:T(8,128)(2,1)}, bf16[256,1024]{1,0:T(8,128)(2,1)S(1)}, u32[]{:S(2)}, u32[]{:S(2)}) collective-permute-start(bf16[256,1024]{1,0:T(8,128)(2,1)} %bitcast.15), channel_id=1, source_target_pairs={{0,16},{1,9},{2,18},{3,11},{4,20},{5,13},{6,22},{7,15},{8,24},{9,1... | collective-permute-start | bytes 1572872 | tf_op jit(solution)/shard_map/ppermute | solution.py:343
  12.5 1.6 %copy-done = bf16[1024,1024]{1,0:T(8,128)(2,1)S(1)} copy-done((bf16[1024,1024]{1,0:T(8,128)(2,1)S(1)}, bf16[1024,1024]{1,0:T(8,128)(2,1)}, u32[]{:S(2)}) %copy-start) | copy-done | bytes 2097176
  14.1 1.0 %copy-done.3 = bf16[1,256,1024]{2,1,0:T(8,128)(2,1)S(1)} copy-done((bf16[1,256,1024]{2,1,0:T(8,128)(2,1)S(1)}, bf16[1,256,1024]{2,1,0:T(8,128)(2,1)}, u32[]{:S(2)}) %copy-start.3) | copy-done | bytes 524312
  15.1 1.0 %copy-done.6 = bf16[1,256,1024]{2,1,0:T(8,128)(2,1)S(1)} copy-done((bf16[1,256,1024]{2,1,0:T(8,128)(2,1)S(1)}, bf16[1,256,1024]{2,1,0:T(8,128)(2,1)}, u32[]{:S(2)}) %copy-start.6) | copy-done | bytes 524312
  16.2 1.0 %copy-done.8 = bf16[1,256,1024]{2,1,0:T(8,128)(2,1)S(1)} copy-done((bf16[1,256,1024]{2,1,0:T(8,128)(2,1)S(1)}, bf16[1,256,1024]{2,1,0:T(8,128)(2,1)}, u32[]{:S(2)}) %copy-start.8) | copy-done | bytes 524312
  17.2 1.0 %copy-done.10 = bf16[1,256,1024]{2,1,0:T(8,128)(2,1)S(1)} copy-done((bf16[1,256,1024]{2,1,0:T(8,128)(2,1)S(1)}, bf16[1,256,1024]{2,1,0:T(8,128)(2,1)}, u32[]{:S(2)}) %copy-start.10) | copy-done | bytes 524312
  18.3 2.3 %early.1 = (bf16[3,256,1024]{2,1,0:T(8,128)(2,1)S(1)}, bf16[1024,256]{1,0:T(8,128)(2,1)S(1)}, bf16[8,256,256]{2,1,0:T(8,128)(2,1)S(1)}, f32[1024,256]{1,0:T(8,12...) custom-call(bf16[256,1024]{1,0:T(8,128)(2,1)S(1)} %bitcast.18, ...), custom_call_target="tpu_custom_call" | custom-call | flops 1 | bytes 1 | tf_op jit(solution)/shard_map/early/pallas_call | solution.py:46
  20.6 0.0 collective-permute-done.3.refs_6_
  20.6 1.5 %collective-permute-done.4.refs_8_ = bf16[2,32,1024]{2,1,0:T(8,128)(2,1)S(1)} collective-permute-done((bf16[2,32,1024]{2,1,0:T(8,128)(2,1)S(1)}, bf16[2,32,1024]{2,1,0:T(8,128)(2,1)S(1)}, u32[]{:S(2)}, u32[]{:S(2)}) %collective-permute-start.4) | collective-permute-done | bytes 131104 | tf_op jit(solution)/shard_map/ppermute | solution.py:348
  22.1 0.0 collective-permute-done.2.refs_4_
  22.2 0.0 collective-permute-start.5
  22.2 0.0 collective-permute-done.refs_5_
  22.2 0.6 %collective-permute-start.12 = (bf16[256,1024]{1,0:T(8,128)(2,1)S(1)}, bf16[256,1024]{1,0:T(8,128)(2,1)S(1)}, u32[]{:S(2)}, u32[]{:S(2)}) collective-permute-start(bf16[256,1024]{1,0:T(8,128)(2,1)S(1)} %collective-permute-done.refs_5_), channel_id=1, source_target_pairs={{0,16},{1,9},{2,18},{3,11},{4,20},{5,13},{6,22},{7,15},{8,24},{9,1... | collective-permute-start | bytes 1572872 | tf_op jit(solution)/shard_map/ppermute | solution.py:343
  22.7 1.1 %collective-permute-start.6 = (bf16[2,64,1024]{2,1,0:T(8,128)(2,1)S(1)}, bf16[2,64,1024]{2,1,0:T(8,128)(2,1)S(1)}, u32[]{:S(2)}, u32[]{:S(2)}) collective-permute-start(bf16[2,64,1024]{2,1,0:T(8,128)(2,1)S(1)} %collective-permute-done.2.refs_4_), channel_id=1, source_target_pairs={{0,1},{1,0},{2,3},{3,2},{4,5},{5,4},{6,7},{7,6},{8,9},{9,8},{10,11... | collective-permute-start | bytes 786440 | tf_op jit(solution)/shard_map/ppermute | solution.py:348
  23.9 0.0 collective-permute-start.8
  23.9 0.0 collective-permute-done.1.refs_6_
  23.9 0.5 collective-permute-start.7
  24.4 0.8 %collective-permute-done.8.refs_9_ = bf16[2,32,1024]{2,1,0:T(8,128)(2,1)S(1)} collective-permute-done((bf16[2,32,1024]{2,1,0:T(8,128)(2,1)S(1)}, bf16[2,32,1024]{2,1,0:T(8,128)(2,1)S(1)}, u32[]{:S(2)}, u32[]{:S(2)}) %collective-permute-start.8) | collective-permute-done | bytes 131104 | tf_op jit(solution)/shard_map/ppermute | solution.py:348
  25.2 0.2 collective-permute-done.7.refs_7_
  25.4 0.0 collective-permute-done.6.refs_5_
  25.4 0.0 collective-permute-done.5.refs_3_
  25.4 2.6 %forward.1 = (bf16[8,384,256]{2,1,0:T(8,128)(2,1)S(1)}, bf16[1024,256]{1,0:T(8,128)(2,1)S(1)}, bf16[1024,256]{1,0:T(8,128)(2,1)S(1)}, f32[16,256]{1,0:T(8,128)S(...) custom-call(bf16[3,256,1024]{2,1,0:T(8,128)(2,1)S(1)} %get-tuple-ele, ...), custom_call_target="tpu_custom_call" | custom-call | flops 1 | bytes 1 | tf_op jit(solution)/shard_map/forward/pallas_call | solution.py:46
  28.0 0.8 %collective-permute-start.10 = (bf16[256,256]{1,0:T(8,128)(2,1)S(1)}, bf16[256,256]{1,0:T(8,128)(2,1)S(1)}, u32[]{:S(2)}, u32[]{:S(2)}) collective-permute-start(bf16[256,256]{1,0:T(8,128)(2,1)S(1)} %get-tuple-element.82), channel_id=1, source_target_pairs={{0,16},{1,9},{2,18},{3,11},{4,20},{5,13},{6,22},{7,15},{8,24},{9,1... | collective-permute-start | bytes 393224 | tf_op jit(solution)/shard_map/ppermute | solution.py:343
  28.8 1.6 %collective-permute-start.11 = (bf16[256,256]{1,0:T(8,128)(2,1)S(1)}, bf16[256,256]{1,0:T(8,128)(2,1)S(1)}, u32[]{:S(2)}, u32[]{:S(2)}) collective-permute-start(bf16[256,256]{1,0:T(8,128)(2,1)S(1)} %get-tuple-element.83), channel_id=1, source_target_pairs={{0,24},{1,25},{2,26},{3,27},{4,28},{5,29},{6,30},{7,31},{8,16},{9,... | collective-permute-start | bytes 393224 | tf_op jit(solution)/shard_map/ppermute | solution.py:343
  30.4 1.1 %collective-permute-start.9 = (bf16[256,256]{1,0:T(8,128)(2,1)S(1)}, bf16[256,256]{1,0:T(8,128)(2,1)S(1)}, u32[]{:S(2)}, u32[]{:S(2)}) collective-permute-start(bf16[256,256]{1,0:T(8,128)(2,1)S(1)} %get-tuple-element.81), channel_id=1, source_target_pairs={{0,8},{1,17},{2,10},{3,19},{4,12},{5,21},{6,14},{7,23},{8,0},{9,25... | collective-permute-start | bytes 393224 | tf_op jit(solution)/shard_map/ppermute | solution.py:343
  31.6 0.0 collective-permute-done.12.refs_7_
  31.6 0.7 %collective-permute-start.16 = (bf16[64,2176]{1,0:T(8,128)(2,1)S(1)}, bf16[64,2176]{1,0:T(8,128)(2,1)S(1)}, u32[]{:S(2)}, u32[]{:S(2)}) collective-permute-start(bf16[64,2176]{1,0:T(8,128)(2,1)S(1)} %get-tuple-element.90), channel_id=1, source_target_pairs={{0,2},{1,3},{2,0},{3,1},{4,6},{5,7},{6,4},{7,5},{8,10},{9,11},{10,... | collective-permute-start | bytes 835592 | tf_op jit(solution)/shard_map/ppermute | solution.py:348
  32.3 1.9 %collective-permute-start.19 = (bf16[32,2176]{1,0:T(8,128)(2,1)S(1)}, bf16[32,2176]{1,0:T(8,128)(2,1)S(1)}, u32[]{:S(2)}, u32[]{:S(2)}) collective-permute-start(bf16[32,2176]{1,0:T(8,128)(2,1)S(1)} %get-tuple-element.108), channel_id=1, source_target_pairs={{0,4},{1,5},{2,6},{3,7},{4,0},{5,1},{6,2},{7,3},{8,12},{9,13},{10,... | collective-permute-start | bytes 417800 | tf_op jit(solution)/shard_map/ppermute | solution.py:348
  34.1 2.4 %collective-permute-done.10.refs_2_ = bf16[256,256]{1,0:T(8,128)(2,1)S(1)} collective-permute-done((bf16[256,256]{1,0:T(8,128)(2,1)S(1)}, bf16[256,256]{1,0:T(8,128)(2,1)S(1)}, u32[]{:S(2)}, u32[]{:S(2)}) %collective-permute-start.10) | collective-permute-done | bytes 131104 | tf_op jit(solution)/shard_map/ppermute | solution.py:343
  36.5 0.2 collective-permute-done.9.refs_1_
  36.7 0.8 %weight.1 = (f32[4,32,1024]{2,1,0:T(8,128)S(1)}, bf16[2,32,1024]{2,1,0:T(8,128)(2,1)S(1)}, bf16[2,32,1024]{2,1,0:T(8,128)(2,1)S(1)}) custom-call(bf16[256,256]{1,0:T(8,128)(2,1)S(1)} %get-tuple-element.80.refs_0_, bf16[256,256]{1,0:T(8,128)(2,1)S(1)} %collective-permute-done.9.refs_1_, bf16[256,256]{1,0:T(8,128)(2,1)S(1)} %collective-permute-done.10.refs_2_, ...), custom_call_target="tpu_custom_call" | custom-call | flops 5000000000 | bytes 1 | tf_op jit(solution)/shard_map/weight/pallas_call | solution.py:46
  37.5 0.7 %collective-permute-start.13 = (bf16[2,32,1024]{2,1,0:T(8,128)(2,1)S(1)}, bf16[2,32,1024]{2,1,0:T(8,128)(2,1)S(1)}, u32[]{:S(2)}, u32[]{:S(2)}) collective-permute-start(bf16[2,32,1024]{2,1,0:T(8,128)(2,1)S(1)} %get-tuple-element.85), channel_id=1, source_target_pairs={{0,1},{1,0},{2,3},{3,2},{4,5},{5,4},{6,7},{7,6},{8,9},{9,8},{10,11... | collective-permute-start | bytes 393224 | tf_op jit(solution)/shard_map/ppermute | solution.py:348
  38.3 0.1 collective-permute-start.14
  38.3 0.9 %collective-permute-done.13.refs_0_ = bf16[2,32,1024]{2,1,0:T(8,128)(2,1)S(1)} collective-permute-done((bf16[2,32,1024]{2,1,0:T(8,128)(2,1)S(1)}, bf16[2,32,1024]{2,1,0:T(8,128)(2,1)S(1)}, u32[]{:S(2)}, u32[]{:S(2)}) %collective-permute-start.13) | collective-permute-done | bytes 131104 | tf_op jit(solution)/shard_map/ppermute | solution.py:348
  39.2 0.4 collective-permute-done.14.refs_1_
  39.7 0.7 %collective-permute-start.18 = (bf16[2,32,1024]{2,1,0:T(8,128)(2,1)S(1)}, bf16[2,32,1024]{2,1,0:T(8,128)(2,1)S(1)}, u32[]{:S(2)}, u32[]{:S(2)}) collective-permute-start(bf16[2,32,1024]{2,1,0:T(8,128)(2,1)S(1)} %get-tuple-element.100), channel_id=1, source_target_pairs={{0,2},{1,3},{2,0},{3,1},{4,6},{5,7},{6,4},{7,5},{8,10},{9,11},{10,... | collective-permute-start | bytes 393224 | tf_op jit(solution)/shard_map/ppermute | solution.py:348
  40.4 0.0 collective-permute-start.15
  40.4 0.6 %collective-permute-done.19.refs_1_ = bf16[32,2176]{1,0:T(8,128)(2,1)S(1)} collective-permute-done((bf16[32,2176]{1,0:T(8,128)(2,1)S(1)}, bf16[32,2176]{1,0:T(8,128)(2,1)S(1)}, u32[]{:S(2)}, u32[]{:S(2)}) %collective-permute-start.19) | collective-permute-done | bytes 139296 | tf_op jit(solution)/shard_map/ppermute | solution.py:348
  41.0 1.8 %collective-permute-done.16.refs_3_ = bf16[64,2176]{1,0:T(8,128)(2,1)S(1)} collective-permute-done((bf16[64,2176]{1,0:T(8,128)(2,1)S(1)}, bf16[64,2176]{1,0:T(8,128)(2,1)S(1)}, u32[]{:S(2)}, u32[]{:S(2)}) %collective-permute-start.16) | collective-permute-done | bytes 278560 | tf_op jit(solution)/shard_map/ppermute | solution.py:348
  42.8 1.7 %collective-permute-start.21 = (bf16[32,2176]{1,0:T(8,128)(2,1)S(1)}, bf16[32,2176]{1,0:T(8,128)(2,1)S(1)}, u32[]{:S(2)}, u32[]{:S(2)}) collective-permute-start(bf16[32,2176]{1,0:T(8,128)(2,1)S(1)} %collective-permute-done.19.refs_1_), channel_id=1, source_target_pairs={{0,2},{1,3},{2,0},{3,1},{4,6},{5,7},{6,4},{7,5},{8,10},{9,11},{10,... | collective-permute-start | bytes 417800 | tf_op jit(solution)/shard_map/ppermute | solution.py:348
  44.5 3.4 %backward.1 = (bf16[256,1024]{1,0:T(8,128)(2,1)}, bf16[256,1024]{1,0:T(8,128)(2,1)S(1)}, bf16[256,1024]{1,0:T(8,128)(2,1)S(1)}) custom-call(bf16[8,256,256]{2,1,0:T(8,128)(2,1)S(1)} %get-tuple-element.92.e0_ref, bf16[8,384,256]{2,1,0:T(8,128)(2,1)S(1)} %get-tuple-element.93.e_ref, bf16[1024,256]{1,0:T(8,128)(2,1)S(1)} %get-tuple-element.94.grt0_ref, ...), custom_call_target="tpu_custom_call" | custom-call | flops 5000000000 | bytes 1 | tf_op jit(solution)/shard_map/backward/pallas_call | solution.py:46
  47.9 0.0 collective-permute-done.18.refs_0_
  47.9 0.0 copy-start.1
  47.9 0.6 collective-permute-start.20
  48.5 0.0 collective-permute-done.21.refs_3_
  48.5 0.1 collective-permute-start.22
  48.6 1.6 %collective-permute-start.23 = (bf16[1,32,1024]{2,1,0:T(8,128)(2,1)S(1)}, bf16[1,32,1024]{2,1,0:T(8,128)(2,1)S(1)}, u32[]{:S(2)}, u32[]{:S(2)}) collective-permute-start(bf16[1,32,1024]{2,1,0:T(8,128)(2,1)S(1)} %get-tuple-element.101), channel_id=1, source_target_pairs={{0,4},{1,5},{2,6},{3,7},{4,0},{5,1},{6,2},{7,3},{8,12},{9,13},{10,... | collective-permute-start | bytes 196616 | tf_op jit(solution)/shard_map/ppermute | solution.py:348
  50.2 0.0 collective-permute-done.17.refs_4_
  50.2 0.0 collective-permute-done.15.refs_2_
  50.2 1.5 %owner.2 = (f32[256,1024]{1,0:T(8,128)S(1)}, f32[256,1024]{1,0:T(8,128)S(1)}) custom-call(bf16[2,128,1024]{2,1,0:T(8,128)(2,1)S(1)} %get-tuple-element.74.refs_0_, bf16[2,64,1024]{2,1,0:T(8,128)(2,1)S(1)} %get-tuple-element.72.refs_1_, bf16[128,2176]{1,0:T(8,128)(2,1)S(1)} %collective-permute-done.15.refs_2_, ...), custom_call_target="tpu_custom_call" | custom-call | flops 1 | bytes 1 | tf_op jit(solution)/shard_map/owner/pallas_call | solution.py:46
  51.7 1.5 %mixed.1 = bf16[256,1024]{1,0:T(8,128)(2,1)} custom-call(bf16[1024,256]{1,0:T(8,128)(2,1)S(1)} %get-tuple-element.105.att_ref, bf16[1024,1024]{1,0:T(8,128)(2,1)S(1)} %copy-done.1), custom_call_target="tpu_custom_call" | custom-call | flops 1 | bytes 1 | tf_op jit(solution)/shard_map/mixed/pallas_call | solution.py:46
  53.2 0.0 collective-permute-done.20.refs_2_
  53.2 0.0 collective-permute-done.22.refs_4_
  53.2 1.9 %owner.3 = (bf16[256,1024]{1,0:T(8,128)(2,1)}, bf16[256,1024]{1,0:T(8,128)(2,1)}) custom-call(bf16[2,32,1024]{2,1,0:T(8,128)(2,1)S(1)} %get-tuple-element.73.refs_0_, bf16[32,2176]{1,0:T(8,128)(2,1)S(1)} %collective-permute-done.19.refs_1_, bf16[32,2176]{1,0:T(8,128)(2,1)S(1)} %collective-permute-done.20.refs_2_, ...), custom_call_target="tpu_custom_call" | custom-call | flops 1 | bytes 1 | tf_op jit(solution)/shard_map/owner/pallas_call | solution.py:46
  55.1 0.2 collective-permute-done.23.got_ref
  55.3 0.7 %total.1 = f32[32,1024]{1,0:T(8,128)} custom-call(f32[1,32,1024]{2,1,0:T(8,128)S(1)} %get-tuple-element.116.keep_ref, bf16[1,32,1024]{2,1,0:T(8,128)(2,1)S(1)} %collective-permute-done.23.got_ref), custom_call_target="tpu_custom_call" | custom-call | flops 1 | bytes 1 | tf_op jit(solution)/shard_map/total/pallas_call | solution.py:46
  (19 shorter events, 0.1 us)
Async XLA Ops:
  0.6 1.0 %copy-start.2 = (bf16[1,256,1024]{2,1,0:T(8,128)(2,1)S(1)}, bf16[1,256,1024]{2,1,0:T(8,128)(2,1)}, u32[]{:S(2)}) copy-start(bf16[1,256,1024]{2,1,0:T(8,128)(2,1)} %param.6) | copy-start | bytes 1572868
  1.7 1.0 %copy-start.5 = (bf16[1,256,1024]{2,1,0:T(8,128)(2,1)S(1)}, bf16[1,256,1024]{2,1,0:T(8,128)(2,1)}, u32[]{:S(2)}) copy-start(bf16[1,256,1024]{2,1,0:T(8,128)(2,1)} %param.7) | copy-start | bytes 1572868
  3.6 18.6 %collective-permute-start = (bf16[256,1024]{1,0:T(8,128)(2,1)}, bf16[256,1024]{1,0:T(8,128)(2,1)S(1)}, u32[]{:S(2)}, u32[]{:S(2)}) collective-permute-start(bf16[256,1024]{1,0:T(8,128)(2,1)} %bitcast.14), channel_id=1, source_target_pairs={{0,8},{1,17},{2,10},{3,19},{4,12},{5,21},{6,14},{7,23},{8,0},{9,25... | collective-permute-start | bytes 1572872 | tf_op jit(solution)/shard_map/ppermute | solution.py:343
  6.6 15.5 %collective-permute-start.2 = (bf16[2,64,1024]{2,1,0:T(8,128)(2,1)S(1)}, bf16[2,64,1024]{2,1,0:T(8,128)(2,1)S(1)}, u32[]{:S(2)}, u32[]{:S(2)}) collective-permute-start(bf16[2,64,1024]{2,1,0:T(8,128)(2,1)S(1)} %get-tuple-element.72.refs_1_), channel_id=1, source_target_pairs={{0,2},{1,3},{2,0},{3,1},{4,6},{5,7},{6,4},{7,5},{8,10},{9,11},{10,... | collective-permute-start | bytes 786440 | tf_op jit(solution)/shard_map/ppermute | solution.py:348
  8.2 12.4 %collective-permute-start.3 = (bf16[2,32,1024]{2,1,0:T(8,128)(2,1)S(1)}, bf16[2,32,1024]{2,1,0:T(8,128)(2,1)S(1)}, u32[]{:S(2)}, u32[]{:S(2)}) collective-permute-start(bf16[2,32,1024]{2,1,0:T(8,128)(2,1)S(1)} %get-tuple-element.73.refs_0_), channel_id=1, source_target_pairs={{0,4},{1,5},{2,6},{3,7},{4,0},{5,1},{6,2},{7,3},{8,12},{9,13},{10,... | collective-permute-start | bytes 393224 | tf_op jit(solution)/shard_map/ppermute | solution.py:348
  10.8 11.4 %collective-permute-start.4 = (bf16[2,32,1024]{2,1,0:T(8,128)(2,1)S(1)}, bf16[2,32,1024]{2,1,0:T(8,128)(2,1)S(1)}, u32[]{:S(2)}, u32[]{:S(2)}) collective-permute-start(bf16[2,32,1024]{2,1,0:T(8,128)(2,1)S(1)} %get-tuple-element.73.refs_0_), channel_id=1, source_target_pairs={{0,6},{1,7},{2,4},{3,5},{4,2},{5,3},{6,0},{7,1},{8,14},{9,15},{10,... | collective-permute-start | bytes 393224 | tf_op jit(solution)/shard_map/ppermute | solution.py:348
  11.0 12.9 %collective-permute-start.1 = (bf16[256,1024]{1,0:T(8,128)(2,1)}, bf16[256,1024]{1,0:T(8,128)(2,1)S(1)}, u32[]{:S(2)}, u32[]{:S(2)}) collective-permute-start(bf16[256,1024]{1,0:T(8,128)(2,1)} %bitcast.15), channel_id=1, source_target_pairs={{0,16},{1,9},{2,18},{3,11},{4,20},{5,13},{6,22},{7,15},{8,24},{9,1... | collective-permute-start | bytes 1572872 | tf_op jit(solution)/shard_map/ppermute | solution.py:343
  12.5 1.6 %copy-start = (bf16[1024,1024]{1,0:T(8,128)(2,1)S(1)}, bf16[1024,1024]{1,0:T(8,128)(2,1)}, u32[]{:S(2)}) copy-start(bf16[1024,1024]{1,0:T(8,128)(2,1)} %w_ref.3) | copy-start | bytes 6291460
  14.1 1.0 %copy-start.3 = (bf16[1,256,1024]{2,1,0:T(8,128)(2,1)S(1)}, bf16[1,256,1024]{2,1,0:T(8,128)(2,1)}, u32[]{:S(2)}) copy-start(bf16[1,256,1024]{2,1,0:T(8,128)(2,1)} %param.6) | copy-start | bytes 1572868
  15.1 1.0 %copy-start.6 = (bf16[1,256,1024]{2,1,0:T(8,128)(2,1)S(1)}, bf16[1,256,1024]{2,1,0:T(8,128)(2,1)}, u32[]{:S(2)}) copy-start(bf16[1,256,1024]{2,1,0:T(8,128)(2,1)} %param.7) | copy-start | bytes 1572868
  16.2 1.0 %copy-start.8 = (bf16[1,256,1024]{2,1,0:T(8,128)(2,1)S(1)}, bf16[1,256,1024]{2,1,0:T(8,128)(2,1)}, u32[]{:S(2)}) copy-start(bf16[1,256,1024]{2,1,0:T(8,128)(2,1)} %param.8) | copy-start | bytes 1572868
  17.2 1.0 %copy-start.10 = (bf16[1,256,1024]{2,1,0:T(8,128)(2,1)S(1)}, bf16[1,256,1024]{2,1,0:T(8,128)(2,1)}, u32[]{:S(2)}) copy-start(bf16[1,256,1024]{2,1,0:T(8,128)(2,1)} %param.5) | copy-start | bytes 1572868
  22.2 3.3 %collective-permute-start.5 = (bf16[2,128,1024]{2,1,0:T(8,128)(2,1)S(1)}, bf16[2,128,1024]{2,1,0:T(8,128)(2,1)S(1)}, u32[]{:S(2)}, u32[]{:S(2)}) collective-permute-start(bf16[2,128,1024]{2,1,0:T(8,128)(2,1)S(1)} %get-tuple-element.74.refs_0_), channel_id=1, source_target_pairs={{0,1},{1,0},{2,3},{3,2},{4,5},{5,4},{6,7},{7,6},{8,9},{9,8},{10,11... | collective-permute-start | bytes 1572872 | tf_op jit(solution)/shard_map/ppermute | solution.py:348
  22.2 9.4 %collective-permute-start.12 = (bf16[256,1024]{1,0:T(8,128)(2,1)S(1)}, bf16[256,1024]{1,0:T(8,128)(2,1)S(1)}, u32[]{:S(2)}, u32[]{:S(2)}) collective-permute-start(bf16[256,1024]{1,0:T(8,128)(2,1)S(1)} %collective-permute-done.refs_5_), channel_id=1, source_target_pairs={{0,16},{1,9},{2,18},{3,11},{4,20},{5,13},{6,22},{7,15},{8,24},{9,1... | collective-permute-start | bytes 1572872 | tf_op jit(solution)/shard_map/ppermute | solution.py:343
  22.7 2.7 %collective-permute-start.6 = (bf16[2,64,1024]{2,1,0:T(8,128)(2,1)S(1)}, bf16[2,64,1024]{2,1,0:T(8,128)(2,1)S(1)}, u32[]{:S(2)}, u32[]{:S(2)}) collective-permute-start(bf16[2,64,1024]{2,1,0:T(8,128)(2,1)S(1)} %collective-permute-done.2.refs_4_), channel_id=1, source_target_pairs={{0,1},{1,0},{2,3},{3,2},{4,5},{5,4},{6,7},{7,6},{8,9},{9,8},{10,11... | collective-permute-start | bytes 786440 | tf_op jit(solution)/shard_map/ppermute | solution.py:348
  23.9 1.3 %collective-permute-start.8 = (bf16[2,32,1024]{2,1,0:T(8,128)(2,1)S(1)}, bf16[2,32,1024]{2,1,0:T(8,128)(2,1)S(1)}, u32[]{:S(2)}, u32[]{:S(2)}) collective-permute-start(bf16[2,32,1024]{2,1,0:T(8,128)(2,1)S(1)} %collective-permute-done.4.refs_8_), channel_id=1, source_target_pairs={{0,1},{1,0},{2,3},{3,2},{4,5},{5,4},{6,7},{7,6},{8,9},{9,8},{10,11... | collective-permute-start | bytes 393224 | tf_op jit(solution)/shard_map/ppermute | solution.py:348
  23.9 1.5 %collective-permute-start.7 = (bf16[2,32,1024]{2,1,0:T(8,128)(2,1)S(1)}, bf16[2,32,1024]{2,1,0:T(8,128)(2,1)S(1)}, u32[]{:S(2)}, u32[]{:S(2)}) collective-permute-start(bf16[2,32,1024]{2,1,0:T(8,128)(2,1)S(1)} %collective-permute-done.3.refs_6_), channel_id=1, source_target_pairs={{0,1},{1,0},{2,3},{3,2},{4,5},{5,4},{6,7},{7,6},{8,9},{9,8},{10,11... | collective-permute-start | bytes 393224 | tf_op jit(solution)/shard_map/ppermute | solution.py:348
  25.4 11.3 %copy-start.9 = (bf16[1,256,1024]{2,1,0:T(8,128)(2,1)S(1)}, bf16[1,256,1024]{2,1,0:T(8,128)(2,1)}, u32[]{:S(2)}) copy-start(bf16[1,256,1024]{2,1,0:T(8,128)(2,1)} %param.8) | copy-start | bytes 1572868
  28.0 8.5 %collective-permute-start.10 = (bf16[256,256]{1,0:T(8,128)(2,1)S(1)}, bf16[256,256]{1,0:T(8,128)(2,1)S(1)}, u32[]{:S(2)}, u32[]{:S(2)}) collective-permute-start(bf16[256,256]{1,0:T(8,128)(2,1)S(1)} %get-tuple-element.82), channel_id=1, source_target_pairs={{0,16},{1,9},{2,18},{3,11},{4,20},{5,13},{6,22},{7,15},{8,24},{9,1... | collective-permute-start | bytes 393224 | tf_op jit(solution)/shard_map/ppermute | solution.py:343
  28.8 7.6 %collective-permute-start.11 = (bf16[256,256]{1,0:T(8,128)(2,1)S(1)}, bf16[256,256]{1,0:T(8,128)(2,1)S(1)}, u32[]{:S(2)}, u32[]{:S(2)}) collective-permute-start(bf16[256,256]{1,0:T(8,128)(2,1)S(1)} %get-tuple-element.83), channel_id=1, source_target_pairs={{0,24},{1,25},{2,26},{3,27},{4,28},{5,29},{6,30},{7,31},{8,16},{9,... | collective-permute-start | bytes 393224 | tf_op jit(solution)/shard_map/ppermute | solution.py:343
  30.4 6.3 %collective-permute-start.9 = (bf16[256,256]{1,0:T(8,128)(2,1)S(1)}, bf16[256,256]{1,0:T(8,128)(2,1)S(1)}, u32[]{:S(2)}, u32[]{:S(2)}) collective-permute-start(bf16[256,256]{1,0:T(8,128)(2,1)S(1)} %get-tuple-element.81), channel_id=1, source_target_pairs={{0,8},{1,17},{2,10},{3,19},{4,12},{5,21},{6,14},{7,23},{8,0},{9,25... | collective-permute-start | bytes 393224 | tf_op jit(solution)/shard_map/ppermute | solution.py:343
  31.6 11.2 %collective-permute-start.16 = (bf16[64,2176]{1,0:T(8,128)(2,1)S(1)}, bf16[64,2176]{1,0:T(8,128)(2,1)S(1)}, u32[]{:S(2)}, u32[]{:S(2)}) collective-permute-start(bf16[64,2176]{1,0:T(8,128)(2,1)S(1)} %get-tuple-element.90), channel_id=1, source_target_pairs={{0,2},{1,3},{2,0},{3,1},{4,6},{5,7},{6,4},{7,5},{8,10},{9,11},{10,... | collective-permute-start | bytes 835592 | tf_op jit(solution)/shard_map/ppermute | solution.py:348
  32.3 8.7 %collective-permute-start.19 = (bf16[32,2176]{1,0:T(8,128)(2,1)S(1)}, bf16[32,2176]{1,0:T(8,128)(2,1)S(1)}, u32[]{:S(2)}, u32[]{:S(2)}) collective-permute-start(bf16[32,2176]{1,0:T(8,128)(2,1)S(1)} %get-tuple-element.108), channel_id=1, source_target_pairs={{0,4},{1,5},{2,6},{3,7},{4,0},{5,1},{6,2},{7,3},{8,12},{9,13},{10,... | collective-permute-start | bytes 417800 | tf_op jit(solution)/shard_map/ppermute | solution.py:348
  36.7 7.7 %copy-start.4 = (bf16[1,256,1024]{2,1,0:T(8,128)(2,1)S(1)}, bf16[1,256,1024]{2,1,0:T(8,128)(2,1)}, u32[]{:S(2)}) copy-start(bf16[1,256,1024]{2,1,0:T(8,128)(2,1)} %param.6) | copy-start | bytes 1572868
  36.7 7.7 %copy-start.7 = (bf16[1,256,1024]{2,1,0:T(8,128)(2,1)S(1)}, bf16[1,256,1024]{2,1,0:T(8,128)(2,1)}, u32[]{:S(2)}) copy-start(bf16[1,256,1024]{2,1,0:T(8,128)(2,1)} %param.7) | copy-start | bytes 1572868
  36.7 7.7 %copy-start.11 = (bf16[1,256,1024]{2,1,0:T(8,128)(2,1)S(1)}, bf16[1,256,1024]{2,1,0:T(8,128)(2,1)}, u32[]{:S(2)}) copy-start(bf16[1,256,1024]{2,1,0:T(8,128)(2,1)} %param.5) | copy-start | bytes 1572868
  37.5 1.7 %collective-permute-start.13 = (bf16[2,32,1024]{2,1,0:T(8,128)(2,1)S(1)}, bf16[2,32,1024]{2,1,0:T(8,128)(2,1)S(1)}, u32[]{:S(2)}, u32[]{:S(2)}) collective-permute-start(bf16[2,32,1024]{2,1,0:T(8,128)(2,1)S(1)} %get-tuple-element.85), channel_id=1, source_target_pairs={{0,1},{1,0},{2,3},{3,2},{4,5},{5,4},{6,7},{7,6},{8,9},{9,8},{10,11... | collective-permute-start | bytes 393224 | tf_op jit(solution)/shard_map/ppermute | solution.py:348
  38.3 1.3 %collective-permute-start.14 = (bf16[2,32,1024]{2,1,0:T(8,128)(2,1)S(1)}, bf16[2,32,1024]{2,1,0:T(8,128)(2,1)S(1)}, u32[]{:S(2)}, u32[]{:S(2)}) collective-permute-start(bf16[2,32,1024]{2,1,0:T(8,128)(2,1)S(1)} %get-tuple-element.86), channel_id=1, source_target_pairs={{0,1},{1,0},{2,3},{3,2},{4,5},{5,4},{6,7},{7,6},{8,9},{9,8},{10,11... | collective-permute-start | bytes 393224 | tf_op jit(solution)/shard_map/ppermute | solution.py:348
  39.7 8.2 %collective-permute-start.18 = (bf16[2,32,1024]{2,1,0:T(8,128)(2,1)S(1)}, bf16[2,32,1024]{2,1,0:T(8,128)(2,1)S(1)}, u32[]{:S(2)}, u32[]{:S(2)}) collective-permute-start(bf16[2,32,1024]{2,1,0:T(8,128)(2,1)S(1)} %get-tuple-element.100), channel_id=1, source_target_pairs={{0,2},{1,3},{2,0},{3,1},{4,6},{5,7},{6,4},{7,5},{8,10},{9,11},{10,... | collective-permute-start | bytes 393224 | tf_op jit(solution)/shard_map/ppermute | solution.py:348
  40.4 9.8 %collective-permute-start.15 = (bf16[128,2176]{1,0:T(8,128)(2,1)S(1)}, bf16[128,2176]{1,0:T(8,128)(2,1)S(1)}, u32[]{:S(2)}, u32[]{:S(2)}) collective-permute-start(bf16[128,2176]{1,0:T(8,128)(2,1)S(1)} %get-tuple-element.88), channel_id=1, source_target_pairs={{0,1},{1,0},{2,3},{3,2},{4,5},{5,4},{6,7},{7,6},{8,9},{9,8},{10,11... | collective-permute-start | bytes 1671176 | tf_op jit(solution)/shard_map/ppermute | solution.py:348
  42.8 5.7 %collective-permute-start.21 = (bf16[32,2176]{1,0:T(8,128)(2,1)S(1)}, bf16[32,2176]{1,0:T(8,128)(2,1)S(1)}, u32[]{:S(2)}, u32[]{:S(2)}) collective-permute-start(bf16[32,2176]{1,0:T(8,128)(2,1)S(1)} %collective-permute-done.19.refs_1_), channel_id=1, source_target_pairs={{0,2},{1,3},{2,0},{3,1},{4,6},{5,7},{6,4},{7,5},{8,10},{9,11},{10,... | collective-permute-start | bytes 417800 | tf_op jit(solution)/shard_map/ppermute | solution.py:348
  44.5 5.7 %collective-permute-start.17 = (bf16[64,2176]{1,0:T(8,128)(2,1)S(1)}, bf16[64,2176]{1,0:T(8,128)(2,1)S(1)}, u32[]{:S(2)}, u32[]{:S(2)}) collective-permute-start(bf16[64,2176]{1,0:T(8,128)(2,1)S(1)} %collective-permute-done.16.refs_3_), channel_id=1, source_target_pairs={{0,1},{1,0},{2,3},{3,2},{4,5},{5,4},{6,7},{7,6},{8,9},{9,8},{10,11... | collective-permute-start | bytes 835592 | tf_op jit(solution)/shard_map/ppermute | solution.py:348
  47.9 3.8 %copy-start.1 = (bf16[1024,1024]{1,0:T(8,128)(2,1)S(1)}, bf16[1024,1024]{1,0:T(8,128)(2,1)}, u32[]{:S(2)}) copy-start(bf16[1024,1024]{1,0:T(8,128)(2,1)} %w_ref.3) | copy-start | bytes 6291460
  47.9 5.3 %collective-permute-start.20 = (bf16[32,2176]{1,0:T(8,128)(2,1)S(1)}, bf16[32,2176]{1,0:T(8,128)(2,1)S(1)}, u32[]{:S(2)}, u32[]{:S(2)}) collective-permute-start(bf16[32,2176]{1,0:T(8,128)(2,1)S(1)} %collective-permute-done.19.refs_1_), channel_id=1, source_target_pairs={{0,1},{1,0},{2,3},{3,2},{4,5},{5,4},{6,7},{7,6},{8,9},{9,8},{10,11... | collective-permute-start | bytes 417800 | tf_op jit(solution)/shard_map/ppermute | solution.py:348
  48.5 4.8 %collective-permute-start.22 = (bf16[32,2176]{1,0:T(8,128)(2,1)S(1)}, bf16[32,2176]{1,0:T(8,128)(2,1)S(1)}, u32[]{:S(2)}, u32[]{:S(2)}) collective-permute-start(bf16[32,2176]{1,0:T(8,128)(2,1)S(1)} %collective-permute-done.21.refs_3_), channel_id=1, source_target_pairs={{0,1},{1,0},{2,3},{3,2},{4,5},{5,4},{6,7},{7,6},{8,9},{9,8},{10,11... | collective-permute-start | bytes 417800 | tf_op jit(solution)/shard_map/ppermute | solution.py:348
  48.6 6.7 %collective-permute-start.23 = (bf16[1,32,1024]{2,1,0:T(8,128)(2,1)S(1)}, bf16[1,32,1024]{2,1,0:T(8,128)(2,1)S(1)}, u32[]{:S(2)}, u32[]{:S(2)}) collective-permute-start(bf16[1,32,1024]{2,1,0:T(8,128)(2,1)S(1)} %get-tuple-element.101), channel_id=1, source_target_pairs={{0,4},{1,5},{2,6},{3,7},{4,0},{5,1},{6,2},{7,3},{8,12},{9,13},{10,... | collective-permute-start | bytes 196616 | tf_op jit(solution)/shard_map/ppermute | solution.py:348

commit v3 on v2

--- a/solution.py
+++ b/solution.py
@@ -42,7 +42,7 @@
     return jnp.where(r == c, value, 0.0).astype(BF16)
 
 
-def call(kernel, outs, name, cost, *operands, scratch=(), space=pltpu.VMEM):
+def call(kernel, outs, name, cost, *operands, scratch=(), space=pltpu.VMEM, limit=VMEM_LIMIT):
     return pl.pallas_call(
         kernel,
         name=name,
@@ -50,27 +50,21 @@
         in_specs=[pl.BlockSpec(memory_space=space)] * len(operands),
         out_specs=[pl.BlockSpec(memory_space=pltpu.VMEM)] * len(outs),
         scratch_shapes=list(scratch),
-        compiler_params=pltpu.CompilerParams(vmem_limit_bytes=VMEM_LIMIT),
+        compiler_params=pltpu.CompilerParams(vmem_limit_bytes=limit),
         cost_estimate=pl.CostEstimate(flops=cost, bytes_accessed=1, transcendentals=0),
     )(*operands)
 
 
-def pool_kernel(levels, k_ref, v_ref, *refs):
-    outs, (held, sems) = refs[:-2], refs[-2:]
+def pool_kernel(levels, k_ref, v_ref, *outs):
     tokens, width = k_ref.shape
-    copies = [
-        pltpu.make_async_copy(src, held.at[i], sems.at[i]) for i, src in enumerate((k_ref, v_ref))
-    ]
-    for copy in copies:
-        copy.start()
     pools = [member(tokens >> l, tokens, 0, l, 0.5**l) for l in range(1, levels)]
-    for i, copy in enumerate(copies):
-        copy.wait()
+    for i, src in enumerate((k_ref, v_ref)):
+        x = src[...]
         for pool, out in zip(pools, outs):
-            out[i] = nn(pool, held[i]).astype(BF16)
-
-
-def early_kernel(levels, q_ref, k_ref, v_ref, g_ref, w_ref, *refs):
+            out[i] = nn(pool, x).astype(BF16)
+
+
+def early_kernel(levels, q_ref, k_ref, v_ref, g_ref, w_ref, kv_ref, *refs):
     qhat_ref, gat_ref, e_ref, o_ref, stat_ref = refs[:5]
     qls = refs[5:]
     tokens, width = q_ref.shape
@@ -78,39 +72,47 @@
     for l in range(1, levels):
         qhat_ref[l - 1] = nn(member(tokens, tokens, l, l, 0.5**l), q).astype(BF16)
         qls[l - 1][...] = nn(member(tokens >> l, tokens, 0, l, 0.5**l), q).astype(BF16)
-    ones = jnp.ones((16, tokens), BF16)
-
-    def attend(h, raw):
-        hs = slice(h * HEAD_DIM, (h + 1) * HEAD_DIM)
-        top = jnp.max(raw, axis=0, keepdims=True) * SCALE2
-        e = jnp.exp2(raw * SCALE2 - top).astype(BF16)
-        e_ref[h] = e
-        both = nn(jnp.concatenate([v_ref[:, hs].T, ones], axis=0), e)
+    ones = jnp.ones((16, tokens + BLOCK), BF16)
+
+    def attend(h, raw0, raw1):
+        hs = slice(h * HEAD_DIM, (h + 1) * HEAD_DIM)
+        top1 = jnp.max(raw1, axis=0, keepdims=True)
+        top = jnp.max(raw0, axis=0, keepdims=True) * SCALE2
+        top = jnp.maximum(top, top1 * SCALE2 + 1.0)
+        e0 = jnp.exp2(raw0 * SCALE2 - top).astype(BF16)
+        e1 = jnp.exp2(raw1 * SCALE2 + (1.0 - top)).astype(BF16)
+        e_ref[h, :tokens, :] = e0
+        e_ref[h, tokens:, :] = e1
+        vals = jnp.concatenate([v_ref[:, hs], kv_ref[1, :, hs]], axis=0)
+        both = nn(
+            jnp.concatenate([vals.T, ones], axis=0), jnp.concatenate([e0, e1], axis=0)
+        )
         o_ref[hs, :] = both[:HEAD_DIM]
         stat_ref[h : h + 1, :] = top
         stat_ref[HEADS + h : HEADS + h + 1, :] = both[HEAD_DIM : HEAD_DIM + 1]
+        stat_ref[2 * HEADS + h : 2 * HEADS + h + 1, :] = top1
 
     def scores(h):
         hs = slice(h * HEAD_DIM, (h + 1) * HEAD_DIM)
-        return nt(k_ref[:, hs], q_ref[:, hs])
+        return nt(k_ref[:, hs], q_ref[:, hs]), nt(kv_ref[0, :, hs], qhat_ref[0, :, hs])
 
     g = g_ref[...]
-    ahead = scores(0)
+    ahead = [scores(0), scores(1)]
     for h in range(HEADS):
-        raw = ahead
-        if h + 1 < HEADS:
-            ahead = scores(h + 1)
+        raws = ahead.pop(0)
+        if h + 2 < HEADS:
+            ahead.append(scores(h + 2))
         if h % 2 == 0:
             rows = slice(h * HEAD_DIM, (h + 2) * HEAD_DIM)
             gat_ref[rows, :] = nt(w_ref[rows, :], g).astype(BF16)
-        attend(h, raw)
-
-
-def gathered(levels, pieces, kvs, which, hs):
+        attend(h, *raws)
+
+
+def gathered(pieces, kvs, which, hs):
     out, at = [], 0
-    for l in range(1, levels):
-        part = kvs[at : at + pieces[l - 1]]
-        at += pieces[l - 1]
+    for count in pieces:
+        part = kvs[at : at + count]
+        at += count
         out.append(jnp.concatenate([p[which, :, hs] for p in part], axis=0))
     return out
 
@@ -123,26 +125,26 @@
     kvs, refs = refs[:count], refs[count:]
     e_ref, grt_ref, grt0_ref, dd_ref, att_ref = refs[:5]
     blocks, msgs, aux_ref = refs[5 : 5 + dp], refs[5 + dp : -1], refs[-1]
-    ones = jnp.ones((16, upper * BLOCK), BF16)
+    ones = jnp.ones((16, (upper - 1) * BLOCK), BF16)
     sums = [member(tokens >> l, tokens, 0, l, 1.0) for l in range(1, levels)]
     aux_ref[...] = jnp.zeros_like(aux_ref)
 
     def scores(h):
         hs = slice(h * HEAD_DIM, (h + 1) * HEAD_DIM)
-        keys = gathered(levels, pieces, kvs, 0, hs)
-        return [nt(keys[l - 1], qhat_ref[l - 1, :, hs]) for l in range(1, levels)]
+        keys = gathered(pieces, kvs, 0, hs)
+        return [nt(keys[l - 2], qhat_ref[l - 1, :, hs]) for l in range(2, levels)]
 
     def attend(h, raws):
         hs = slice(h * HEAD_DIM, (h + 1) * HEAD_DIM)
         tops = [jnp.max(raw, axis=0, keepdims=True) for raw in raws]
         top = stat_ref[h : h + 1, :]
-        for l in range(1, levels):
-            top = jnp.maximum(top, tops[l - 1] * SCALE2 + float(l))
+        for l in range(2, levels):
+            top = jnp.maximum(top, tops[l - 2] * SCALE2 + float(l))
         es = []
-        for l, raw in enumerate(raws, 1):
+        for l, raw in enumerate(raws, 2):
             es.append(jnp.exp2(raw * SCALE2 + (float(l) - top)).astype(BF16))
-            e_ref[h, (l - 1) * BLOCK : l * BLOCK, :] = es[-1]
-        vals = jnp.concatenate(gathered(levels, pieces, kvs, 1, hs), axis=0)
+            e_ref[h, (l - 2) * BLOCK : (l - 1) * BLOCK, :] = es[-1]
+        vals = jnp.concatenate(gathered(pieces, kvs, 1, hs), axis=0)
         lhs = jnp.concatenate([vals.T, ones], axis=0)
         return top, tops, nn(lhs, jnp.concatenate(es, axis=0))
 
@@ -159,6 +161,7 @@
         delta = jnp.sum(grt * att.astype(F32), axis=0, keepdims=True)
         dd_ref[h : h + 1, :] = delta
         dd_ref[HEADS + h : HEADS + h + 1, :] = delta * a0
+        tops = [stat_ref[2 * HEADS + h : 2 * HEADS + h + 1, :]] + tops
         for l in range(1, levels):
             mu = tops[l - 1].astype(BF16).astype(F32)
             a = jnp.exp2(mu * SCALE2 + (float(l) - top))
@@ -166,11 +169,11 @@
             aux_ref[l - 1, h : h + 1, :] = mu * 0.5**l
             aux_ref[l - 1, HEADS + h : HEADS + h + 1, :] = delta * a
 
-    ahead, behind = scores(0), None
+    ahead, behind = [scores(0), scores(1)], None
     for h in range(HEADS):
-        raws = ahead
-        if h + 1 < HEADS:
-            ahead = scores(h + 1)
+        raws = ahead.pop(0)
+        if h + 2 < HEADS:
+            ahead.append(scores(h + 2))
         state = attend(h, raws)
         if behind is not None:
             finish(h - 1, *behind)
@@ -187,33 +190,35 @@
 
 
 def backward_kernel(levels, pieces, e0_ref, e_ref, grt0_ref, grt_ref, dd_ref, *refs):
-    q_ref, k_ref, v_ref = refs[:3]
+    q_ref, k_ref, v_ref, kv_ref = refs[:4]
     tokens, width = q_ref.shape
-    kvs, (gq_ref, dk_ref, dv_ref, y_ref) = refs[3:-4], refs[-4:]
+    kvs, (gq_ref, dk_ref, dv_ref, y_ref) = refs[4:-4], refs[-4:]
 
     def probs(h):
         hs = slice(h * HEAD_DIM, (h + 1) * HEAD_DIM)
-        vals = jnp.concatenate(gathered(levels, pieces, kvs, 1, hs), axis=0)
-        return nn(v_ref[:, hs], grt0_ref[hs, :]), nn(vals, grt_ref[hs, :])
+        vals0 = jnp.concatenate([v_ref[:, hs], kv_ref[1, :, hs]], axis=0)
+        vals = jnp.concatenate(gathered(pieces, kvs, 1, hs), axis=0)
+        return nn(vals0, grt0_ref[hs, :]), nn(vals, grt_ref[hs, :])
 
     def rest(h, dpt0, dpt):
         hs = slice(h * HEAD_DIM, (h + 1) * HEAD_DIM)
         e0 = e0_ref[h]
         ds0 = (e0.astype(F32) * (dpt0 - dd_ref[HEADS + h : HEADS + h + 1, :])).astype(BF16)
         ds = (e_ref[h].astype(F32) * (dpt - dd_ref[h : h + 1, :])).astype(BF16)
-        keys = gathered(levels, pieces, kvs, 0, hs)
-        y_ref[hs, :tokens] = tn(k_ref[:, hs], ds0).astype(BF16)
-        for l in range(1, levels):
-            part = ds[(l - 1) * BLOCK : l * BLOCK]
-            y_ref[hs, l * tokens : (l + 1) * tokens] = tn(keys[l - 1], part).astype(BF16)
-        dv_ref[:, hs] = nt(e0, grt0_ref[hs, :]).astype(BF16)
-        dk_ref[:, hs] = (nn(ds0, q_ref[:, hs]) * SCALE).astype(BF16)
-
-    ahead = probs(0)
+        keys = gathered(pieces, kvs, 0, hs)
+        y_ref[hs, :tokens] = tn(k_ref[:, hs], ds0[:tokens]).astype(BF16)
+        y_ref[hs, tokens : 2 * tokens] = tn(kv_ref[0, :, hs], ds0[tokens:]).astype(BF16)
+        for l in range(2, levels):
+            part = ds[(l - 2) * BLOCK : (l - 1) * BLOCK]
+            y_ref[hs, l * tokens : (l + 1) * tokens] = tn(keys[l - 2], part).astype(BF16)
+        dv_ref[:, hs] = nt(e0[:tokens], grt0_ref[hs, :]).astype(BF16)
+        dk_ref[:, hs] = (nn(ds0[:tokens], q_ref[:, hs]) * SCALE).astype(BF16)
+
+    ahead = [probs(0), probs(1)]
     for h in range(HEADS):
-        now = ahead
-        if h + 1 < HEADS:
-            ahead = probs(h + 1)
+        now = ahead.pop(0)
+        if h + 2 < HEADS:
+            ahead.append(probs(h + 2))
         rest(h, *now)
     spread = jnp.concatenate(
         [member(tokens, tokens, l, l, 0.5**l) for l in range(levels)], axis=1
@@ -250,9 +255,10 @@
     def total(i):
         return keep_ref[i] + got[i % count][i // count].astype(F32)
 
-    for i in range(next_ref.shape[0]):
-        next_ref[i] = total(2 * i)
-        send_ref[i] = total(2 * i + 1).astype(BF16)
+    kept = next_ref.shape[0]
+    for i in range(kept):
+        next_ref[i] = total(i)
+        send_ref[i] = total(kept + i).astype(BF16)
 
 
 def mixed_kernel(att_ref, w_ref, out_ref):
@@ -308,7 +314,7 @@
             dks_ref[at : at + n, hs] = (nn(ds, q) * SCALE).astype(BF16)
             at += n
 
-    depth = 2 if len(chosen) > 1 else HEADS
+    depth = 4
     ahead = [products(h) for h in range(depth)]
     for h in range(HEADS):
         parts = ahead.pop(0)
@@ -362,11 +368,9 @@
         functools.partial(pool_kernel, levels),
         [((2, tokens >> l, width), BF16) for l in range(1, levels)],
         "pool",
-        1,
+        COST,
         k,
         v,
-        scratch=[pltpu.VMEM((2, tokens, width), BF16), pltpu.SemaphoreType.DMA((2,))],
-        space=pltpu.HBM,
     )
 
     def across(per_level):
@@ -375,23 +379,28 @@
         ]
 
     def joined(first, received, *wait):
-        got = [[swap(first, "seq", 1)]] + [[] for _ in range(upper - 1)]
+        got = [[first]] + [[] for _ in range(upper - 1)]
         for at, x in received:
             x = after(x, *wait)
             got[at] += [x, swap(x, "seq", 1)]
         axis = first.ndim - 2
         return [x if x[0].shape[axis] >= 16 else [jnp.concatenate(x, axis=axis)] for x in got]
 
-    received = across(own)
+    kv1 = swap(own[0], "seq", 1)
+    if nz == 4:
+        through = swap(own[2], "seq", 4)
+        received = [(1, swap(own[1], "seq", 2)), (2, through), (2, swap(through, "seq", 2))]
+    else:
+        received = across(own)
 
     early = call(
         functools.partial(early_kernel, levels),
         [
             ((upper, tokens, width), BF16),
             ((width, tokens), BF16),
-            ((HEADS, tokens, tokens), BF16),
+            ((HEADS, tokens + BLOCK, tokens), BF16),
             ((width, tokens), F32),
-            ((2 * HEADS, tokens), F32),
+            ((3 * HEADS, tokens), F32),
         ]
         + [((tokens >> l, width), BF16) for l in range(1, levels)],
         "early",
@@ -401,26 +410,26 @@
         v,
         g,
         w_out,
+        kv1,
     )
     qhat, gat, e0, o0, stats = early[:5]
     qls = early[5:]
 
-    g_late = after(g, own[0])
-    grads = [g] + [exchange_role(g_late, r) for r in range(1, min(dp, 3))]
+    grads = [g] + [exchange_role(g, r) for r in range(1, min(dp, 3))]
     if dp == 4:
         grads.append(exchange_role(grads[1], 2))
     else:
-        grads += [exchange_role(g_late, r) for r in range(3, dp)]
-
-    stats = after(stats, *grads[1:3])
+        grads += [exchange_role(g, r) for r in range(3, dp)]
+
+    stats = after(stats, grads[1])
     arrived = [x for _, x in received]
     arrived += [gat]
-    pairs = joined(after(own[0], *arrived), received, *arrived)
+    pairs = joined(kv1, received, *arrived)[1:]
     pieces = [len(x) for x in pairs]
     flat = [x for part in pairs for x in part]
 
     outs = [
-        ((HEADS, upper * BLOCK, tokens), BF16),
+        ((HEADS, (upper - 1) * BLOCK, tokens), BF16),
         ((width, tokens), BF16),
         ((width, tokens), BF16),
         ((2 * HEADS, tokens), F32),
@@ -454,11 +463,13 @@
 
     rows = width // dp
     own_rows = rows // (2 * nz)
+    mixed = call(mixed_kernel, [((tokens, width), BF16)], "mixed", COST, att, w_out)[0]
+    atts[0] = after(atts[0], mixed)
     keep, even, odd = call(
         functools.partial(weight_kernel, dp, nz),
         [((nz, own_rows, width), F32)] + [((nz // 2, own_rows, width), BF16)] * 2,
         "weight",
-        COST,
+        1,
         *atts,
         *grads,
         scratch=[pltpu.VMEM((rows, width), F32)],
@@ -470,9 +481,9 @@
         return call(functools.partial(halve_kernel, len(got)), outs, "halve", 1, keep, *got)
 
     keep, send = halve(keep, swap(even, "seq", 1), swap(odd, "seq", 1))
-    came = swap(send, "seq", 2)
+    came = swap(send, "seq", nz)
     if relayed:
-        relay = swap(after(far, keep, near), "seq", 2)
+        relay = swap(after(far, keep), "seq", 2)
         near = after(near, keep)
     grt = after(grt, keep)
 
@@ -489,13 +500,13 @@
         q,
         k,
         v,
+        kv1,
         *flat,
         scratch=[pltpu.VMEM((width, levels * tokens), BF16)],
     )
 
     def owned(chosen, messages, dk, dv, dtype):
         flat = [x for part in messages for x in part]
-        rows = sum(tokens >> l for l in chosen)
         return call(
             functools.partial(owner_kernel, chosen, [len(x) for x in messages], tokens),
             [((tokens, width), dtype)] * 2,
@@ -505,26 +516,25 @@
             *flat,
             dk,
             dv,
-            scratch=[pltpu.VMEM((rows, width), BF16)] * 2,
+            scratch=[pltpu.VMEM((sum(tokens >> l for l in chosen), width), BF16)] * 2,
         )
 
     last = levels - 1
     some = list(range(1, last))
-    step = 2
+    step = nz
     first = after(outgoing[0], keep)
     keep = after(keep, dk0)
     while keep.shape[0] > 1:
         keep, send = halve(keep, came)
-        step *= 2
+        step //= 2
         came = swap(send, "seq", step)
     if relayed:
         messages = [[swap(first, "seq", 1)], [near, swap(near, "seq", 1)]]
         far, relay = after(far, send), after(relay, send)
         messages.append([far, swap(far, "seq", 1), relay, swap(relay, "seq", 1)])
     else:
-        messages = joined(first, received, dk0, send)
+        messages = joined(swap(first, "seq", 1), received, dk0, send)
     gk, gv = owned(some, messages[:-1], after(dk0, send), dv0, F32)
-    mixed = call(mixed_kernel, [((tokens, width), BF16)], "mixed", 1, after(att, gk), w_out)[0]
     gk, gv = owned([last], messages[-1:], gk, gv, BF16)
 
     (gw,) = call(

time: 56.4 us -> 53.2 us (0.943)
  local copies, waits for them, and re-layouts: 7.85 us -> 2.1 us
  waiting for transfers between devices: 9.02 us -> 11.3 us
  starting transfers between devices: 22.7 us -> 23.6 us
    unnamed x24 -> x14, local copies, waits for them, and re-layouts: 7.85 us -> 2.1 us
    ppermute x18, waiting for transfers between devices: 6.41 us -> 10.2 us  [swap(): return lax.ppermute(x, axis, [(i, i ^ mask) for i in range(count)])]
    ppermute x6, waiting for transfers between devices: 2.61 us -> 1.02 us  [exchange_role(): return lax.ppermute(x, ('dp', 'seq'), pairs)]
    ppermute x18, starting transfers between devices: 14 us -> 14.9 us  [swap(): return lax.ppermute(x, axis, [(i, i ^ mask) for i in range(count)])]
  transfers between devices with their start and end apart: 24 -> 24, of which waited for: 10 -> 11; matrix products, arithmetic and copies ran while one was open for 0% -> 0% of each run, Pallas kernels for 25% -> 28%
where the time goes in v3:
time: 53.2 us; the launch traced here: 53 us
  starting transfers between devices  23.6 us (44%)
  Pallas kernels  15.3 us (29%)
  waiting for transfers between devices  11.3 us (21%)
  local copies, waits for them, and re-layouts  2.1 us (4%)
  between operations  0.75 us (1%)
    pallas_call x11, Pallas kernels, call(): pl.pallas_call(kernel, name=name, out_shape=[jax.ShapeDtypeStruct(s, t) f...  15.3 us
    ppermute x18, starting transfers between devices, swap(): return lax.ppermute(x, axis, [(i, i ^ mask) for i in range(count)])  14.9 us
    ppermute x18, waiting for transfers between devices, swap(): return lax.ppermute(x, axis, [(i, i ^ mask) for i in range(count)])  10.2 us
    ppermute x6, starting transfers between devices, exchange_role(): return lax.ppermute(x, ('dp', 'seq'), pairs)  8.64 us
    unnamed x14, local copies, waits for them, and re-layouts  2.1 us
  transfers between devices with their start and end apart: 24, of which 11 were waited for; matrix products, arithmetic and copies ran while one was open for 0% of the time, Pallas kernels for 28%

profile of v3, /device:TPU:0, one launch (start us, length us, event | category | flops | bytes accessed | tf_op | source)
XLA Modules:
  0.0 53.0 jit_solution(2065497550731689934)
XLA Ops:
  0.6 3.0 %collective-permute-start.1 = (bf16[256,1024]{1,0:T(8,128)(2,1)}, bf16[256,1024]{1,0:T(8,128)(2,1)S(1)}, u32[]{:S(2)}, u32[]{:S(2)}) collective-permute-start(bf16[256,1024]{1,0:T(8,128)(2,1)} %bitcast.8), channel_id=1, source_target_pairs={{0,8},{1,17},{2,10},{3,19},{4,12},{5,21},{6,14},{7,23},{8,0},{9,25... | collective-permute-start | bytes 1572872 | tf_op jit(solution)/shard_map/ppermute | solution.py:349
  3.6 1.0 %copy-done.3 = bf16[1,256,1024]{2,1,0:T(8,128)(2,1)S(1)} copy-done((bf16[1,256,1024]{2,1,0:T(8,128)(2,1)S(1)}, bf16[1,256,1024]{2,1,0:T(8,128)(2,1)}, u32[]{:S(2)}) %copy-start.3) | copy-done | bytes 524312
  4.7 1.0 %copy-done.5 = bf16[1,256,1024]{2,1,0:T(8,128)(2,1)S(1)} copy-done((bf16[1,256,1024]{2,1,0:T(8,128)(2,1)S(1)}, bf16[1,256,1024]{2,1,0:T(8,128)(2,1)}, u32[]{:S(2)}) %copy-start.5) | copy-done | bytes 524312
  5.7 0.6 %pool.1 = (bf16[2,128,1024]{2,1,0:T(8,128)(2,1)S(1)}, bf16[2,64,1024]{2,1,0:T(8,128)(2,1)S(1)}, bf16[2,32,1024]{2,1,0:T(8,128)(2,1)S(1)}) custom-call(bf16[256,1024]{1,0:T(8,128)(2,1)S(1)} %bitcast.14, bf16[256,1024]{1,0:T(8,128)(2,1)S(1)} %bitcast.17), custom_call_target="tpu_custom_call" | custom-call | flops 5000000000 | bytes 1 | tf_op jit(solution)/shard_map/pool/pallas_call | solution.py:46
  6.4 0.0 collective-permute-start
  6.4 2.7 %collective-permute-start.3 = (bf16[2,32,1024]{2,1,0:T(8,128)(2,1)S(1)}, bf16[2,32,1024]{2,1,0:T(8,128)(2,1)S(1)}, u32[]{:S(2)}, u32[]{:S(2)}) collective-permute-start(bf16[2,32,1024]{2,1,0:T(8,128)(2,1)S(1)} %get-tuple-element.70.refs_0_), channel_id=1, source_target_pairs={{0,4},{1,5},{2,6},{3,7},{4,0},{5,1},{6,2},{7,3},{8,12},{9,13},{10,... | collective-permute-start | bytes 393224 | tf_op jit(solution)/shard_map/ppermute | solution.py:354
  9.1 1.6 %collective-permute-start.2 = (bf16[2,64,1024]{2,1,0:T(8,128)(2,1)S(1)}, bf16[2,64,1024]{2,1,0:T(8,128)(2,1)S(1)}, u32[]{:S(2)}, u32[]{:S(2)}) collective-permute-start(bf16[2,64,1024]{2,1,0:T(8,128)(2,1)S(1)} %get-tuple-element.69.refs_1_), channel_id=1, source_target_pairs={{0,2},{1,3},{2,0},{3,1},{4,6},{5,7},{6,4},{7,5},{8,10},{9,11},{10,... | collective-permute-start | bytes 786440 | tf_op jit(solution)/shard_map/ppermute | solution.py:354
  10.7 0.4 collective-permute-done.1.refs_5_
  11.0 2.0 %collective-permute-start.12 = (bf16[256,1024]{1,0:T(8,128)(2,1)S(1)}, bf16[256,1024]{1,0:T(8,128)(2,1)S(1)}, u32[]{:S(2)}, u32[]{:S(2)}) collective-permute-start(bf16[256,1024]{1,0:T(8,128)(2,1)S(1)} %collective-permute-done.1.refs_5_), channel_id=1, source_target_pairs={{0,16},{1,9},{2,18},{3,11},{4,20},{5,13},{6,22},{7,15},{8,24},{9,1... | collective-permute-start | bytes 1572872 | tf_op jit(solution)/shard_map/ppermute | solution.py:349
  13.1 0.0 copy-done
  13.1 0.0 collective-permute-start.11
  13.1 3.1 %collective-permute-done.3.refs_5_.refs_6_ = bf16[2,32,1024]{2,1,0:T(8,128)(2,1)S(1)} collective-permute-done((bf16[2,32,1024]{2,1,0:T(8,128)(2,1)S(1)}, bf16[2,32,1024]{2,1,0:T(8,128)(2,1)S(1)}, u32[]{:S(2)}, u32[]{:S(2)}) %collective-permute-start.3) | collective-permute-done | bytes 131104 | tf_op jit(solution)/shard_map/ppermute | solution.py:354
  16.1 0.6 %collective-permute-start.4 = (bf16[2,32,1024]{2,1,0:T(8,128)(2,1)S(1)}, bf16[2,32,1024]{2,1,0:T(8,128)(2,1)S(1)}, u32[]{:S(2)}, u32[]{:S(2)}) collective-permute-start(bf16[2,32,1024]{2,1,0:T(8,128)(2,1)S(1)} %collective-permute-done.3.refs_5_.refs_6_), channel_id=1, source_target_pairs={{0,2},{1,3},{2,0},{3,1},{4,6},{5,7},{6,4},{7,5},{8,10},{9,11},{10,... | collective-permute-start | bytes 393224 | tf_op jit(solution)/shard_map/ppermute | solution.py:354
  16.8 0.0 collective-permute-done.kv_ref.refs_3_
  16.8 0.0 copy-done.1
  16.8 0.0 copy-done.2
  16.8 2.7 %early.1 = (bf16[3,256,1024]{2,1,0:T(8,128)(2,1)S(1)}, bf16[1024,256]{1,0:T(8,128)(2,1)S(1)}, bf16[8,384,256]{2,1,0:T(8,128)(2,1)S(1)}, f32[1024,256]{1,0:T(8,12...) custom-call(bf16[256,1024]{1,0:T(8,128)(2,1)S(1)} %bitcast.12, ...), custom_call_target="tpu_custom_call" | custom-call | flops 1 | bytes 1 | tf_op jit(solution)/shard_map/early/pallas_call | solution.py:46
  19.5 2.5 %collective-permute-done.4.refs_7_.refs_8_ = bf16[2,32,1024]{2,1,0:T(8,128)(2,1)S(1)} collective-permute-done((bf16[2,32,1024]{2,1,0:T(8,128)(2,1)S(1)}, bf16[2,32,1024]{2,1,0:T(8,128)(2,1)S(1)}, u32[]{:S(2)}, u32[]{:S(2)}) %collective-permute-start.4) | collective-permute-done | bytes 131104 | tf_op jit(solution)/shard_map/ppermute | solution.py:354
  22.0 0.0 collective-permute-done.2.refs_3_.refs_4_
  22.0 0.0 collective-permute-start.5
  22.0 0.5 collective-permute-start.7
  22.5 0.0 collective-permute-start.6
  22.5 1.2 %collective-permute-done.7.refs_8_.refs_9_ = bf16[2,32,1024]{2,1,0:T(8,128)(2,1)S(1)} collective-permute-done((bf16[2,32,1024]{2,1,0:T(8,128)(2,1)S(1)}, bf16[2,32,1024]{2,1,0:T(8,128)(2,1)S(1)}, u32[]{:S(2)}, u32[]{:S(2)}) %collective-permute-start.7) | collective-permute-done | bytes 131104 | tf_op jit(solution)/shard_map/ppermute | solution.py:354
  23.7 0.2 collective-permute-done.6.refs_6_.refs_7_
  23.9 0.0 collective-permute-done.5.refs_4_.refs_5_
  23.9 2.1 %forward.1 = (bf16[8,256,256]{2,1,0:T(8,128)(2,1)S(1)}, bf16[1024,256]{1,0:T(8,128)(2,1)S(1)}, bf16[1024,256]{1,0:T(8,128)(2,1)S(1)}, f32[16,256]{1,0:T(8,128)S(...) custom-call(bf16[3,256,1024]{2,1,0:T(8,128)(2,1)S(1)} %get-tuple-ele, ...), custom_call_target="tpu_custom_call" | custom-call | flops 1 | bytes 1 | tf_op jit(solution)/shard_map/forward/pallas_call | solution.py:46
  26.0 1.6 %collective-permute-start.10 = (bf16[256,256]{1,0:T(8,128)(2,1)S(1)}, bf16[256,256]{1,0:T(8,128)(2,1)S(1)}, u32[]{:S(2)}, u32[]{:S(2)}) collective-permute-start(bf16[256,256]{1,0:T(8,128)(2,1)S(1)} %get-tuple-element.83), channel_id=1, source_target_pairs={{0,24},{1,25},{2,26},{3,27},{4,28},{5,29},{6,30},{7,31},{8,16},{9,... | collective-permute-start | bytes 393224 | tf_op jit(solution)/shard_map/ppermute | solution.py:349
  27.5 1.5 %collective-permute-start.8 = (bf16[256,256]{1,0:T(8,128)(2,1)S(1)}, bf16[256,256]{1,0:T(8,128)(2,1)S(1)}, u32[]{:S(2)}, u32[]{:S(2)}) collective-permute-start(bf16[256,256]{1,0:T(8,128)(2,1)S(1)} %get-tuple-element.81), channel_id=1, source_target_pairs={{0,8},{1,17},{2,10},{3,19},{4,12},{5,21},{6,14},{7,23},{8,0},{9,25... | collective-permute-start | bytes 393224 | tf_op jit(solution)/shard_map/ppermute | solution.py:349
  29.0 0.5 collective-permute-start.9
  29.5 0.0 collective-permute-done.12.refs_7_
  29.5 1.4 %collective-permute-start.21 = (bf16[64,2176]{1,0:T(8,128)(2,1)S(1)}, bf16[64,2176]{1,0:T(8,128)(2,1)S(1)}, u32[]{:S(2)}, u32[]{:S(2)}) collective-permute-start(bf16[64,2176]{1,0:T(8,128)(2,1)S(1)} %get-tuple-element.103), channel_id=1, source_target_pairs={{0,2},{1,3},{2,0},{3,1},{4,6},{5,7},{6,4},{7,5},{8,10},{9,11},{10,... | collective-permute-start | bytes 835592 | tf_op jit(solution)/shard_map/ppermute | solution.py:354
  31.0 0.0 collective-permute-done.11.refs_6_
  31.0 2.2 %collective-permute-start.15 = (bf16[32,2176]{1,0:T(8,128)(2,1)S(1)}, bf16[32,2176]{1,0:T(8,128)(2,1)S(1)}, u32[]{:S(2)}, u32[]{:S(2)}) collective-permute-start(bf16[32,2176]{1,0:T(8,128)(2,1)S(1)} %get-tuple-element.92), channel_id=1, source_target_pairs={{0,4},{1,5},{2,6},{3,7},{4,0},{5,1},{6,2},{7,3},{8,12},{9,13},{10,... | collective-permute-start | bytes 417800 | tf_op jit(solution)/shard_map/ppermute | solution.py:354
  33.2 1.5 %mixed.1 = bf16[256,1024]{1,0:T(8,128)(2,1)} custom-call(bf16[1024,256]{1,0:T(8,128)(2,1)S(1)} %get-tuple-element.74.att_ref, bf16[1024,1024]{1,0:T(8,128)(2,1)S(1)} %copy-done.1), custom_call_target="tpu_custom_call" | custom-call | flops 5000000000 | bytes 1 | tf_op jit(solution)/shard_map/mixed/pallas_call | solution.py:46
  34.7 0.0 collective-permute-done.10.refs_3_
  34.7 0.7 %collective-permute-done.8.refs_1_ = bf16[256,256]{1,0:T(8,128)(2,1)S(1)} collective-permute-done((bf16[256,256]{1,0:T(8,128)(2,1)S(1)}, bf16[256,256]{1,0:T(8,128)(2,1)S(1)}, u32[]{:S(2)}, u32[]{:S(2)}) %collective-permute-start.8) | collective-permute-done | bytes 131104 | tf_op jit(solution)/shard_map/ppermute | solution.py:349
  35.4 0.0 collective-permute-done.9.refs_2_
  35.4 0.8 %weight.1 = (f32[4,32,1024]{2,1,0:T(8,128)S(1)}, bf16[2,32,1024]{2,1,0:T(8,128)(2,1)S(1)}, bf16[2,32,1024]{2,1,0:T(8,128)(2,1)S(1)}) custom-call(bf16[256,256]{1,0:T(8,128)(2,1)S(1)} %get-tuple-element.80.refs_0_, bf16[256,256]{1,0:T(8,128)(2,1)S(1)} %collective-permute-done.8.refs_1_, bf16[256,256]{1,0:T(8,128)(2,1)S(1)} %collective-permute-done.9.refs_2_, ...), custom_call_target="tpu_custom_call" | custom-call | flops 1 | bytes 1 | tf_op jit(solution)/shard_map/weight/pallas_call | solution.py:46
  36.2 0.1 collective-permute-start.13
  36.3 0.5 collective-permute-start.14
  36.8 0.8 %collective-permute-done.13.refs_0_ = bf16[2,32,1024]{2,1,0:T(8,128)(2,1)S(1)} collective-permute-done((bf16[2,32,1024]{2,1,0:T(8,128)(2,1)S(1)}, bf16[2,32,1024]{2,1,0:T(8,128)(2,1)S(1)}, u32[]{:S(2)}, u32[]{:S(2)}) %collective-permute-start.13) | collective-permute-done | bytes 131104 | tf_op jit(solution)/shard_map/ppermute | solution.py:354
  37.6 0.2 collective-permute-done.14.refs_1_
  37.9 2.0 %collective-permute-start.16 = (bf16[2,32,1024]{2,1,0:T(8,128)(2,1)S(1)}, bf16[2,32,1024]{2,1,0:T(8,128)(2,1)S(1)}, u32[]{:S(2)}, u32[]{:S(2)}) collective-permute-start(bf16[2,32,1024]{2,1,0:T(8,128)(2,1)S(1)} %get-tuple-element.95), channel_id=1, source_target_pairs={{0,4},{1,5},{2,6},{3,7},{4,0},{5,1},{6,2},{7,3},{8,12},{9,13},{10,... | collective-permute-start | bytes 393224 | tf_op jit(solution)/shard_map/ppermute | solution.py:354
  39.8 0.0 collective-permute-start.20
  39.9 0.0 collective-permute-done.15.refs_1_
  39.9 2.4 %collective-permute-start.18 = (bf16[32,2176]{1,0:T(8,128)(2,1)S(1)}, bf16[32,2176]{1,0:T(8,128)(2,1)S(1)}, u32[]{:S(2)}, u32[]{:S(2)}) collective-permute-start(bf16[32,2176]{1,0:T(8,128)(2,1)S(1)} %collective-permute-done.15.refs_1_), channel_id=1, source_target_pairs={{0,2},{1,3},{2,0},{3,1},{4,6},{5,7},{6,4},{7,5},{8,10},{9,11},{10,... | collective-permute-start | bytes 417800 | tf_op jit(solution)/shard_map/ppermute | solution.py:354
  42.3 0.0 collective-permute-done.21.refs_3_
  42.3 0.0 collective-permute-start.22
  42.3 0.0 copy-done.4
  42.3 0.0 copy-done.6
  42.3 3.4 %backward.1 = (bf16[256,1024]{1,0:T(8,128)(2,1)}, bf16[256,1024]{1,0:T(8,128)(2,1)S(1)}, bf16[256,1024]{1,0:T(8,128)(2,1)S(1)}) custom-call(bf16[8,384,256]{2,1,0:T(8,128)(2,1)S(1)} %get-tuple-element.75.e0_ref, bf16[8,256,256]{2,1,0:T(8,128)(2,1)S(1)} %get-tuple-element.76.e_ref, bf16[1024,256]{1,0:T(8,128)(2,1)S(1)} %get-tuple-element.77.grt0_ref, ...), custom_call_target="tpu_custom_call" | custom-call | flops 5000000000 | bytes 1 | tf_op jit(solution)/shard_map/backward/pallas_call | solution.py:46
  45.7 1.7 %collective-permute-done.16.refs_0_ = bf16[2,32,1024]{2,1,0:T(8,128)(2,1)S(1)} collective-permute-done((bf16[2,32,1024]{2,1,0:T(8,128)(2,1)S(1)}, bf16[2,32,1024]{2,1,0:T(8,128)(2,1)S(1)}, u32[]{:S(2)}, u32[]{:S(2)}) %collective-permute-start.16) | collective-permute-done | bytes 131104 | tf_op jit(solution)/shard_map/ppermute | solution.py:354
  47.5 0.1 collective-permute-start.17
  47.6 0.2 collective-permute-done.18.refs_3_
  47.8 0.3 collective-permute-start.19
  48.1 0.5 collective-permute-start.23
  48.6 0.0 collective-permute-done.22.refs_4_
  48.6 0.0 collective-permute-done.20.refs_2_
  48.6 1.5 %owner.2 = (f32[256,1024]{1,0:T(8,128)S(1)}, f32[256,1024]{1,0:T(8,128)S(1)}) custom-call(bf16[2,128,1024]{2,1,0:T(8,128)(2,1)S(1)} %get-tuple-element.59.refs_0_, bf16[2,64,1024]{2,1,0:T(8,128)(2,1)S(1)} %get-tuple-element.69.refs_1_, bf16[128,2176]{1,0:T(8,128)(2,1)S(1)} %collective-permute-done.20.refs_2_, ...), custom_call_target="tpu_custom_call" | custom-call | flops 1 | bytes 1 | tf_op jit(solution)/shard_map/owner/pallas_call | solution.py:46
  50.1 0.0 collective-permute-done.17.refs_2_
  50.1 0.0 collective-permute-done.19.refs_4_
  50.1 1.9 %owner.3 = (bf16[256,1024]{1,0:T(8,128)(2,1)}, bf16[256,1024]{1,0:T(8,128)(2,1)}) custom-call(bf16[2,32,1024]{2,1,0:T(8,128)(2,1)S(1)} %get-tuple-element.70.refs_0_, bf16[32,2176]{1,0:T(8,128)(2,1)S(1)} %collective-permute-done.15.refs_1_, bf16[32,2176]{1,0:T(8,128)(2,1)S(1)} %collective-permute-done.17.refs_2_, ...), custom_call_target="tpu_custom_call" | custom-call | flops 1 | bytes 1 | tf_op jit(solution)/shard_map/owner/pallas_call | solution.py:46
  52.0 0.3 collective-permute-done.23.got_ref
  52.3 0.7 %total.1 = f32[32,1024]{1,0:T(8,128)} custom-call(f32[1,32,1024]{2,1,0:T(8,128)S(1)} %get-tuple-element.112.keep_ref, bf16[1,32,1024]{2,1,0:T(8,128)(2,1)S(1)} %collective-permute-done.23.got_ref), custom_call_target="tpu_custom_call" | custom-call | flops 1 | bytes 1 | tf_op jit(solution)/shard_map/total/pallas_call | solution.py:46
  (9 shorter events, 0.1 us)
Async XLA Ops:
  0.6 10.4 %collective-permute-start.1 = (bf16[256,1024]{1,0:T(8,128)(2,1)}, bf16[256,1024]{1,0:T(8,128)(2,1)S(1)}, u32[]{:S(2)}, u32[]{:S(2)}) collective-permute-start(bf16[256,1024]{1,0:T(8,128)(2,1)} %bitcast.8), channel_id=1, source_target_pairs={{0,8},{1,17},{2,10},{3,19},{4,12},{5,21},{6,14},{7,23},{8,0},{9,25... | collective-permute-start | bytes 1572872 | tf_op jit(solution)/shard_map/ppermute | solution.py:349
  3.6 1.0 %copy-start.3 = (bf16[1,256,1024]{2,1,0:T(8,128)(2,1)S(1)}, bf16[1,256,1024]{2,1,0:T(8,128)(2,1)}, u32[]{:S(2)}) copy-start(bf16[1,256,1024]{2,1,0:T(8,128)(2,1)} %param.6) | copy-start | bytes 1572868
  4.7 1.0 %copy-start.5 = (bf16[1,256,1024]{2,1,0:T(8,128)(2,1)S(1)}, bf16[1,256,1024]{2,1,0:T(8,128)(2,1)}, u32[]{:S(2)}) copy-start(bf16[1,256,1024]{2,1,0:T(8,128)(2,1)} %param.7) | copy-start | bytes 1572868
  5.7 7.3 %copy-start = (bf16[1,256,1024]{2,1,0:T(8,128)(2,1)S(1)}, bf16[1,256,1024]{2,1,0:T(8,128)(2,1)}, u32[]{:S(2)}) copy-start(bf16[1,256,1024]{2,1,0:T(8,128)(2,1)} %param.8) | copy-start | bytes 1572868
  5.7 11.1 %copy-start.1 = (bf16[1024,1024]{1,0:T(8,128)(2,1)S(1)}, bf16[1024,1024]{1,0:T(8,128)(2,1)}, u32[]{:S(2)}) copy-start(bf16[1024,1024]{1,0:T(8,128)(2,1)} %w_ref.3) | copy-start | bytes 6291460
  5.7 11.1 %copy-start.2 = (bf16[1,256,1024]{2,1,0:T(8,128)(2,1)S(1)}, bf16[1,256,1024]{2,1,0:T(8,128)(2,1)}, u32[]{:S(2)}) copy-start(bf16[1,256,1024]{2,1,0:T(8,128)(2,1)} %param.5) | copy-start | bytes 1572868
  6.4 10.4 %collective-permute-start = (bf16[2,128,1024]{2,1,0:T(8,128)(2,1)S(1)}, bf16[2,128,1024]{2,1,0:T(8,128)(2,1)S(1)}, u32[]{:S(2)}, u32[]{:S(2)}) collective-permute-start(bf16[2,128,1024]{2,1,0:T(8,128)(2,1)S(1)} %get-tuple-element.59.refs_0_), channel_id=1, source_target_pairs={{0,1},{1,0},{2,3},{3,2},{4,5},{5,4},{6,7},{7,6},{8,9},{9,8},{10,11... | collective-permute-start | bytes 1572872 | tf_op jit(solution)/shard_map/ppermute | solution.py:354
  6.4 9.7 %collective-permute-start.3 = (bf16[2,32,1024]{2,1,0:T(8,128)(2,1)S(1)}, bf16[2,32,1024]{2,1,0:T(8,128)(2,1)S(1)}, u32[]{:S(2)}, u32[]{:S(2)}) collective-permute-start(bf16[2,32,1024]{2,1,0:T(8,128)(2,1)S(1)} %get-tuple-element.70.refs_0_), channel_id=1, source_target_pairs={{0,4},{1,5},{2,6},{3,7},{4,0},{5,1},{6,2},{7,3},{8,12},{9,13},{10,... | collective-permute-start | bytes 393224 | tf_op jit(solution)/shard_map/ppermute | solution.py:354
  9.1 12.9 %collective-permute-start.2 = (bf16[2,64,1024]{2,1,0:T(8,128)(2,1)S(1)}, bf16[2,64,1024]{2,1,0:T(8,128)(2,1)S(1)}, u32[]{:S(2)}, u32[]{:S(2)}) collective-permute-start(bf16[2,64,1024]{2,1,0:T(8,128)(2,1)S(1)} %get-tuple-element.69.refs_1_), channel_id=1, source_target_pairs={{0,2},{1,3},{2,0},{3,1},{4,6},{5,7},{6,4},{7,5},{8,10},{9,11},{10,... | collective-permute-start | bytes 786440 | tf_op jit(solution)/shard_map/ppermute | solution.py:354
  11.0 18.5 %collective-permute-start.12 = (bf16[256,1024]{1,0:T(8,128)(2,1)S(1)}, bf16[256,1024]{1,0:T(8,128)(2,1)S(1)}, u32[]{:S(2)}, u32[]{:S(2)}) collective-permute-start(bf16[256,1024]{1,0:T(8,128)(2,1)S(1)} %collective-permute-done.1.refs_5_), channel_id=1, source_target_pairs={{0,16},{1,9},{2,18},{3,11},{4,20},{5,13},{6,22},{7,15},{8,24},{9,1... | collective-permute-start | bytes 1572872 | tf_op jit(solution)/shard_map/ppermute | solution.py:349
  13.1 17.9 %collective-permute-start.11 = (bf16[256,1024]{1,0:T(8,128)(2,1)S(1)}, bf16[256,1024]{1,0:T(8,128)(2,1)S(1)}, u32[]{:S(2)}, u32[]{:S(2)}) collective-permute-start(bf16[256,1024]{1,0:T(8,128)(2,1)S(1)} %bitcast.9), channel_id=1, source_target_pairs={{0,16},{1,9},{2,18},{3,11},{4,20},{5,13},{6,22},{7,15},{8,24},{9,1... | collective-permute-start | bytes 1572872 | tf_op jit(solution)/shard_map/ppermute | solution.py:349
  16.1 5.8 %collective-permute-start.4 = (bf16[2,32,1024]{2,1,0:T(8,128)(2,1)S(1)}, bf16[2,32,1024]{2,1,0:T(8,128)(2,1)S(1)}, u32[]{:S(2)}, u32[]{:S(2)}) collective-permute-start(bf16[2,32,1024]{2,1,0:T(8,128)(2,1)S(1)} %collective-permute-done.3.refs_5_.refs_6_), channel_id=1, source_target_pairs={{0,2},{1,3},{2,0},{3,1},{4,6},{5,7},{6,4},{7,5},{8,10},{9,11},{10,... | collective-permute-start | bytes 393224 | tf_op jit(solution)/shard_map/ppermute | solution.py:354
  22.0 1.9 %collective-permute-start.5 = (bf16[2,64,1024]{2,1,0:T(8,128)(2,1)S(1)}, bf16[2,64,1024]{2,1,0:T(8,128)(2,1)S(1)}, u32[]{:S(2)}, u32[]{:S(2)}) collective-permute-start(bf16[2,64,1024]{2,1,0:T(8,128)(2,1)S(1)} %collective-permute-done.2.refs_3_.refs_4_), channel_id=1, source_target_pairs={{0,1},{1,0},{2,3},{3,2},{4,5},{5,4},{6,7},{7,6},{8,9},{9,8},{10,11... | collective-permute-start | bytes 786440 | tf_op jit(solution)/shard_map/ppermute | solution.py:354
  22.0 1.7 %collective-permute-start.7 = (bf16[2,32,1024]{2,1,0:T(8,128)(2,1)S(1)}, bf16[2,32,1024]{2,1,0:T(8,128)(2,1)S(1)}, u32[]{:S(2)}, u32[]{:S(2)}) collective-permute-start(bf16[2,32,1024]{2,1,0:T(8,128)(2,1)S(1)} %collective-permute-done.4.refs_7_.refs_8_), channel_id=1, source_target_pairs={{0,1},{1,0},{2,3},{3,2},{4,5},{5,4},{6,7},{7,6},{8,9},{9,8},{10,11... | collective-permute-start | bytes 393224 | tf_op jit(solution)/shard_map/ppermute | solution.py:354
  22.5 1.4 %collective-permute-start.6 = (bf16[2,32,1024]{2,1,0:T(8,128)(2,1)S(1)}, bf16[2,32,1024]{2,1,0:T(8,128)(2,1)S(1)}, u32[]{:S(2)}, u32[]{:S(2)}) collective-permute-start(bf16[2,32,1024]{2,1,0:T(8,128)(2,1)S(1)} %collective-permute-done.3.refs_5_.refs_6_), channel_id=1, source_target_pairs={{0,1},{1,0},{2,3},{3,2},{4,5},{5,4},{6,7},{7,6},{8,9},{9,8},{10,11... | collective-permute-start | bytes 393224 | tf_op jit(solution)/shard_map/ppermute | solution.py:354
  26.0 8.8 %collective-permute-start.10 = (bf16[256,256]{1,0:T(8,128)(2,1)S(1)}, bf16[256,256]{1,0:T(8,128)(2,1)S(1)}, u32[]{:S(2)}, u32[]{:S(2)}) collective-permute-start(bf16[256,256]{1,0:T(8,128)(2,1)S(1)} %get-tuple-element.83), channel_id=1, source_target_pairs={{0,24},{1,25},{2,26},{3,27},{4,28},{5,29},{6,30},{7,31},{8,16},{9,... | collective-permute-start | bytes 393224 | tf_op jit(solution)/shard_map/ppermute | solution.py:349
  27.5 7.9 %collective-permute-start.8 = (bf16[256,256]{1,0:T(8,128)(2,1)S(1)}, bf16[256,256]{1,0:T(8,128)(2,1)S(1)}, u32[]{:S(2)}, u32[]{:S(2)}) collective-permute-start(bf16[256,256]{1,0:T(8,128)(2,1)S(1)} %get-tuple-element.81), channel_id=1, source_target_pairs={{0,8},{1,17},{2,10},{3,19},{4,12},{5,21},{6,14},{7,23},{8,0},{9,25... | collective-permute-start | bytes 393224 | tf_op jit(solution)/shard_map/ppermute | solution.py:349
  29.0 6.4 %collective-permute-start.9 = (bf16[256,256]{1,0:T(8,128)(2,1)S(1)}, bf16[256,256]{1,0:T(8,128)(2,1)S(1)}, u32[]{:S(2)}, u32[]{:S(2)}) collective-permute-start(bf16[256,256]{1,0:T(8,128)(2,1)S(1)} %get-tuple-element.82), channel_id=1, source_target_pairs={{0,16},{1,9},{2,18},{3,11},{4,20},{5,13},{6,22},{7,15},{8,24},{9,1... | collective-permute-start | bytes 393224 | tf_op jit(solution)/shard_map/ppermute | solution.py:349
  29.5 12.8 %collective-permute-start.21 = (bf16[64,2176]{1,0:T(8,128)(2,1)S(1)}, bf16[64,2176]{1,0:T(8,128)(2,1)S(1)}, u32[]{:S(2)}, u32[]{:S(2)}) collective-permute-start(bf16[64,2176]{1,0:T(8,128)(2,1)S(1)} %get-tuple-element.103), channel_id=1, source_target_pairs={{0,2},{1,3},{2,0},{3,1},{4,6},{5,7},{6,4},{7,5},{8,10},{9,11},{10,... | collective-permute-start | bytes 835592 | tf_op jit(solution)/shard_map/ppermute | solution.py:354
  31.0 8.9 %collective-permute-start.15 = (bf16[32,2176]{1,0:T(8,128)(2,1)S(1)}, bf16[32,2176]{1,0:T(8,128)(2,1)S(1)}, u32[]{:S(2)}, u32[]{:S(2)}) collective-permute-start(bf16[32,2176]{1,0:T(8,128)(2,1)S(1)} %get-tuple-element.92), channel_id=1, source_target_pairs={{0,4},{1,5},{2,6},{3,7},{4,0},{5,1},{6,2},{7,3},{8,12},{9,13},{10,... | collective-permute-start | bytes 417800 | tf_op jit(solution)/shard_map/ppermute | solution.py:354
  34.7 7.6 %copy-start.4 = (bf16[1,256,1024]{2,1,0:T(8,128)(2,1)S(1)}, bf16[1,256,1024]{2,1,0:T(8,128)(2,1)}, u32[]{:S(2)}) copy-start(bf16[1,256,1024]{2,1,0:T(8,128)(2,1)} %param.6) | copy-start | bytes 1572868
  34.7 7.6 %copy-start.6 = (bf16[1,256,1024]{2,1,0:T(8,128)(2,1)S(1)}, bf16[1,256,1024]{2,1,0:T(8,128)(2,1)}, u32[]{:S(2)}) copy-start(bf16[1,256,1024]{2,1,0:T(8,128)(2,1)} %param.7) | copy-start | bytes 1572868
  36.2 1.4 %collective-permute-start.13 = (bf16[2,32,1024]{2,1,0:T(8,128)(2,1)S(1)}, bf16[2,32,1024]{2,1,0:T(8,128)(2,1)S(1)}, u32[]{:S(2)}, u32[]{:S(2)}) collective-permute-start(bf16[2,32,1024]{2,1,0:T(8,128)(2,1)S(1)} %get-tuple-element.85), channel_id=1, source_target_pairs={{0,1},{1,0},{2,3},{3,2},{4,5},{5,4},{6,7},{7,6},{8,9},{9,8},{10,11... | collective-permute-start | bytes 393224 | tf_op jit(solution)/shard_map/ppermute | solution.py:354
  36.3 1.5 %collective-permute-start.14 = (bf16[2,32,1024]{2,1,0:T(8,128)(2,1)S(1)}, bf16[2,32,1024]{2,1,0:T(8,128)(2,1)S(1)}, u32[]{:S(2)}, u32[]{:S(2)}) collective-permute-start(bf16[2,32,1024]{2,1,0:T(8,128)(2,1)S(1)} %get-tuple-element.86), channel_id=1, source_target_pairs={{0,1},{1,0},{2,3},{3,2},{4,5},{5,4},{6,7},{7,6},{8,9},{9,8},{10,11... | collective-permute-start | bytes 393224 | tf_op jit(solution)/shard_map/ppermute | solution.py:354
  37.9 9.6 %collective-permute-start.16 = (bf16[2,32,1024]{2,1,0:T(8,128)(2,1)S(1)}, bf16[2,32,1024]{2,1,0:T(8,128)(2,1)S(1)}, u32[]{:S(2)}, u32[]{:S(2)}) collective-permute-start(bf16[2,32,1024]{2,1,0:T(8,128)(2,1)S(1)} %get-tuple-element.95), channel_id=1, source_target_pairs={{0,4},{1,5},{2,6},{3,7},{4,0},{5,1},{6,2},{7,3},{8,12},{9,13},{10,... | collective-permute-start | bytes 393224 | tf_op jit(solution)/shard_map/ppermute | solution.py:354
  39.8 8.8 %collective-permute-start.20 = (bf16[128,2176]{1,0:T(8,128)(2,1)S(1)}, bf16[128,2176]{1,0:T(8,128)(2,1)S(1)}, u32[]{:S(2)}, u32[]{:S(2)}) collective-permute-start(bf16[128,2176]{1,0:T(8,128)(2,1)S(1)} %get-tuple-element.101), channel_id=1, source_target_pairs={{0,1},{1,0},{2,3},{3,2},{4,5},{5,4},{6,7},{7,6},{8,9},{9,8},{10,11... | collective-permute-start | bytes 1671176 | tf_op jit(solution)/shard_map/ppermute | solution.py:354
  39.9 7.9 %collective-permute-start.18 = (bf16[32,2176]{1,0:T(8,128)(2,1)S(1)}, bf16[32,2176]{1,0:T(8,128)(2,1)S(1)}, u32[]{:S(2)}, u32[]{:S(2)}) collective-permute-start(bf16[32,2176]{1,0:T(8,128)(2,1)S(1)} %collective-permute-done.15.refs_1_), channel_id=1, source_target_pairs={{0,2},{1,3},{2,0},{3,1},{4,6},{5,7},{6,4},{7,5},{8,10},{9,11},{10,... | collective-permute-start | bytes 417800 | tf_op jit(solution)/shard_map/ppermute | solution.py:354
  42.3 6.3 %collective-permute-start.22 = (bf16[64,2176]{1,0:T(8,128)(2,1)S(1)}, bf16[64,2176]{1,0:T(8,128)(2,1)S(1)}, u32[]{:S(2)}, u32[]{:S(2)}) collective-permute-start(bf16[64,2176]{1,0:T(8,128)(2,1)S(1)} %collective-permute-done.21.refs_3_), channel_id=1, source_target_pairs={{0,1},{1,0},{2,3},{3,2},{4,5},{5,4},{6,7},{7,6},{8,9},{9,8},{10,11... | collective-permute-start | bytes 835592 | tf_op jit(solution)/shard_map/ppermute | solution.py:354
  47.5 2.6 %collective-permute-start.17 = (bf16[32,2176]{1,0:T(8,128)(2,1)S(1)}, bf16[32,2176]{1,0:T(8,128)(2,1)S(1)}, u32[]{:S(2)}, u32[]{:S(2)}) collective-permute-start(bf16[32,2176]{1,0:T(8,128)(2,1)S(1)} %collective-permute-done.15.refs_1_), channel_id=1, source_target_pairs={{0,1},{1,0},{2,3},{3,2},{4,5},{5,4},{6,7},{7,6},{8,9},{9,8},{10,11... | collective-permute-start | bytes 417800 | tf_op jit(solution)/shard_map/ppermute | solution.py:354
  47.8 2.3 %collective-permute-start.19 = (bf16[32,2176]{1,0:T(8,128)(2,1)S(1)}, bf16[32,2176]{1,0:T(8,128)(2,1)S(1)}, u32[]{:S(2)}, u32[]{:S(2)}) collective-permute-start(bf16[32,2176]{1,0:T(8,128)(2,1)S(1)} %collective-permute-done.18.refs_3_), channel_id=1, source_target_pairs={{0,1},{1,0},{2,3},{3,2},{4,5},{5,4},{6,7},{7,6},{8,9},{9,8},{10,11... | collective-permute-start | bytes 417800 | tf_op jit(solution)/shard_map/ppermute | solution.py:354
  48.1 4.3 %collective-permute-start.23 = (bf16[1,32,1024]{2,1,0:T(8,128)(2,1)S(1)}, bf16[1,32,1024]{2,1,0:T(8,128)(2,1)S(1)}, u32[]{:S(2)}, u32[]{:S(2)}) collective-permute-start(bf16[1,32,1024]{2,1,0:T(8,128)(2,1)S(1)} %get-tuple-element.96), channel_id=1, source_target_pairs={{0,2},{1,3},{2,0},{3,1},{4,6},{5,7},{6,4},{7,5},{8,10},{9,11},{10,... | collective-permute-start | bytes 196616 | tf_op jit(solution)/shard_map/ppermute | solution.py:354

commit v4 on v3

--- a/solution.py
+++ b/solution.py
@@ -128,6 +128,7 @@
     ones = jnp.ones((16, (upper - 1) * BLOCK), BF16)
     sums = [member(tokens >> l, tokens, 0, l, 1.0) for l in range(1, levels)]
     aux_ref[...] = jnp.zeros_like(aux_ref)
+    waiting = {}
 
     def scores(h):
         hs = slice(h * HEAD_DIM, (h + 1) * HEAD_DIM)
@@ -165,15 +166,21 @@
         for l in range(1, levels):
             mu = tops[l - 1].astype(BF16).astype(F32)
             a = jnp.exp2(mu * SCALE2 + (float(l) - top))
-            msgs[l - 1][:, hs] = nt(sums[l - 1], (grt * a).astype(BF16)).astype(BF16)
+            weighted = (grt * a).astype(BF16)
+            if h % 2 == 0:
+                waiting[l] = weighted
+            else:
+                pair = jnp.concatenate([waiting[l], weighted], axis=0)
+                ps = slice((h - 1) * HEAD_DIM, (h + 1) * HEAD_DIM)
+                msgs[l - 1][:, ps] = nt(sums[l - 1], pair).astype(BF16)
             aux_ref[l - 1, h : h + 1, :] = mu * 0.5**l
             aux_ref[l - 1, HEADS + h : HEADS + h + 1, :] = delta * a
 
-    ahead, behind = [scores(0), scores(1)], None
+    ahead, behind = [scores(0), scores(1), scores(2)], None
     for h in range(HEADS):
         raws = ahead.pop(0)
-        if h + 2 < HEADS:
-            ahead.append(scores(h + 2))
+        if h + 3 < HEADS:
+            ahead.append(scores(h + 3))
         state = attend(h, raws)
         if behind is not None:
             finish(h - 1, *behind)
@@ -534,7 +541,7 @@
         messages.append([far, swap(far, "seq", 1), relay, swap(relay, "seq", 1)])
     else:
         messages = joined(swap(first, "seq", 1), received, dk0, send)
-    gk, gv = owned(some, messages[:-1], after(dk0, send), dv0, F32)
+    gk, gv = owned(some, messages[:-1], after(dk0, send), dv0, BF16)
     gk, gv = owned([last], messages[-1:], gk, gv, BF16)
 
     (gw,) = call(

time: 53.2 us -> 53.2 us (level)
  no operation moved by 1% of the time
where the time goes in v4:
time: 53.2 us; the launch traced here: 53 us
  starting transfers between devices  23.6 us (44%)
  Pallas kernels  15.3 us (29%)
  waiting for transfers between devices  11.2 us (21%)
  local copies, waits for them, and re-layouts  2.1 us (4%)
  between operations  0.75 us (1%)
    pallas_call x11, Pallas kernels, call(): pl.pallas_call(kernel, name=name, out_shape=[jax.ShapeDtypeStruct(s, t) f...  15.3 us
    ppermute x18, starting transfers between devices, swap(): return lax.ppermute(x, axis, [(i, i ^ mask) for i in range(count)])  15 us
    ppermute x18, waiting for transfers between devices, swap(): return lax.ppermute(x, axis, [(i, i ^ mask) for i in range(count)])  10.2 us
    ppermute x6, starting transfers between devices, exchange_role(): return lax.ppermute(x, ('dp', 'seq'), pairs)  8.62 us
    unnamed x14, local copies, waits for them, and re-layouts  2.1 us
  transfers between devices with their start and end apart: 24, of which 11 were waited for; matrix products, arithmetic and copies ran while one was open for 0% of the time, Pallas kernels for 28%

profile of v4, /device:TPU:0, one launch (start us, length us, event | category | flops | bytes accessed | tf_op | source)
XLA Modules:
  0.0 53.0 jit_solution(18391441535606281457)
XLA Ops:
  0.6 3.0 %collective-permute-start.1 = (bf16[256,1024]{1,0:T(8,128)(2,1)}, bf16[256,1024]{1,0:T(8,128)(2,1)S(1)}, u32[]{:S(2)}, u32[]{:S(2)}) collective-permute-start(bf16[256,1024]{1,0:T(8,128)(2,1)} %bitcast.8), channel_id=1, source_target_pairs={{0,8},{1,17},{2,10},{3,19},{4,12},{5,21},{6,14},{7,23},{8,0},{9,25... | collective-permute-start | bytes 1572872 | tf_op jit(solution)/shard_map/ppermute | solution.py:356
  3.6 1.0 %copy-done.3 = bf16[1,256,1024]{2,1,0:T(8,128)(2,1)S(1)} copy-done((bf16[1,256,1024]{2,1,0:T(8,128)(2,1)S(1)}, bf16[1,256,1024]{2,1,0:T(8,128)(2,1)}, u32[]{:S(2)}) %copy-start.3) | copy-done | bytes 524312
  4.7 1.0 %copy-done.5 = bf16[1,256,1024]{2,1,0:T(8,128)(2,1)S(1)} copy-done((bf16[1,256,1024]{2,1,0:T(8,128)(2,1)S(1)}, bf16[1,256,1024]{2,1,0:T(8,128)(2,1)}, u32[]{:S(2)}) %copy-start.5) | copy-done | bytes 524312
  5.7 0.6 %pool.1 = (bf16[2,128,1024]{2,1,0:T(8,128)(2,1)S(1)}, bf16[2,64,1024]{2,1,0:T(8,128)(2,1)S(1)}, bf16[2,32,1024]{2,1,0:T(8,128)(2,1)S(1)}) custom-call(bf16[256,1024]{1,0:T(8,128)(2,1)S(1)} %bitcast.14, bf16[256,1024]{1,0:T(8,128)(2,1)S(1)} %bitcast.17), custom_call_target="tpu_custom_call" | custom-call | flops 5000000000 | bytes 1 | tf_op jit(solution)/shard_map/pool/pallas_call | solution.py:46
  6.4 0.0 collective-permute-start
  6.4 2.7 %collective-permute-start.3 = (bf16[2,32,1024]{2,1,0:T(8,128)(2,1)S(1)}, bf16[2,32,1024]{2,1,0:T(8,128)(2,1)S(1)}, u32[]{:S(2)}, u32[]{:S(2)}) collective-permute-start(bf16[2,32,1024]{2,1,0:T(8,128)(2,1)S(1)} %get-tuple-element.70.refs_0_), channel_id=1, source_target_pairs={{0,4},{1,5},{2,6},{3,7},{4,0},{5,1},{6,2},{7,3},{8,12},{9,13},{10,... | collective-permute-start | bytes 393224 | tf_op jit(solution)/shard_map/ppermute | solution.py:361
  9.1 1.6 %collective-permute-start.2 = (bf16[2,64,1024]{2,1,0:T(8,128)(2,1)S(1)}, bf16[2,64,1024]{2,1,0:T(8,128)(2,1)S(1)}, u32[]{:S(2)}, u32[]{:S(2)}) collective-permute-start(bf16[2,64,1024]{2,1,0:T(8,128)(2,1)S(1)} %get-tuple-element.69.refs_1_), channel_id=1, source_target_pairs={{0,2},{1,3},{2,0},{3,1},{4,6},{5,7},{6,4},{7,5},{8,10},{9,11},{10,... | collective-permute-start | bytes 786440 | tf_op jit(solution)/shard_map/ppermute | solution.py:361
  10.7 0.4 collective-permute-done.1.refs_5_
  11.0 2.0 %collective-permute-start.12 = (bf16[256,1024]{1,0:T(8,128)(2,1)S(1)}, bf16[256,1024]{1,0:T(8,128)(2,1)S(1)}, u32[]{:S(2)}, u32[]{:S(2)}) collective-permute-start(bf16[256,1024]{1,0:T(8,128)(2,1)S(1)} %collective-permute-done.1.refs_5_), channel_id=1, source_target_pairs={{0,16},{1,9},{2,18},{3,11},{4,20},{5,13},{6,22},{7,15},{8,24},{9,1... | collective-permute-start | bytes 1572872 | tf_op jit(solution)/shard_map/ppermute | solution.py:356
  13.1 0.0 copy-done
  13.1 0.0 collective-permute-start.11
  13.1 3.1 %collective-permute-done.3.refs_5_.refs_6_ = bf16[2,32,1024]{2,1,0:T(8,128)(2,1)S(1)} collective-permute-done((bf16[2,32,1024]{2,1,0:T(8,128)(2,1)S(1)}, bf16[2,32,1024]{2,1,0:T(8,128)(2,1)S(1)}, u32[]{:S(2)}, u32[]{:S(2)}) %collective-permute-start.3) | collective-permute-done | bytes 131104 | tf_op jit(solution)/shard_map/ppermute | solution.py:361
  16.1 0.6 %collective-permute-start.4 = (bf16[2,32,1024]{2,1,0:T(8,128)(2,1)S(1)}, bf16[2,32,1024]{2,1,0:T(8,128)(2,1)S(1)}, u32[]{:S(2)}, u32[]{:S(2)}) collective-permute-start(bf16[2,32,1024]{2,1,0:T(8,128)(2,1)S(1)} %collective-permute-done.3.refs_5_.refs_6_), channel_id=1, source_target_pairs={{0,2},{1,3},{2,0},{3,1},{4,6},{5,7},{6,4},{7,5},{8,10},{9,11},{10,... | collective-permute-start | bytes 393224 | tf_op jit(solution)/shard_map/ppermute | solution.py:361
  16.8 0.0 collective-permute-done.kv_ref.refs_3_
  16.8 0.0 copy-done.1
  16.8 0.0 copy-done.2
  16.8 2.7 %early.1 = (bf16[3,256,1024]{2,1,0:T(8,128)(2,1)S(1)}, bf16[1024,256]{1,0:T(8,128)(2,1)S(1)}, bf16[8,384,256]{2,1,0:T(8,128)(2,1)S(1)}, f32[1024,256]{1,0:T(8,12...) custom-call(bf16[256,1024]{1,0:T(8,128)(2,1)S(1)} %bitcast.12, ...), custom_call_target="tpu_custom_call" | custom-call | flops 1 | bytes 1 | tf_op jit(solution)/shard_map/early/pallas_call | solution.py:46
  19.5 2.5 %collective-permute-done.4.refs_7_.refs_8_ = bf16[2,32,1024]{2,1,0:T(8,128)(2,1)S(1)} collective-permute-done((bf16[2,32,1024]{2,1,0:T(8,128)(2,1)S(1)}, bf16[2,32,1024]{2,1,0:T(8,128)(2,1)S(1)}, u32[]{:S(2)}, u32[]{:S(2)}) %collective-permute-start.4) | collective-permute-done | bytes 131104 | tf_op jit(solution)/shard_map/ppermute | solution.py:361
  22.0 0.0 collective-permute-done.2.refs_3_.refs_4_
  22.0 0.0 collective-permute-start.5
  22.0 0.5 collective-permute-start.7
  22.5 0.0 collective-permute-start.6
  22.5 1.2 %collective-permute-done.7.refs_8_.refs_9_ = bf16[2,32,1024]{2,1,0:T(8,128)(2,1)S(1)} collective-permute-done((bf16[2,32,1024]{2,1,0:T(8,128)(2,1)S(1)}, bf16[2,32,1024]{2,1,0:T(8,128)(2,1)S(1)}, u32[]{:S(2)}, u32[]{:S(2)}) %collective-permute-start.7) | collective-permute-done | bytes 131104 | tf_op jit(solution)/shard_map/ppermute | solution.py:361
  23.7 0.2 collective-permute-done.6.refs_6_.refs_7_
  23.9 0.0 collective-permute-done.5.refs_4_.refs_5_
  23.9 2.1 %forward.1 = (bf16[8,256,256]{2,1,0:T(8,128)(2,1)S(1)}, bf16[1024,256]{1,0:T(8,128)(2,1)S(1)}, bf16[1024,256]{1,0:T(8,128)(2,1)S(1)}, f32[16,256]{1,0:T(8,128)S(...) custom-call(bf16[3,256,1024]{2,1,0:T(8,128)(2,1)S(1)} %get-tuple-ele, ...), custom_call_target="tpu_custom_call" | custom-call | flops 1 | bytes 1 | tf_op jit(solution)/shard_map/forward/pallas_call | solution.py:46
  26.0 1.5 %collective-permute-start.10 = (bf16[256,256]{1,0:T(8,128)(2,1)S(1)}, bf16[256,256]{1,0:T(8,128)(2,1)S(1)}, u32[]{:S(2)}, u32[]{:S(2)}) collective-permute-start(bf16[256,256]{1,0:T(8,128)(2,1)S(1)} %get-tuple-element.83), channel_id=1, source_target_pairs={{0,24},{1,25},{2,26},{3,27},{4,28},{5,29},{6,30},{7,31},{8,16},{9,... | collective-permute-start | bytes 393224 | tf_op jit(solution)/shard_map/ppermute | solution.py:356
  27.5 1.5 %collective-permute-start.8 = (bf16[256,256]{1,0:T(8,128)(2,1)S(1)}, bf16[256,256]{1,0:T(8,128)(2,1)S(1)}, u32[]{:S(2)}, u32[]{:S(2)}) collective-permute-start(bf16[256,256]{1,0:T(8,128)(2,1)S(1)} %get-tuple-element.81), channel_id=1, source_target_pairs={{0,8},{1,17},{2,10},{3,19},{4,12},{5,21},{6,14},{7,23},{8,0},{9,25... | collective-permute-start | bytes 393224 | tf_op jit(solution)/shard_map/ppermute | solution.py:356
  29.0 0.5 collective-permute-start.9
  29.5 0.0 collective-permute-done.12.refs_7_
  29.5 1.4 %collective-permute-start.21 = (bf16[64,2176]{1,0:T(8,128)(2,1)S(1)}, bf16[64,2176]{1,0:T(8,128)(2,1)S(1)}, u32[]{:S(2)}, u32[]{:S(2)}) collective-permute-start(bf16[64,2176]{1,0:T(8,128)(2,1)S(1)} %get-tuple-element.103), channel_id=1, source_target_pairs={{0,2},{1,3},{2,0},{3,1},{4,6},{5,7},{6,4},{7,5},{8,10},{9,11},{10,... | collective-permute-start | bytes 835592 | tf_op jit(solution)/shard_map/ppermute | solution.py:361
  31.0 0.0 collective-permute-done.11.refs_6_
  31.0 2.2 %collective-permute-start.15 = (bf16[32,2176]{1,0:T(8,128)(2,1)S(1)}, bf16[32,2176]{1,0:T(8,128)(2,1)S(1)}, u32[]{:S(2)}, u32[]{:S(2)}) collective-permute-start(bf16[32,2176]{1,0:T(8,128)(2,1)S(1)} %get-tuple-element.92), channel_id=1, source_target_pairs={{0,4},{1,5},{2,6},{3,7},{4,0},{5,1},{6,2},{7,3},{8,12},{9,13},{10,... | collective-permute-start | bytes 417800 | tf_op jit(solution)/shard_map/ppermute | solution.py:361
  33.2 1.6 %mixed.1 = bf16[256,1024]{1,0:T(8,128)(2,1)} custom-call(bf16[1024,256]{1,0:T(8,128)(2,1)S(1)} %get-tuple-element.74.att_ref, bf16[1024,1024]{1,0:T(8,128)(2,1)S(1)} %copy-done.1), custom_call_target="tpu_custom_call" | custom-call | flops 5000000000 | bytes 1 | tf_op jit(solution)/shard_map/mixed/pallas_call | solution.py:46
  34.7 0.0 collective-permute-done.10.refs_3_
  34.7 0.6 %collective-permute-done.8.refs_1_ = bf16[256,256]{1,0:T(8,128)(2,1)S(1)} collective-permute-done((bf16[256,256]{1,0:T(8,128)(2,1)S(1)}, bf16[256,256]{1,0:T(8,128)(2,1)S(1)}, u32[]{:S(2)}, u32[]{:S(2)}) %collective-permute-start.8) | collective-permute-done | bytes 131104 | tf_op jit(solution)/shard_map/ppermute | solution.py:356
  35.4 0.0 collective-permute-done.9.refs_2_
  35.4 0.8 %weight.1 = (f32[4,32,1024]{2,1,0:T(8,128)S(1)}, bf16[2,32,1024]{2,1,0:T(8,128)(2,1)S(1)}, bf16[2,32,1024]{2,1,0:T(8,128)(2,1)S(1)}) custom-call(bf16[256,256]{1,0:T(8,128)(2,1)S(1)} %get-tuple-element.80.refs_0_, bf16[256,256]{1,0:T(8,128)(2,1)S(1)} %collective-permute-done.8.refs_1_, bf16[256,256]{1,0:T(8,128)(2,1)S(1)} %collective-permute-done.9.refs_2_, ...), custom_call_target="tpu_custom_call" | custom-call | flops 1 | bytes 1 | tf_op jit(solution)/shard_map/weight/pallas_call | solution.py:46
  36.2 0.1 collective-permute-start.13
  36.2 0.5 collective-permute-start.14
  36.7 0.8 %collective-permute-done.13.refs_0_ = bf16[2,32,1024]{2,1,0:T(8,128)(2,1)S(1)} collective-permute-done((bf16[2,32,1024]{2,1,0:T(8,128)(2,1)S(1)}, bf16[2,32,1024]{2,1,0:T(8,128)(2,1)S(1)}, u32[]{:S(2)}, u32[]{:S(2)}) %collective-permute-start.13) | collective-permute-done | bytes 131104 | tf_op jit(solution)/shard_map/ppermute | solution.py:361
  37.6 0.2 collective-permute-done.14.refs_1_
  37.8 0.1 halve.2
  37.8 2.0 %collective-permute-start.16 = (bf16[2,32,1024]{2,1,0:T(8,128)(2,1)S(1)}, bf16[2,32,1024]{2,1,0:T(8,128)(2,1)S(1)}, u32[]{:S(2)}, u32[]{:S(2)}) collective-permute-start(bf16[2,32,1024]{2,1,0:T(8,128)(2,1)S(1)} %get-tuple-element.95), channel_id=1, source_target_pairs={{0,4},{1,5},{2,6},{3,7},{4,0},{5,1},{6,2},{7,3},{8,12},{9,13},{10,... | collective-permute-start | bytes 393224 | tf_op jit(solution)/shard_map/ppermute | solution.py:361
  39.8 0.0 collective-permute-start.20
  39.8 0.0 collective-permute-done.15.refs_1_
  39.8 2.4 %collective-permute-start.18 = (bf16[32,2176]{1,0:T(8,128)(2,1)S(1)}, bf16[32,2176]{1,0:T(8,128)(2,1)S(1)}, u32[]{:S(2)}, u32[]{:S(2)}) collective-permute-start(bf16[32,2176]{1,0:T(8,128)(2,1)S(1)} %collective-permute-done.15.refs_1_), channel_id=1, source_target_pairs={{0,2},{1,3},{2,0},{3,1},{4,6},{5,7},{6,4},{7,5},{8,10},{9,11},{10,... | collective-permute-start | bytes 417800 | tf_op jit(solution)/shard_map/ppermute | solution.py:361
  42.3 0.0 collective-permute-done.21.refs_3_
  42.3 0.0 collective-permute-start.22
  42.3 0.0 copy-done.4
  42.3 3.4 %backward.1 = (bf16[256,1024]{1,0:T(8,128)(2,1)}, bf16[256,1024]{1,0:T(8,128)(2,1)S(1)}, bf16[256,1024]{1,0:T(8,128)(2,1)S(1)}) custom-call(bf16[8,384,256]{2,1,0:T(8,128)(2,1)S(1)} %get-tuple-element.75.e0_ref, bf16[8,256,256]{2,1,0:T(8,128)(2,1)S(1)} %get-tuple-element.76.e_ref, bf16[1024,256]{1,0:T(8,128)(2,1)S(1)} %get-tuple-element.77.grt0_ref, ...), custom_call_target="tpu_custom_call" | custom-call | flops 5000000000 | bytes 1 | tf_op jit(solution)/shard_map/backward/pallas_call | solution.py:46
  45.7 1.7 %collective-permute-done.16.refs_0_ = bf16[2,32,1024]{2,1,0:T(8,128)(2,1)S(1)} collective-permute-done((bf16[2,32,1024]{2,1,0:T(8,128)(2,1)S(1)}, bf16[2,32,1024]{2,1,0:T(8,128)(2,1)S(1)}, u32[]{:S(2)}, u32[]{:S(2)}) %collective-permute-start.16) | collective-permute-done | bytes 131104 | tf_op jit(solution)/shard_map/ppermute | solution.py:361
  47.5 0.1 collective-permute-start.17
  47.5 0.2 collective-permute-done.18.refs_3_
  47.7 0.3 collective-permute-start.19
  48.0 0.5 collective-permute-start.23
  48.6 0.0 collective-permute-done.22.refs_4_
  48.6 0.0 collective-permute-done.20.refs_2_
  48.6 1.5 %owner.2 = (bf16[256,1024]{1,0:T(8,128)(2,1)S(1)}, bf16[256,1024]{1,0:T(8,128)(2,1)S(1)}) custom-call(bf16[2,128,1024]{2,1,0:T(8,128)(2,1)S(1)} %get-tuple-element.59.refs_0_, bf16[2,64,1024]{2,1,0:T(8,128)(2,1)S(1)} %get-tuple-element.69.refs_1_, bf16[128,2176]{1,0:T(8,128)(2,1)S(1)} %collective-permute-done.20.refs_2_, ...), custom_call_target="tpu_custom_call" | custom-call | flops 1 | bytes 1 | tf_op jit(solution)/shard_map/owner/pallas_call | solution.py:46
  50.0 0.0 collective-permute-done.17.refs_2_
  50.1 0.0 collective-permute-done.19.refs_4_
  50.1 1.9 %owner.3 = (bf16[256,1024]{1,0:T(8,128)(2,1)}, bf16[256,1024]{1,0:T(8,128)(2,1)}) custom-call(bf16[2,32,1024]{2,1,0:T(8,128)(2,1)S(1)} %get-tuple-element.70.refs_0_, bf16[32,2176]{1,0:T(8,128)(2,1)S(1)} %collective-permute-done.15.refs_1_, bf16[32,2176]{1,0:T(8,128)(2,1)S(1)} %collective-permute-done.17.refs_2_, ...), custom_call_target="tpu_custom_call" | custom-call | flops 1 | bytes 1 | tf_op jit(solution)/shard_map/owner/pallas_call | solution.py:46
  52.0 0.3 collective-permute-done.23.got_ref
  52.3 0.7 %total.1 = f32[32,1024]{1,0:T(8,128)} custom-call(f32[1,32,1024]{2,1,0:T(8,128)S(1)} %get-tuple-element.112.keep_ref, bf16[1,32,1024]{2,1,0:T(8,128)(2,1)S(1)} %collective-permute-done.23.got_ref), custom_call_target="tpu_custom_call" | custom-call | flops 1 | bytes 1 | tf_op jit(solution)/shard_map/total/pallas_call | solution.py:46
  (9 shorter events, 0.0 us)
Async XLA Ops:
  0.6 10.4 %collective-permute-start.1 = (bf16[256,1024]{1,0:T(8,128)(2,1)}, bf16[256,1024]{1,0:T(8,128)(2,1)S(1)}, u32[]{:S(2)}, u32[]{:S(2)}) collective-permute-start(bf16[256,1024]{1,0:T(8,128)(2,1)} %bitcast.8), channel_id=1, source_target_pairs={{0,8},{1,17},{2,10},{3,19},{4,12},{5,21},{6,14},{7,23},{8,0},{9,25... | collective-permute-start | bytes 1572872 | tf_op jit(solution)/shard_map/ppermute | solution.py:356
  3.6 1.0 %copy-start.3 = (bf16[1,256,1024]{2,1,0:T(8,128)(2,1)S(1)}, bf16[1,256,1024]{2,1,0:T(8,128)(2,1)}, u32[]{:S(2)}) copy-start(bf16[1,256,1024]{2,1,0:T(8,128)(2,1)} %param.6) | copy-start | bytes 1572868
  4.7 1.0 %copy-start.5 = (bf16[1,256,1024]{2,1,0:T(8,128)(2,1)S(1)}, bf16[1,256,1024]{2,1,0:T(8,128)(2,1)}, u32[]{:S(2)}) copy-start(bf16[1,256,1024]{2,1,0:T(8,128)(2,1)} %param.7) | copy-start | bytes 1572868
  5.7 7.3 %copy-start = (bf16[1,256,1024]{2,1,0:T(8,128)(2,1)S(1)}, bf16[1,256,1024]{2,1,0:T(8,128)(2,1)}, u32[]{:S(2)}) copy-start(bf16[1,256,1024]{2,1,0:T(8,128)(2,1)} %param.8) | copy-start | bytes 1572868
  5.7 11.1 %copy-start.1 = (bf16[1024,1024]{1,0:T(8,128)(2,1)S(1)}, bf16[1024,1024]{1,0:T(8,128)(2,1)}, u32[]{:S(2)}) copy-start(bf16[1024,1024]{1,0:T(8,128)(2,1)} %w_ref.3) | copy-start | bytes 6291460
  5.7 11.1 %copy-start.2 = (bf16[1,256,1024]{2,1,0:T(8,128)(2,1)S(1)}, bf16[1,256,1024]{2,1,0:T(8,128)(2,1)}, u32[]{:S(2)}) copy-start(bf16[1,256,1024]{2,1,0:T(8,128)(2,1)} %param.5) | copy-start | bytes 1572868
  6.4 10.4 %collective-permute-start = (bf16[2,128,1024]{2,1,0:T(8,128)(2,1)S(1)}, bf16[2,128,1024]{2,1,0:T(8,128)(2,1)S(1)}, u32[]{:S(2)}, u32[]{:S(2)}) collective-permute-start(bf16[2,128,1024]{2,1,0:T(8,128)(2,1)S(1)} %get-tuple-element.59.refs_0_), channel_id=1, source_target_pairs={{0,1},{1,0},{2,3},{3,2},{4,5},{5,4},{6,7},{7,6},{8,9},{9,8},{10,11... | collective-permute-start | bytes 1572872 | tf_op jit(solution)/shard_map/ppermute | solution.py:361
  6.4 9.7 %collective-permute-start.3 = (bf16[2,32,1024]{2,1,0:T(8,128)(2,1)S(1)}, bf16[2,32,1024]{2,1,0:T(8,128)(2,1)S(1)}, u32[]{:S(2)}, u32[]{:S(2)}) collective-permute-start(bf16[2,32,1024]{2,1,0:T(8,128)(2,1)S(1)} %get-tuple-element.70.refs_0_), channel_id=1, source_target_pairs={{0,4},{1,5},{2,6},{3,7},{4,0},{5,1},{6,2},{7,3},{8,12},{9,13},{10,... | collective-permute-start | bytes 393224 | tf_op jit(solution)/shard_map/ppermute | solution.py:361
  9.1 12.9 %collective-permute-start.2 = (bf16[2,64,1024]{2,1,0:T(8,128)(2,1)S(1)}, bf16[2,64,1024]{2,1,0:T(8,128)(2,1)S(1)}, u32[]{:S(2)}, u32[]{:S(2)}) collective-permute-start(bf16[2,64,1024]{2,1,0:T(8,128)(2,1)S(1)} %get-tuple-element.69.refs_1_), channel_id=1, source_target_pairs={{0,2},{1,3},{2,0},{3,1},{4,6},{5,7},{6,4},{7,5},{8,10},{9,11},{10,... | collective-permute-start | bytes 786440 | tf_op jit(solution)/shard_map/ppermute | solution.py:361
  11.0 18.5 %collective-permute-start.12 = (bf16[256,1024]{1,0:T(8,128)(2,1)S(1)}, bf16[256,1024]{1,0:T(8,128)(2,1)S(1)}, u32[]{:S(2)}, u32[]{:S(2)}) collective-permute-start(bf16[256,1024]{1,0:T(8,128)(2,1)S(1)} %collective-permute-done.1.refs_5_), channel_id=1, source_target_pairs={{0,16},{1,9},{2,18},{3,11},{4,20},{5,13},{6,22},{7,15},{8,24},{9,1... | collective-permute-start | bytes 1572872 | tf_op jit(solution)/shard_map/ppermute | solution.py:356
  13.1 17.9 %collective-permute-start.11 = (bf16[256,1024]{1,0:T(8,128)(2,1)S(1)}, bf16[256,1024]{1,0:T(8,128)(2,1)S(1)}, u32[]{:S(2)}, u32[]{:S(2)}) collective-permute-start(bf16[256,1024]{1,0:T(8,128)(2,1)S(1)} %bitcast.9), channel_id=1, source_target_pairs={{0,16},{1,9},{2,18},{3,11},{4,20},{5,13},{6,22},{7,15},{8,24},{9,1... | collective-permute-start | bytes 1572872 | tf_op jit(solution)/shard_map/ppermute | solution.py:356
  16.1 5.8 %collective-permute-start.4 = (bf16[2,32,1024]{2,1,0:T(8,128)(2,1)S(1)}, bf16[2,32,1024]{2,1,0:T(8,128)(2,1)S(1)}, u32[]{:S(2)}, u32[]{:S(2)}) collective-permute-start(bf16[2,32,1024]{2,1,0:T(8,128)(2,1)S(1)} %collective-permute-done.3.refs_5_.refs_6_), channel_id=1, source_target_pairs={{0,2},{1,3},{2,0},{3,1},{4,6},{5,7},{6,4},{7,5},{8,10},{9,11},{10,... | collective-permute-start | bytes 393224 | tf_op jit(solution)/shard_map/ppermute | solution.py:361
  22.0 1.9 %collective-permute-start.5 = (bf16[2,64,1024]{2,1,0:T(8,128)(2,1)S(1)}, bf16[2,64,1024]{2,1,0:T(8,128)(2,1)S(1)}, u32[]{:S(2)}, u32[]{:S(2)}) collective-permute-start(bf16[2,64,1024]{2,1,0:T(8,128)(2,1)S(1)} %collective-permute-done.2.refs_3_.refs_4_), channel_id=1, source_target_pairs={{0,1},{1,0},{2,3},{3,2},{4,5},{5,4},{6,7},{7,6},{8,9},{9,8},{10,11... | collective-permute-start | bytes 786440 | tf_op jit(solution)/shard_map/ppermute | solution.py:361
  22.0 1.7 %collective-permute-start.7 = (bf16[2,32,1024]{2,1,0:T(8,128)(2,1)S(1)}, bf16[2,32,1024]{2,1,0:T(8,128)(2,1)S(1)}, u32[]{:S(2)}, u32[]{:S(2)}) collective-permute-start(bf16[2,32,1024]{2,1,0:T(8,128)(2,1)S(1)} %collective-permute-done.4.refs_7_.refs_8_), channel_id=1, source_target_pairs={{0,1},{1,0},{2,3},{3,2},{4,5},{5,4},{6,7},{7,6},{8,9},{9,8},{10,11... | collective-permute-start | bytes 393224 | tf_op jit(solution)/shard_map/ppermute | solution.py:361
  22.5 1.4 %collective-permute-start.6 = (bf16[2,32,1024]{2,1,0:T(8,128)(2,1)S(1)}, bf16[2,32,1024]{2,1,0:T(8,128)(2,1)S(1)}, u32[]{:S(2)}, u32[]{:S(2)}) collective-permute-start(bf16[2,32,1024]{2,1,0:T(8,128)(2,1)S(1)} %collective-permute-done.3.refs_5_.refs_6_), channel_id=1, source_target_pairs={{0,1},{1,0},{2,3},{3,2},{4,5},{5,4},{6,7},{7,6},{8,9},{9,8},{10,11... | collective-permute-start | bytes 393224 | tf_op jit(solution)/shard_map/ppermute | solution.py:361
  26.0 8.8 %collective-permute-start.10 = (bf16[256,256]{1,0:T(8,128)(2,1)S(1)}, bf16[256,256]{1,0:T(8,128)(2,1)S(1)}, u32[]{:S(2)}, u32[]{:S(2)}) collective-permute-start(bf16[256,256]{1,0:T(8,128)(2,1)S(1)} %get-tuple-element.83), channel_id=1, source_target_pairs={{0,24},{1,25},{2,26},{3,27},{4,28},{5,29},{6,30},{7,31},{8,16},{9,... | collective-permute-start | bytes 393224 | tf_op jit(solution)/shard_map/ppermute | solution.py:356
  27.5 7.9 %collective-permute-start.8 = (bf16[256,256]{1,0:T(8,128)(2,1)S(1)}, bf16[256,256]{1,0:T(8,128)(2,1)S(1)}, u32[]{:S(2)}, u32[]{:S(2)}) collective-permute-start(bf16[256,256]{1,0:T(8,128)(2,1)S(1)} %get-tuple-element.81), channel_id=1, source_target_pairs={{0,8},{1,17},{2,10},{3,19},{4,12},{5,21},{6,14},{7,23},{8,0},{9,25... | collective-permute-start | bytes 393224 | tf_op jit(solution)/shard_map/ppermute | solution.py:356
  29.0 6.4 %collective-permute-start.9 = (bf16[256,256]{1,0:T(8,128)(2,1)S(1)}, bf16[256,256]{1,0:T(8,128)(2,1)S(1)}, u32[]{:S(2)}, u32[]{:S(2)}) collective-permute-start(bf16[256,256]{1,0:T(8,128)(2,1)S(1)} %get-tuple-element.82), channel_id=1, source_target_pairs={{0,16},{1,9},{2,18},{3,11},{4,20},{5,13},{6,22},{7,15},{8,24},{9,1... | collective-permute-start | bytes 393224 | tf_op jit(solution)/shard_map/ppermute | solution.py:356
  29.5 12.8 %collective-permute-start.21 = (bf16[64,2176]{1,0:T(8,128)(2,1)S(1)}, bf16[64,2176]{1,0:T(8,128)(2,1)S(1)}, u32[]{:S(2)}, u32[]{:S(2)}) collective-permute-start(bf16[64,2176]{1,0:T(8,128)(2,1)S(1)} %get-tuple-element.103), channel_id=1, source_target_pairs={{0,2},{1,3},{2,0},{3,1},{4,6},{5,7},{6,4},{7,5},{8,10},{9,11},{10,... | collective-permute-start | bytes 835592 | tf_op jit(solution)/shard_map/ppermute | solution.py:361
  31.0 8.9 %collective-permute-start.15 = (bf16[32,2176]{1,0:T(8,128)(2,1)S(1)}, bf16[32,2176]{1,0:T(8,128)(2,1)S(1)}, u32[]{:S(2)}, u32[]{:S(2)}) collective-permute-start(bf16[32,2176]{1,0:T(8,128)(2,1)S(1)} %get-tuple-element.92), channel_id=1, source_target_pairs={{0,4},{1,5},{2,6},{3,7},{4,0},{5,1},{6,2},{7,3},{8,12},{9,13},{10,... | collective-permute-start | bytes 417800 | tf_op jit(solution)/shard_map/ppermute | solution.py:361
  34.7 7.6 %copy-start.4 = (bf16[1,256,1024]{2,1,0:T(8,128)(2,1)S(1)}, bf16[1,256,1024]{2,1,0:T(8,128)(2,1)}, u32[]{:S(2)}) copy-start(bf16[1,256,1024]{2,1,0:T(8,128)(2,1)} %param.6) | copy-start | bytes 1572868
  34.7 7.6 %copy-start.6 = (bf16[1,256,1024]{2,1,0:T(8,128)(2,1)S(1)}, bf16[1,256,1024]{2,1,0:T(8,128)(2,1)}, u32[]{:S(2)}) copy-start(bf16[1,256,1024]{2,1,0:T(8,128)(2,1)} %param.7) | copy-start | bytes 1572868
  36.2 1.4 %collective-permute-start.13 = (bf16[2,32,1024]{2,1,0:T(8,128)(2,1)S(1)}, bf16[2,32,1024]{2,1,0:T(8,128)(2,1)S(1)}, u32[]{:S(2)}, u32[]{:S(2)}) collective-permute-start(bf16[2,32,1024]{2,1,0:T(8,128)(2,1)S(1)} %get-tuple-element.85), channel_id=1, source_target_pairs={{0,1},{1,0},{2,3},{3,2},{4,5},{5,4},{6,7},{7,6},{8,9},{9,8},{10,11... | collective-permute-start | bytes 393224 | tf_op jit(solution)/shard_map/ppermute | solution.py:361
  36.2 1.5 %collective-permute-start.14 = (bf16[2,32,1024]{2,1,0:T(8,128)(2,1)S(1)}, bf16[2,32,1024]{2,1,0:T(8,128)(2,1)S(1)}, u32[]{:S(2)}, u32[]{:S(2)}) collective-permute-start(bf16[2,32,1024]{2,1,0:T(8,128)(2,1)S(1)} %get-tuple-element.86), channel_id=1, source_target_pairs={{0,1},{1,0},{2,3},{3,2},{4,5},{5,4},{6,7},{7,6},{8,9},{9,8},{10,11... | collective-permute-start | bytes 393224 | tf_op jit(solution)/shard_map/ppermute | solution.py:361
  37.8 9.6 %collective-permute-start.16 = (bf16[2,32,1024]{2,1,0:T(8,128)(2,1)S(1)}, bf16[2,32,1024]{2,1,0:T(8,128)(2,1)S(1)}, u32[]{:S(2)}, u32[]{:S(2)}) collective-permute-start(bf16[2,32,1024]{2,1,0:T(8,128)(2,1)S(1)} %get-tuple-element.95), channel_id=1, source_target_pairs={{0,4},{1,5},{2,6},{3,7},{4,0},{5,1},{6,2},{7,3},{8,12},{9,13},{10,... | collective-permute-start | bytes 393224 | tf_op jit(solution)/shard_map/ppermute | solution.py:361
  39.8 8.8 %collective-permute-start.20 = (bf16[128,2176]{1,0:T(8,128)(2,1)S(1)}, bf16[128,2176]{1,0:T(8,128)(2,1)S(1)}, u32[]{:S(2)}, u32[]{:S(2)}) collective-permute-start(bf16[128,2176]{1,0:T(8,128)(2,1)S(1)} %get-tuple-element.101), channel_id=1, source_target_pairs={{0,1},{1,0},{2,3},{3,2},{4,5},{5,4},{6,7},{7,6},{8,9},{9,8},{10,11... | collective-permute-start | bytes 1671176 | tf_op jit(solution)/shard_map/ppermute | solution.py:361
  39.8 7.9 %collective-permute-start.18 = (bf16[32,2176]{1,0:T(8,128)(2,1)S(1)}, bf16[32,2176]{1,0:T(8,128)(2,1)S(1)}, u32[]{:S(2)}, u32[]{:S(2)}) collective-permute-start(bf16[32,2176]{1,0:T(8,128)(2,1)S(1)} %collective-permute-done.15.refs_1_), channel_id=1, source_target_pairs={{0,2},{1,3},{2,0},{3,1},{4,6},{5,7},{6,4},{7,5},{8,10},{9,11},{10,... | collective-permute-start | bytes 417800 | tf_op jit(solution)/shard_map/ppermute | solution.py:361
  42.3 6.3 %collective-permute-start.22 = (bf16[64,2176]{1,0:T(8,128)(2,1)S(1)}, bf16[64,2176]{1,0:T(8,128)(2,1)S(1)}, u32[]{:S(2)}, u32[]{:S(2)}) collective-permute-start(bf16[64,2176]{1,0:T(8,128)(2,1)S(1)} %collective-permute-done.21.refs_3_), channel_id=1, source_target_pairs={{0,1},{1,0},{2,3},{3,2},{4,5},{5,4},{6,7},{7,6},{8,9},{9,8},{10,11... | collective-permute-start | bytes 835592 | tf_op jit(solution)/shard_map/ppermute | solution.py:361
  47.5 2.6 %collective-permute-start.17 = (bf16[32,2176]{1,0:T(8,128)(2,1)S(1)}, bf16[32,2176]{1,0:T(8,128)(2,1)S(1)}, u32[]{:S(2)}, u32[]{:S(2)}) collective-permute-start(bf16[32,2176]{1,0:T(8,128)(2,1)S(1)} %collective-permute-done.15.refs_1_), channel_id=1, source_target_pairs={{0,1},{1,0},{2,3},{3,2},{4,5},{5,4},{6,7},{7,6},{8,9},{9,8},{10,11... | collective-permute-start | bytes 417800 | tf_op jit(solution)/shard_map/ppermute | solution.py:361
  47.7 2.3 %collective-permute-start.19 = (bf16[32,2176]{1,0:T(8,128)(2,1)S(1)}, bf16[32,2176]{1,0:T(8,128)(2,1)S(1)}, u32[]{:S(2)}, u32[]{:S(2)}) collective-permute-start(bf16[32,2176]{1,0:T(8,128)(2,1)S(1)} %collective-permute-done.18.refs_3_), channel_id=1, source_target_pairs={{0,1},{1,0},{2,3},{3,2},{4,5},{5,4},{6,7},{7,6},{8,9},{9,8},{10,11... | collective-permute-start | bytes 417800 | tf_op jit(solution)/shard_map/ppermute | solution.py:361
  48.0 4.3 %collective-permute-start.23 = (bf16[1,32,1024]{2,1,0:T(8,128)(2,1)S(1)}, bf16[1,32,1024]{2,1,0:T(8,128)(2,1)S(1)}, u32[]{:S(2)}, u32[]{:S(2)}) collective-permute-start(bf16[1,32,1024]{2,1,0:T(8,128)(2,1)S(1)} %get-tuple-element.96), channel_id=1, source_target_pairs={{0,2},{1,3},{2,0},{3,1},{4,6},{5,7},{6,4},{7,5},{8,10},{9,11},{10,... | collective-permute-start | bytes 196616 | tf_op jit(solution)/shard_map/ppermute | solution.py:361

commit v5 on v4

--- a/solution.py
+++ b/solution.py
@@ -274,10 +274,6 @@
         out_ref[:, c : c + 256] = nn(att, w_ref[:, c : c + 256]).astype(BF16)
 
 
-def final_kernel(factor, keep_ref, got_ref, out_ref):
-    out_ref[...] = (keep_ref[0] + got_ref[0].astype(F32)) * factor
-
-
 def owner_kernel(chosen, pieces, tokens, *refs):
     kvs, refs = refs[: len(chosen)], refs[len(chosen) :]
     msgs, refs = refs[: sum(pieces)], refs[sum(pieces) :]
@@ -544,14 +540,7 @@
     gk, gv = owned(some, messages[:-1], after(dk0, send), dv0, BF16)
     gk, gv = owned([last], messages[-1:], gk, gv, BF16)
 
-    (gw,) = call(
-        functools.partial(final_kernel, factor),
-        [((own_rows, width), F32)],
-        "total",
-        1,
-        after(keep, gk),
-        came,
-    )
+    gw = (after(keep, gk)[0] + came[0].astype(F32)) * factor
     return (mixed[None], gq[None], gk[None], gv[None], gw)
 
 

time: 53.2 us -> 53.2 us (level)
  other arithmetic: 0 us -> 0.68 us
  Pallas kernels: 15.3 us -> 14.7 us
    mul x0 -> x1, other arithmetic: none -> 0.68 us  [body(): gw = (after(keep, gk)[0] + came[0].astype(F32)) * factor]
    pallas_call x11 -> x10, Pallas kernels: 15.3 us -> 14.7 us  [call(): pl.pallas_call(kernel, name=name, out_shape=[jax.ShapeDtypeStruct(s, t) f...]
where the time goes in v5:
time: 53.2 us; the launch traced here: 53 us
  starting transfers between devices  23.6 us (44%)
  Pallas kernels  14.7 us (28%)
  waiting for transfers between devices  11.2 us (21%)
  local copies, waits for them, and re-layouts  2.1 us (4%)
  between operations  0.75 us (1%)
  other arithmetic  0.68 us (1%)
    ppermute x18, starting transfers between devices, swap(): return lax.ppermute(x, axis, [(i, i ^ mask) for i in range(count)])  15 us
    pallas_call x10, Pallas kernels, call(): pl.pallas_call(kernel, name=name, out_shape=[jax.ShapeDtypeStruct(s, t) f...  14.7 us
    ppermute x18, waiting for transfers between devices, swap(): return lax.ppermute(x, axis, [(i, i ^ mask) for i in range(count)])  10.2 us
    ppermute x6, starting transfers between devices, exchange_role(): return lax.ppermute(x, ('dp', 'seq'), pairs)  8.62 us
    unnamed x14, local copies, waits for them, and re-layouts  2.1 us
  transfers between devices with their start and end apart: 24, of which 11 were waited for; matrix products, arithmetic and copies ran while one was open for 0% of the time, Pallas kernels for 28%

profile of v5, /device:TPU:0, one launch (start us, length us, event | category | flops | bytes accessed | tf_op | source)
XLA Modules:
  0.0 53.0 jit_solution(11716280778608498933)
XLA Ops:
  0.6 3.0 %collective-permute-start.1 = (bf16[256,1024]{1,0:T(8,128)(2,1)}, bf16[256,1024]{1,0:T(8,128)(2,1)S(1)}, u32[]{:S(2)}, u32[]{:S(2)}) collective-permute-start(bf16[256,1024]{1,0:T(8,128)(2,1)} %bitcast.10), channel_id=1, source_target_pairs={{0,8},{1,17},{2,10},{3,19},{4,12},{5,21},{6,14},{7,23},{8,0},{9,25... | collective-permute-start | bytes 1572872 | tf_op jit(solution)/shard_map/ppermute | solution.py:352
  3.6 1.0 %copy-done.3 = bf16[1,256,1024]{2,1,0:T(8,128)(2,1)S(1)} copy-done((bf16[1,256,1024]{2,1,0:T(8,128)(2,1)S(1)}, bf16[1,256,1024]{2,1,0:T(8,128)(2,1)}, u32[]{:S(2)}) %copy-start.3) | copy-done | bytes 524312
  4.7 1.0 %copy-done.5 = bf16[1,256,1024]{2,1,0:T(8,128)(2,1)S(1)} copy-done((bf16[1,256,1024]{2,1,0:T(8,128)(2,1)S(1)}, bf16[1,256,1024]{2,1,0:T(8,128)(2,1)}, u32[]{:S(2)}) %copy-start.5) | copy-done | bytes 524312
  5.7 0.6 %pool.1 = (bf16[2,128,1024]{2,1,0:T(8,128)(2,1)S(1)}, bf16[2,64,1024]{2,1,0:T(8,128)(2,1)S(1)}, bf16[2,32,1024]{2,1,0:T(8,128)(2,1)S(1)}) custom-call(bf16[256,1024]{1,0:T(8,128)(2,1)S(1)} %bitcast.16, bf16[256,1024]{1,0:T(8,128)(2,1)S(1)} %bitcast.19), custom_call_target="tpu_custom_call" | custom-call | flops 5000000000 | bytes 1 | tf_op jit(solution)/shard_map/pool/pallas_call | solution.py:46
  6.4 0.0 collective-permute-start
  6.4 2.7 %collective-permute-start.3 = (bf16[2,32,1024]{2,1,0:T(8,128)(2,1)S(1)}, bf16[2,32,1024]{2,1,0:T(8,128)(2,1)S(1)}, u32[]{:S(2)}, u32[]{:S(2)}) collective-permute-start(bf16[2,32,1024]{2,1,0:T(8,128)(2,1)S(1)} %get-tuple-element.70.refs_0_), channel_id=1, source_target_pairs={{0,4},{1,5},{2,6},{3,7},{4,0},{5,1},{6,2},{7,3},{8,12},{9,13},{10,... | collective-permute-start | bytes 393224 | tf_op jit(solution)/shard_map/ppermute | solution.py:357
  9.1 1.6 %collective-permute-start.2 = (bf16[2,64,1024]{2,1,0:T(8,128)(2,1)S(1)}, bf16[2,64,1024]{2,1,0:T(8,128)(2,1)S(1)}, u32[]{:S(2)}, u32[]{:S(2)}) collective-permute-start(bf16[2,64,1024]{2,1,0:T(8,128)(2,1)S(1)} %get-tuple-element.69.refs_1_), channel_id=1, source_target_pairs={{0,2},{1,3},{2,0},{3,1},{4,6},{5,7},{6,4},{7,5},{8,10},{9,11},{10,... | collective-permute-start | bytes 786440 | tf_op jit(solution)/shard_map/ppermute | solution.py:357
  10.7 0.4 collective-permute-done.1.refs_5_
  11.0 2.0 %collective-permute-start.12 = (bf16[256,1024]{1,0:T(8,128)(2,1)S(1)}, bf16[256,1024]{1,0:T(8,128)(2,1)S(1)}, u32[]{:S(2)}, u32[]{:S(2)}) collective-permute-start(bf16[256,1024]{1,0:T(8,128)(2,1)S(1)} %collective-permute-done.1.refs_5_), channel_id=1, source_target_pairs={{0,16},{1,9},{2,18},{3,11},{4,20},{5,13},{6,22},{7,15},{8,24},{9,1... | collective-permute-start | bytes 1572872 | tf_op jit(solution)/shard_map/ppermute | solution.py:352
  13.1 0.0 copy-done
  13.1 0.0 collective-permute-start.11
  13.1 3.1 %collective-permute-done.3.refs_5_.refs_6_ = bf16[2,32,1024]{2,1,0:T(8,128)(2,1)S(1)} collective-permute-done((bf16[2,32,1024]{2,1,0:T(8,128)(2,1)S(1)}, bf16[2,32,1024]{2,1,0:T(8,128)(2,1)S(1)}, u32[]{:S(2)}, u32[]{:S(2)}) %collective-permute-start.3) | collective-permute-done | bytes 131104 | tf_op jit(solution)/shard_map/ppermute | solution.py:357
  16.1 0.6 %collective-permute-start.4 = (bf16[2,32,1024]{2,1,0:T(8,128)(2,1)S(1)}, bf16[2,32,1024]{2,1,0:T(8,128)(2,1)S(1)}, u32[]{:S(2)}, u32[]{:S(2)}) collective-permute-start(bf16[2,32,1024]{2,1,0:T(8,128)(2,1)S(1)} %collective-permute-done.3.refs_5_.refs_6_), channel_id=1, source_target_pairs={{0,2},{1,3},{2,0},{3,1},{4,6},{5,7},{6,4},{7,5},{8,10},{9,11},{10,... | collective-permute-start | bytes 393224 | tf_op jit(solution)/shard_map/ppermute | solution.py:357
  16.8 0.0 collective-permute-done.kv_ref.refs_3_
  16.8 0.0 copy-done.1
  16.8 0.0 copy-done.2
  16.8 2.7 %early.1 = (bf16[3,256,1024]{2,1,0:T(8,128)(2,1)S(1)}, bf16[1024,256]{1,0:T(8,128)(2,1)S(1)}, bf16[8,384,256]{2,1,0:T(8,128)(2,1)S(1)}, f32[1024,256]{1,0:T(8,12...) custom-call(bf16[256,1024]{1,0:T(8,128)(2,1)S(1)} %bitcast.14, ...), custom_call_target="tpu_custom_call" | custom-call | flops 1 | bytes 1 | tf_op jit(solution)/shard_map/early/pallas_call | solution.py:46
  19.5 2.5 %collective-permute-done.4.refs_7_.refs_8_ = bf16[2,32,1024]{2,1,0:T(8,128)(2,1)S(1)} collective-permute-done((bf16[2,32,1024]{2,1,0:T(8,128)(2,1)S(1)}, bf16[2,32,1024]{2,1,0:T(8,128)(2,1)S(1)}, u32[]{:S(2)}, u32[]{:S(2)}) %collective-permute-start.4) | collective-permute-done | bytes 131104 | tf_op jit(solution)/shard_map/ppermute | solution.py:357
  22.0 0.0 collective-permute-done.2.refs_3_.refs_4_
  22.0 0.0 collective-permute-start.5
  22.0 0.5 collective-permute-start.7
  22.5 0.0 collective-permute-start.6
  22.5 1.2 %collective-permute-done.7.refs_8_.refs_9_ = bf16[2,32,1024]{2,1,0:T(8,128)(2,1)S(1)} collective-permute-done((bf16[2,32,1024]{2,1,0:T(8,128)(2,1)S(1)}, bf16[2,32,1024]{2,1,0:T(8,128)(2,1)S(1)}, u32[]{:S(2)}, u32[]{:S(2)}) %collective-permute-start.7) | collective-permute-done | bytes 131104 | tf_op jit(solution)/shard_map/ppermute | solution.py:357
  23.7 0.2 collective-permute-done.6.refs_6_.refs_7_
  23.9 0.0 collective-permute-done.5.refs_4_.refs_5_
  23.9 2.1 %forward.1 = (bf16[8,256,256]{2,1,0:T(8,128)(2,1)S(1)}, bf16[1024,256]{1,0:T(8,128)(2,1)S(1)}, bf16[1024,256]{1,0:T(8,128)(2,1)S(1)}, f32[16,256]{1,0:T(8,128)S(...) custom-call(bf16[3,256,1024]{2,1,0:T(8,128)(2,1)S(1)} %get-tuple-ele, ...), custom_call_target="tpu_custom_call" | custom-call | flops 1 | bytes 1 | tf_op jit(solution)/shard_map/forward/pallas_call | solution.py:46
  26.0 1.5 %collective-permute-start.10 = (bf16[256,256]{1,0:T(8,128)(2,1)S(1)}, bf16[256,256]{1,0:T(8,128)(2,1)S(1)}, u32[]{:S(2)}, u32[]{:S(2)}) collective-permute-start(bf16[256,256]{1,0:T(8,128)(2,1)S(1)} %get-tuple-element.83), channel_id=1, source_target_pairs={{0,24},{1,25},{2,26},{3,27},{4,28},{5,29},{6,30},{7,31},{8,16},{9,... | collective-permute-start | bytes 393224 | tf_op jit(solution)/shard_map/ppermute | solution.py:352
  27.5 1.5 %collective-permute-start.8 = (bf16[256,256]{1,0:T(8,128)(2,1)S(1)}, bf16[256,256]{1,0:T(8,128)(2,1)S(1)}, u32[]{:S(2)}, u32[]{:S(2)}) collective-permute-start(bf16[256,256]{1,0:T(8,128)(2,1)S(1)} %get-tuple-element.81), channel_id=1, source_target_pairs={{0,8},{1,17},{2,10},{3,19},{4,12},{5,21},{6,14},{7,23},{8,0},{9,25... | collective-permute-start | bytes 393224 | tf_op jit(solution)/shard_map/ppermute | solution.py:352
  29.0 0.5 collective-permute-start.9
  29.5 0.0 collective-permute-done.12.refs_7_
  29.5 1.4 %collective-permute-start.21 = (bf16[64,2176]{1,0:T(8,128)(2,1)S(1)}, bf16[64,2176]{1,0:T(8,128)(2,1)S(1)}, u32[]{:S(2)}, u32[]{:S(2)}) collective-permute-start(bf16[64,2176]{1,0:T(8,128)(2,1)S(1)} %get-tuple-element.103), channel_id=1, source_target_pairs={{0,2},{1,3},{2,0},{3,1},{4,6},{5,7},{6,4},{7,5},{8,10},{9,11},{10,... | collective-permute-start | bytes 835592 | tf_op jit(solution)/shard_map/ppermute | solution.py:357
  31.0 0.0 collective-permute-done.11.refs_6_
  31.0 2.2 %collective-permute-start.15 = (bf16[32,2176]{1,0:T(8,128)(2,1)S(1)}, bf16[32,2176]{1,0:T(8,128)(2,1)S(1)}, u32[]{:S(2)}, u32[]{:S(2)}) collective-permute-start(bf16[32,2176]{1,0:T(8,128)(2,1)S(1)} %get-tuple-element.92), channel_id=1, source_target_pairs={{0,4},{1,5},{2,6},{3,7},{4,0},{5,1},{6,2},{7,3},{8,12},{9,13},{10,... | collective-permute-start | bytes 417800 | tf_op jit(solution)/shard_map/ppermute | solution.py:357
  33.2 1.6 %mixed.1 = bf16[256,1024]{1,0:T(8,128)(2,1)} custom-call(bf16[1024,256]{1,0:T(8,128)(2,1)S(1)} %get-tuple-element.74.att_ref, bf16[1024,1024]{1,0:T(8,128)(2,1)S(1)} %copy-done.1), custom_call_target="tpu_custom_call" | custom-call | flops 5000000000 | bytes 1 | tf_op jit(solution)/shard_map/mixed/pallas_call | solution.py:46
  34.7 0.0 collective-permute-done.10.refs_3_
  34.7 0.6 %collective-permute-done.8.refs_1_ = bf16[256,256]{1,0:T(8,128)(2,1)S(1)} collective-permute-done((bf16[256,256]{1,0:T(8,128)(2,1)S(1)}, bf16[256,256]{1,0:T(8,128)(2,1)S(1)}, u32[]{:S(2)}, u32[]{:S(2)}) %collective-permute-start.8) | collective-permute-done | bytes 131104 | tf_op jit(solution)/shard_map/ppermute | solution.py:352
  35.4 0.0 collective-permute-done.9.refs_2_
  35.4 0.8 %weight.1 = (f32[4,32,1024]{2,1,0:T(8,128)S(1)}, bf16[2,32,1024]{2,1,0:T(8,128)(2,1)S(1)}, bf16[2,32,1024]{2,1,0:T(8,128)(2,1)S(1)}) custom-call(bf16[256,256]{1,0:T(8,128)(2,1)S(1)} %get-tuple-element.80.refs_0_, bf16[256,256]{1,0:T(8,128)(2,1)S(1)} %collective-permute-done.8.refs_1_, bf16[256,256]{1,0:T(8,128)(2,1)S(1)} %collective-permute-done.9.refs_2_, ...), custom_call_target="tpu_custom_call" | custom-call | flops 1 | bytes 1 | tf_op jit(solution)/shard_map/weight/pallas_call | solution.py:46
  36.2 0.1 collective-permute-start.13
  36.2 0.5 collective-permute-start.14
  36.7 0.8 %collective-permute-done.13.refs_0_ = bf16[2,32,1024]{2,1,0:T(8,128)(2,1)S(1)} collective-permute-done((bf16[2,32,1024]{2,1,0:T(8,128)(2,1)S(1)}, bf16[2,32,1024]{2,1,0:T(8,128)(2,1)S(1)}, u32[]{:S(2)}, u32[]{:S(2)}) %collective-permute-start.13) | collective-permute-done | bytes 131104 | tf_op jit(solution)/shard_map/ppermute | solution.py:357
  37.6 0.2 collective-permute-done.14.refs_1_
  37.8 0.1 halve.2
  37.8 2.0 %collective-permute-start.16 = (bf16[2,32,1024]{2,1,0:T(8,128)(2,1)S(1)}, bf16[2,32,1024]{2,1,0:T(8,128)(2,1)S(1)}, u32[]{:S(2)}, u32[]{:S(2)}) collective-permute-start(bf16[2,32,1024]{2,1,0:T(8,128)(2,1)S(1)} %get-tuple-element.95), channel_id=1, source_target_pairs={{0,4},{1,5},{2,6},{3,7},{4,0},{5,1},{6,2},{7,3},{8,12},{9,13},{10,... | collective-permute-start | bytes 393224 | tf_op jit(solution)/shard_map/ppermute | solution.py:357
  39.8 0.0 collective-permute-start.20
  39.8 0.0 collective-permute-done.15.refs_1_
  39.8 2.4 %collective-permute-start.18 = (bf16[32,2176]{1,0:T(8,128)(2,1)S(1)}, bf16[32,2176]{1,0:T(8,128)(2,1)S(1)}, u32[]{:S(2)}, u32[]{:S(2)}) collective-permute-start(bf16[32,2176]{1,0:T(8,128)(2,1)S(1)} %collective-permute-done.15.refs_1_), channel_id=1, source_target_pairs={{0,2},{1,3},{2,0},{3,1},{4,6},{5,7},{6,4},{7,5},{8,10},{9,11},{10,... | collective-permute-start | bytes 417800 | tf_op jit(solution)/shard_map/ppermute | solution.py:357
  42.3 0.0 collective-permute-done.21.refs_3_
  42.3 0.0 collective-permute-start.22
  42.3 0.0 copy-done.4
  42.3 3.4 %backward.1 = (bf16[256,1024]{1,0:T(8,128)(2,1)}, bf16[256,1024]{1,0:T(8,128)(2,1)S(1)}, bf16[256,1024]{1,0:T(8,128)(2,1)S(1)}) custom-call(bf16[8,384,256]{2,1,0:T(8,128)(2,1)S(1)} %get-tuple-element.75.e0_ref, bf16[8,256,256]{2,1,0:T(8,128)(2,1)S(1)} %get-tuple-element.76.e_ref, bf16[1024,256]{1,0:T(8,128)(2,1)S(1)} %get-tuple-element.77.grt0_ref, ...), custom_call_target="tpu_custom_call" | custom-call | flops 5000000000 | bytes 1 | tf_op jit(solution)/shard_map/backward/pallas_call | solution.py:46
  45.7 1.7 %collective-permute-done.16.refs_0_ = bf16[2,32,1024]{2,1,0:T(8,128)(2,1)S(1)} collective-permute-done((bf16[2,32,1024]{2,1,0:T(8,128)(2,1)S(1)}, bf16[2,32,1024]{2,1,0:T(8,128)(2,1)S(1)}, u32[]{:S(2)}, u32[]{:S(2)}) %collective-permute-start.16) | collective-permute-done | bytes 131104 | tf_op jit(solution)/shard_map/ppermute | solution.py:357
  47.5 0.1 collective-permute-start.17
  47.5 0.2 collective-permute-done.18.refs_3_
  47.7 0.3 collective-permute-start.19
  48.0 0.5 collective-permute-start.23
  48.6 0.0 collective-permute-done.22.refs_4_
  48.6 0.0 collective-permute-done.20.refs_2_
  48.6 1.5 %owner.2 = (bf16[256,1024]{1,0:T(8,128)(2,1)S(1)}, bf16[256,1024]{1,0:T(8,128)(2,1)S(1)}) custom-call(bf16[2,128,1024]{2,1,0:T(8,128)(2,1)S(1)} %get-tuple-element.59.refs_0_, bf16[2,64,1024]{2,1,0:T(8,128)(2,1)S(1)} %get-tuple-element.69.refs_1_, bf16[128,2176]{1,0:T(8,128)(2,1)S(1)} %collective-permute-done.20.refs_2_, ...), custom_call_target="tpu_custom_call" | custom-call | flops 1 | bytes 1 | tf_op jit(solution)/shard_map/owner/pallas_call | solution.py:46
  50.0 0.0 collective-permute-done.17.refs_2_
  50.1 0.0 collective-permute-done.19.refs_4_
  50.1 1.9 %owner.3 = (bf16[256,1024]{1,0:T(8,128)(2,1)}, bf16[256,1024]{1,0:T(8,128)(2,1)}) custom-call(bf16[2,32,1024]{2,1,0:T(8,128)(2,1)S(1)} %get-tuple-element.70.refs_0_, bf16[32,2176]{1,0:T(8,128)(2,1)S(1)} %collective-permute-done.15.refs_1_, bf16[32,2176]{1,0:T(8,128)(2,1)S(1)} %collective-permute-done.17.refs_2_, ...), custom_call_target="tpu_custom_call" | custom-call | flops 1 | bytes 1 | tf_op jit(solution)/shard_map/owner/pallas_call | solution.py:46
  52.0 0.3 collective-permute-done.23
  52.3 0.7 %multiply_bitcast_fusion = f32[32,1024]{1,0:T(8,128)} fusion(f32[1,32,1024]{2,1,0:T(8,128)S(1)} %get-tuple-element.112, bf16[1,32,1024]{2,1,0:T(8,128)(2,1)S(1)} %collective-permute-done.23), kind=kLoop, calls=%fused_computation | loop fusion | flops 98304 | bytes 327680 | tf_op jit(solution)/shard_map/mul | solution.py:543
  (9 shorter events, 0.0 us)
Async XLA Ops:
  0.6 10.4 %collective-permute-start.1 = (bf16[256,1024]{1,0:T(8,128)(2,1)}, bf16[256,1024]{1,0:T(8,128)(2,1)S(1)}, u32[]{:S(2)}, u32[]{:S(2)}) collective-permute-start(bf16[256,1024]{1,0:T(8,128)(2,1)} %bitcast.10), channel_id=1, source_target_pairs={{0,8},{1,17},{2,10},{3,19},{4,12},{5,21},{6,14},{7,23},{8,0},{9,25... | collective-permute-start | bytes 1572872 | tf_op jit(solution)/shard_map/ppermute | solution.py:352
  3.6 1.0 %copy-start.3 = (bf16[1,256,1024]{2,1,0:T(8,128)(2,1)S(1)}, bf16[1,256,1024]{2,1,0:T(8,128)(2,1)}, u32[]{:S(2)}) copy-start(bf16[1,256,1024]{2,1,0:T(8,128)(2,1)} %param.6) | copy-start | bytes 1572868
  4.7 1.0 %copy-start.5 = (bf16[1,256,1024]{2,1,0:T(8,128)(2,1)S(1)}, bf16[1,256,1024]{2,1,0:T(8,128)(2,1)}, u32[]{:S(2)}) copy-start(bf16[1,256,1024]{2,1,0:T(8,128)(2,1)} %param.7) | copy-start | bytes 1572868
  5.7 7.3 %copy-start = (bf16[1,256,1024]{2,1,0:T(8,128)(2,1)S(1)}, bf16[1,256,1024]{2,1,0:T(8,128)(2,1)}, u32[]{:S(2)}) copy-start(bf16[1,256,1024]{2,1,0:T(8,128)(2,1)} %param.8) | copy-start | bytes 1572868
  5.7 11.1 %copy-start.1 = (bf16[1024,1024]{1,0:T(8,128)(2,1)S(1)}, bf16[1024,1024]{1,0:T(8,128)(2,1)}, u32[]{:S(2)}) copy-start(bf16[1024,1024]{1,0:T(8,128)(2,1)} %w_ref.3) | copy-start | bytes 6291460
  5.7 11.1 %copy-start.2 = (bf16[1,256,1024]{2,1,0:T(8,128)(2,1)S(1)}, bf16[1,256,1024]{2,1,0:T(8,128)(2,1)}, u32[]{:S(2)}) copy-start(bf16[1,256,1024]{2,1,0:T(8,128)(2,1)} %param.5) | copy-start | bytes 1572868
  6.4 10.4 %collective-permute-start = (bf16[2,128,1024]{2,1,0:T(8,128)(2,1)S(1)}, bf16[2,128,1024]{2,1,0:T(8,128)(2,1)S(1)}, u32[]{:S(2)}, u32[]{:S(2)}) collective-permute-start(bf16[2,128,1024]{2,1,0:T(8,128)(2,1)S(1)} %get-tuple-element.59.refs_0_), channel_id=1, source_target_pairs={{0,1},{1,0},{2,3},{3,2},{4,5},{5,4},{6,7},{7,6},{8,9},{9,8},{10,11... | collective-permute-start | bytes 1572872 | tf_op jit(solution)/shard_map/ppermute | solution.py:357
  6.4 9.7 %collective-permute-start.3 = (bf16[2,32,1024]{2,1,0:T(8,128)(2,1)S(1)}, bf16[2,32,1024]{2,1,0:T(8,128)(2,1)S(1)}, u32[]{:S(2)}, u32[]{:S(2)}) collective-permute-start(bf16[2,32,1024]{2,1,0:T(8,128)(2,1)S(1)} %get-tuple-element.70.refs_0_), channel_id=1, source_target_pairs={{0,4},{1,5},{2,6},{3,7},{4,0},{5,1},{6,2},{7,3},{8,12},{9,13},{10,... | collective-permute-start | bytes 393224 | tf_op jit(solution)/shard_map/ppermute | solution.py:357
  9.1 12.9 %collective-permute-start.2 = (bf16[2,64,1024]{2,1,0:T(8,128)(2,1)S(1)}, bf16[2,64,1024]{2,1,0:T(8,128)(2,1)S(1)}, u32[]{:S(2)}, u32[]{:S(2)}) collective-permute-start(bf16[2,64,1024]{2,1,0:T(8,128)(2,1)S(1)} %get-tuple-element.69.refs_1_), channel_id=1, source_target_pairs={{0,2},{1,3},{2,0},{3,1},{4,6},{5,7},{6,4},{7,5},{8,10},{9,11},{10,... | collective-permute-start | bytes 786440 | tf_op jit(solution)/shard_map/ppermute | solution.py:357
  11.0 18.5 %collective-permute-start.12 = (bf16[256,1024]{1,0:T(8,128)(2,1)S(1)}, bf16[256,1024]{1,0:T(8,128)(2,1)S(1)}, u32[]{:S(2)}, u32[]{:S(2)}) collective-permute-start(bf16[256,1024]{1,0:T(8,128)(2,1)S(1)} %collective-permute-done.1.refs_5_), channel_id=1, source_target_pairs={{0,16},{1,9},{2,18},{3,11},{4,20},{5,13},{6,22},{7,15},{8,24},{9,1... | collective-permute-start | bytes 1572872 | tf_op jit(solution)/shard_map/ppermute | solution.py:352
  13.1 17.9 %collective-permute-start.11 = (bf16[256,1024]{1,0:T(8,128)(2,1)S(1)}, bf16[256,1024]{1,0:T(8,128)(2,1)S(1)}, u32[]{:S(2)}, u32[]{:S(2)}) collective-permute-start(bf16[256,1024]{1,0:T(8,128)(2,1)S(1)} %bitcast.11), channel_id=1, source_target_pairs={{0,16},{1,9},{2,18},{3,11},{4,20},{5,13},{6,22},{7,15},{8,24},{9,1... | collective-permute-start | bytes 1572872 | tf_op jit(solution)/shard_map/ppermute | solution.py:352
  16.1 5.8 %collective-permute-start.4 = (bf16[2,32,1024]{2,1,0:T(8,128)(2,1)S(1)}, bf16[2,32,1024]{2,1,0:T(8,128)(2,1)S(1)}, u32[]{:S(2)}, u32[]{:S(2)}) collective-permute-start(bf16[2,32,1024]{2,1,0:T(8,128)(2,1)S(1)} %collective-permute-done.3.refs_5_.refs_6_), channel_id=1, source_target_pairs={{0,2},{1,3},{2,0},{3,1},{4,6},{5,7},{6,4},{7,5},{8,10},{9,11},{10,... | collective-permute-start | bytes 393224 | tf_op jit(solution)/shard_map/ppermute | solution.py:357
  22.0 1.9 %collective-permute-start.5 = (bf16[2,64,1024]{2,1,0:T(8,128)(2,1)S(1)}, bf16[2,64,1024]{2,1,0:T(8,128)(2,1)S(1)}, u32[]{:S(2)}, u32[]{:S(2)}) collective-permute-start(bf16[2,64,1024]{2,1,0:T(8,128)(2,1)S(1)} %collective-permute-done.2.refs_3_.refs_4_), channel_id=1, source_target_pairs={{0,1},{1,0},{2,3},{3,2},{4,5},{5,4},{6,7},{7,6},{8,9},{9,8},{10,11... | collective-permute-start | bytes 786440 | tf_op jit(solution)/shard_map/ppermute | solution.py:357
  22.0 1.7 %collective-permute-start.7 = (bf16[2,32,1024]{2,1,0:T(8,128)(2,1)S(1)}, bf16[2,32,1024]{2,1,0:T(8,128)(2,1)S(1)}, u32[]{:S(2)}, u32[]{:S(2)}) collective-permute-start(bf16[2,32,1024]{2,1,0:T(8,128)(2,1)S(1)} %collective-permute-done.4.refs_7_.refs_8_), channel_id=1, source_target_pairs={{0,1},{1,0},{2,3},{3,2},{4,5},{5,4},{6,7},{7,6},{8,9},{9,8},{10,11... | collective-permute-start | bytes 393224 | tf_op jit(solution)/shard_map/ppermute | solution.py:357
  22.5 1.4 %collective-permute-start.6 = (bf16[2,32,1024]{2,1,0:T(8,128)(2,1)S(1)}, bf16[2,32,1024]{2,1,0:T(8,128)(2,1)S(1)}, u32[]{:S(2)}, u32[]{:S(2)}) collective-permute-start(bf16[2,32,1024]{2,1,0:T(8,128)(2,1)S(1)} %collective-permute-done.3.refs_5_.refs_6_), channel_id=1, source_target_pairs={{0,1},{1,0},{2,3},{3,2},{4,5},{5,4},{6,7},{7,6},{8,9},{9,8},{10,11... | collective-permute-start | bytes 393224 | tf_op jit(solution)/shard_map/ppermute | solution.py:357
  26.0 8.8 %collective-permute-start.10 = (bf16[256,256]{1,0:T(8,128)(2,1)S(1)}, bf16[256,256]{1,0:T(8,128)(2,1)S(1)}, u32[]{:S(2)}, u32[]{:S(2)}) collective-permute-start(bf16[256,256]{1,0:T(8,128)(2,1)S(1)} %get-tuple-element.83), channel_id=1, source_target_pairs={{0,24},{1,25},{2,26},{3,27},{4,28},{5,29},{6,30},{7,31},{8,16},{9,... | collective-permute-start | bytes 393224 | tf_op jit(solution)/shard_map/ppermute | solution.py:352
  27.5 7.9 %collective-permute-start.8 = (bf16[256,256]{1,0:T(8,128)(2,1)S(1)}, bf16[256,256]{1,0:T(8,128)(2,1)S(1)}, u32[]{:S(2)}, u32[]{:S(2)}) collective-permute-start(bf16[256,256]{1,0:T(8,128)(2,1)S(1)} %get-tuple-element.81), channel_id=1, source_target_pairs={{0,8},{1,17},{2,10},{3,19},{4,12},{5,21},{6,14},{7,23},{8,0},{9,25... | collective-permute-start | bytes 393224 | tf_op jit(solution)/shard_map/ppermute | solution.py:352
  29.0 6.4 %collective-permute-start.9 = (bf16[256,256]{1,0:T(8,128)(2,1)S(1)}, bf16[256,256]{1,0:T(8,128)(2,1)S(1)}, u32[]{:S(2)}, u32[]{:S(2)}) collective-permute-start(bf16[256,256]{1,0:T(8,128)(2,1)S(1)} %get-tuple-element.82), channel_id=1, source_target_pairs={{0,16},{1,9},{2,18},{3,11},{4,20},{5,13},{6,22},{7,15},{8,24},{9,1... | collective-permute-start | bytes 393224 | tf_op jit(solution)/shard_map/ppermute | solution.py:352
  29.5 12.8 %collective-permute-start.21 = (bf16[64,2176]{1,0:T(8,128)(2,1)S(1)}, bf16[64,2176]{1,0:T(8,128)(2,1)S(1)}, u32[]{:S(2)}, u32[]{:S(2)}) collective-permute-start(bf16[64,2176]{1,0:T(8,128)(2,1)S(1)} %get-tuple-element.103), channel_id=1, source_target_pairs={{0,2},{1,3},{2,0},{3,1},{4,6},{5,7},{6,4},{7,5},{8,10},{9,11},{10,... | collective-permute-start | bytes 835592 | tf_op jit(solution)/shard_map/ppermute | solution.py:357
  31.0 8.9 %collective-permute-start.15 = (bf16[32,2176]{1,0:T(8,128)(2,1)S(1)}, bf16[32,2176]{1,0:T(8,128)(2,1)S(1)}, u32[]{:S(2)}, u32[]{:S(2)}) collective-permute-start(bf16[32,2176]{1,0:T(8,128)(2,1)S(1)} %get-tuple-element.92), channel_id=1, source_target_pairs={{0,4},{1,5},{2,6},{3,7},{4,0},{5,1},{6,2},{7,3},{8,12},{9,13},{10,... | collective-permute-start | bytes 417800 | tf_op jit(solution)/shard_map/ppermute | solution.py:357
  34.7 7.6 %copy-start.4 = (bf16[1,256,1024]{2,1,0:T(8,128)(2,1)S(1)}, bf16[1,256,1024]{2,1,0:T(8,128)(2,1)}, u32[]{:S(2)}) copy-start(bf16[1,256,1024]{2,1,0:T(8,128)(2,1)} %param.6) | copy-start | bytes 1572868
  34.7 7.6 %copy-start.6 = (bf16[1,256,1024]{2,1,0:T(8,128)(2,1)S(1)}, bf16[1,256,1024]{2,1,0:T(8,128)(2,1)}, u32[]{:S(2)}) copy-start(bf16[1,256,1024]{2,1,0:T(8,128)(2,1)} %param.7) | copy-start | bytes 1572868
  36.2 1.4 %collective-permute-start.13 = (bf16[2,32,1024]{2,1,0:T(8,128)(2,1)S(1)}, bf16[2,32,1024]{2,1,0:T(8,128)(2,1)S(1)}, u32[]{:S(2)}, u32[]{:S(2)}) collective-permute-start(bf16[2,32,1024]{2,1,0:T(8,128)(2,1)S(1)} %get-tuple-element.85), channel_id=1, source_target_pairs={{0,1},{1,0},{2,3},{3,2},{4,5},{5,4},{6,7},{7,6},{8,9},{9,8},{10,11... | collective-permute-start | bytes 393224 | tf_op jit(solution)/shard_map/ppermute | solution.py:357
  36.2 1.5 %collective-permute-start.14 = (bf16[2,32,1024]{2,1,0:T(8,128)(2,1)S(1)}, bf16[2,32,1024]{2,1,0:T(8,128)(2,1)S(1)}, u32[]{:S(2)}, u32[]{:S(2)}) collective-permute-start(bf16[2,32,1024]{2,1,0:T(8,128)(2,1)S(1)} %get-tuple-element.86), channel_id=1, source_target_pairs={{0,1},{1,0},{2,3},{3,2},{4,5},{5,4},{6,7},{7,6},{8,9},{9,8},{10,11... | collective-permute-start | bytes 393224 | tf_op jit(solution)/shard_map/ppermute | solution.py:357
  37.8 9.6 %collective-permute-start.16 = (bf16[2,32,1024]{2,1,0:T(8,128)(2,1)S(1)}, bf16[2,32,1024]{2,1,0:T(8,128)(2,1)S(1)}, u32[]{:S(2)}, u32[]{:S(2)}) collective-permute-start(bf16[2,32,1024]{2,1,0:T(8,128)(2,1)S(1)} %get-tuple-element.95), channel_id=1, source_target_pairs={{0,4},{1,5},{2,6},{3,7},{4,0},{5,1},{6,2},{7,3},{8,12},{9,13},{10,... | collective-permute-start | bytes 393224 | tf_op jit(solution)/shard_map/ppermute | solution.py:357
  39.8 8.8 %collective-permute-start.20 = (bf16[128,2176]{1,0:T(8,128)(2,1)S(1)}, bf16[128,2176]{1,0:T(8,128)(2,1)S(1)}, u32[]{:S(2)}, u32[]{:S(2)}) collective-permute-start(bf16[128,2176]{1,0:T(8,128)(2,1)S(1)} %get-tuple-element.101), channel_id=1, source_target_pairs={{0,1},{1,0},{2,3},{3,2},{4,5},{5,4},{6,7},{7,6},{8,9},{9,8},{10,11... | collective-permute-start | bytes 1671176 | tf_op jit(solution)/shard_map/ppermute | solution.py:357
  39.8 7.9 %collective-permute-start.18 = (bf16[32,2176]{1,0:T(8,128)(2,1)S(1)}, bf16[32,2176]{1,0:T(8,128)(2,1)S(1)}, u32[]{:S(2)}, u32[]{:S(2)}) collective-permute-start(bf16[32,2176]{1,0:T(8,128)(2,1)S(1)} %collective-permute-done.15.refs_1_), channel_id=1, source_target_pairs={{0,2},{1,3},{2,0},{3,1},{4,6},{5,7},{6,4},{7,5},{8,10},{9,11},{10,... | collective-permute-start | bytes 417800 | tf_op jit(solution)/shard_map/ppermute | solution.py:357
  42.3 6.3 %collective-permute-start.22 = (bf16[64,2176]{1,0:T(8,128)(2,1)S(1)}, bf16[64,2176]{1,0:T(8,128)(2,1)S(1)}, u32[]{:S(2)}, u32[]{:S(2)}) collective-permute-start(bf16[64,2176]{1,0:T(8,128)(2,1)S(1)} %collective-permute-done.21.refs_3_), channel_id=1, source_target_pairs={{0,1},{1,0},{2,3},{3,2},{4,5},{5,4},{6,7},{7,6},{8,9},{9,8},{10,11... | collective-permute-start | bytes 835592 | tf_op jit(solution)/shard_map/ppermute | solution.py:357
  47.5 2.6 %collective-permute-start.17 = (bf16[32,2176]{1,0:T(8,128)(2,1)S(1)}, bf16[32,2176]{1,0:T(8,128)(2,1)S(1)}, u32[]{:S(2)}, u32[]{:S(2)}) collective-permute-start(bf16[32,2176]{1,0:T(8,128)(2,1)S(1)} %collective-permute-done.15.refs_1_), channel_id=1, source_target_pairs={{0,1},{1,0},{2,3},{3,2},{4,5},{5,4},{6,7},{7,6},{8,9},{9,8},{10,11... | collective-permute-start | bytes 417800 | tf_op jit(solution)/shard_map/ppermute | solution.py:357
  47.7 2.3 %collective-permute-start.19 = (bf16[32,2176]{1,0:T(8,128)(2,1)S(1)}, bf16[32,2176]{1,0:T(8,128)(2,1)S(1)}, u32[]{:S(2)}, u32[]{:S(2)}) collective-permute-start(bf16[32,2176]{1,0:T(8,128)(2,1)S(1)} %collective-permute-done.18.refs_3_), channel_id=1, source_target_pairs={{0,1},{1,0},{2,3},{3,2},{4,5},{5,4},{6,7},{7,6},{8,9},{9,8},{10,11... | collective-permute-start | bytes 417800 | tf_op jit(solution)/shard_map/ppermute | solution.py:357
  48.0 4.3 %collective-permute-start.23 = (bf16[1,32,1024]{2,1,0:T(8,128)(2,1)S(1)}, bf16[1,32,1024]{2,1,0:T(8,128)(2,1)S(1)}, u32[]{:S(2)}, u32[]{:S(2)}) collective-permute-start(bf16[1,32,1024]{2,1,0:T(8,128)(2,1)S(1)} %get-tuple-element.96), channel_id=1, source_target_pairs={{0,2},{1,3},{2,0},{3,1},{4,6},{5,7},{6,4},{7,5},{8,10},{9,11},{10,... | collective-permute-start | bytes 196616 | tf_op jit(solution)/shard_map/ppermute | solution.py:357
